TPU v7x, 32 devices: a whole 2x2x4 slice. The times are simulated.
32 devices in a mesh: ctx: 8 (over z, x), fsdp: 4 (over y, core).
Axes of the slice: x: 2, y: 2, z: 4, core: 2. Of those that a mesh axis runs over, the one named last changes fastest.
Arguments:
- tokens: bfloat16 [4, 1024, 2048], P('fsdp', 'ctx'), may hold values from -6 to 6
- doc_lengths: int32 [4, 16], P('fsdp'), may hold values from 1 to 512, 1024 in all within a row
- routes: int32 [4, 1024, 3], P('fsdp', 'ctx'), may hold values from 0 to 5, all different within a row
- slot_order: int32 [4, 1024, 3], P('fsdp', 'ctx'), may hold values from 0 to 383, as said below
- attn_gain: bfloat16 [2048], P('fsdp'), may hold values from 0.5 to 1.5
- w_qkv: bfloat16 [2048, 6144], P('fsdp'), may hold values from -0.125 to 0.125
- q_gain: bfloat16 [2048], P('fsdp'), may hold values from 0.5 to 1.5
- k_gain: bfloat16 [2048], P('fsdp'), may hold values from 0.5 to 1.5
- w_out: bfloat16 [2048, 2048], P('fsdp'), may hold values from -0.375 to 0.375
- ffn_gain: bfloat16 [2048], P('fsdp'), may hold values from 0.5 to 1.5
- w_router: bfloat16 [2048, 6], P('fsdp'), may hold values from -0.09375 to 0.09375
- w_gate: bfloat16 [6, 2048, 1024], P(None, None, 'fsdp'), may hold values from -0.125 to 0.125
- w_up: bfloat16 [6, 2048, 1024], P(None, None, 'fsdp'), may hold values from -0.125 to 0.125
- w_down: bfloat16 [6, 1024, 2048], P(None, 'fsdp'), may hold values from -0.75 to 0.75
- cotangent: bfloat16 [4, 1024, 2048], P('fsdp', 'ctx'), may hold values from -6 to 6
Outputs:
- activations: bfloat16 [4, 1024, 2048], P('fsdp', 'ctx')
- input_grad: float32 [4, 1024, 2048], P('fsdp', 'ctx')
- g_attn_gain: float32 [2048], P('fsdp')
- g_qkv: float32 [2048, 6144], P('fsdp', 'ctx')
- g_q_gain: float32 [2048], P('fsdp')
- g_k_gain: float32 [2048], P('fsdp')
- g_out: float32 [2048, 2048], P('fsdp', 'ctx')
- g_ffn_gain: float32 [2048], P('fsdp')
- g_router: float32 [2048, 6], P('fsdp')
- g_gate: float32 [6, 2048, 1024], P(None, 'ctx', 'fsdp')
- g_up: float32 [6, 2048, 1024], P(None, 'ctx', 'fsdp')
- g_down: float32 [6, 1024, 2048], P(None, 'fsdp', 'ctx')
Inputs may be any that keep to these rules, and one draw needn't show every extreme that they name: `slot_order`: within each aligned block of 128 rows of a stream the 384 values are a permutation. `doc_lengths`: the lengths of a stream sum to 1024; the longest is 512. `routes`: each row names 3 different experts.
All inputs are finite; a program needn't handle non-finite values.
Results may differ from a plain program's by a relative error of at most 0.02.
Values may be sent and summed in bfloat16 or wider, within the bound.
A program may use at most 448 MiB of HBM per device.

v0:
```python
import math

import jax
import jax.numpy as jnp
from jax import lax
from jax.experimental import pallas as pl
from jax.experimental.pallas import tpu as pltpu
from jax.sharding import PartitionSpec as P

HEADS = 16
MESH = pl.DeviceIdType.MESH
ANY = pl.BlockSpec(memory_space=pl.ANY)
HBM = pl.BlockSpec(memory_space=pltpu.HBM)
VMEM = pl.BlockSpec(memory_space=pltpu.VMEM)
DMA = pltpu.SemaphoreType.DMA

EPSILON = 1e-05
ROPE_BASE = 10000.0
MASKED = -1e30


def rms_scale(values, gain_vector):
    return (
        values
        * lax.rsqrt(jnp.mean(values * values, axis=-1, keepdims=True) + EPSILON)
        * gain_vector
    )


def rotate(values, inner_pos):
    half_dim = values.shape[-1] // 2
    freq_table = ROPE_BASE ** (-2.0 * jnp.arange(half_dim, dtype=jnp.float32) / values.shape[-1])
    angles = inner_pos.astype(jnp.float32)[:, None] * freq_table[None, :]
    cosine = jnp.cos(angles)[:, None, :]
    sine_part = jnp.sin(angles)[:, None, :]
    first_half = values[..., :half_dim]
    second_half = values[..., half_dim:]
    return jnp.concatenate(
        [
            first_half * cosine - second_half * sine_part,
            second_half * cosine + first_half * sine_part,
        ],
        axis=-1,
    )


def dealt_position(flat_index, per_device, device_count):
    device_index = flat_index // per_device
    within = flat_index % per_device
    half_rows = per_device // 2
    return jnp.where(
        within < half_rows,
        device_index * half_rows + within,
        (2 * device_count - 1 - device_index) * half_rows + within - half_rows,
    )


def document_info(positions, lengths):
    doc_ends = jnp.sum(jnp.where(jnp.arange(lengths.shape[0])[:, None] >= jnp.arange(lengths.shape[0])[None, :], lengths[None, :], 0), axis=1)
    passed = doc_ends[None, :] <= positions[:, None]
    doc_ids = jnp.sum(passed.astype(jnp.int32), axis=1)
    inner_pos = positions - jnp.sum(jnp.where(passed, lengths[None, :], 0), axis=1)
    return (doc_ids, inner_pos)


def slot_table(route_ids, order_ids, capacity, expert_count):
    pair_count = route_ids.shape[0] * route_ids.shape[1]
    expert_flat = route_ids.reshape(pair_count)
    rank_flat = order_ids.reshape(pair_count)
    earlier = (expert_flat[None, :] == expert_flat[:, None]) & (
        rank_flat[None, :] < rank_flat[:, None]
    )
    slot_index = jnp.sum(earlier.astype(jnp.int32), axis=1)
    placed = jnp.where(
        slot_index < capacity, expert_flat * capacity + slot_index, expert_count * capacity
    )
    source = (
        jnp.full((expert_count * capacity + 1,), pair_count, jnp.int32)
        .at[placed]
        .set(jnp.arange(pair_count, dtype=jnp.int32))
    )
    return (placed, source[: expert_count * capacity])


def masked_scores(query_block, key_block, query_pos, query_doc, key_pos, key_doc, score_scale):
    scores = (
        jnp.einsum("qhd,khd->hqk", query_block, key_block, preferred_element_type=jnp.float32)
        * score_scale
    )
    allowed = (query_doc[:, None] == key_doc[None, :]) & (key_pos[None, :] <= query_pos[:, None])
    return jnp.where(allowed[None], scores, MASKED)


def silu_parts(hidden_grad, slot_gate, slot_up):
    sigma = jax.nn.sigmoid(slot_gate)
    gate_grad_low = (hidden_grad * slot_up * sigma * (1.0 + slot_gate * (1.0 - sigma))).astype(
        jnp.bfloat16
    )
    up_grad_low = (hidden_grad * slot_gate * sigma).astype(jnp.bfloat16)
    return (gate_grad_low, up_grad_low)


def on_device(
    tokens,
    doc_lengths,
    routes,
    slot_order,
    attn_gain,
    w_qkv,
    q_gain,
    k_gain,
    w_out,
    ffn_gain,
    w_router,
    w_gate,
    w_up,
    w_down,
    cotangent,
):
    row_count = tokens.shape[1]
    model_width = tokens.shape[2]
    head_count = HEADS
    head_dim = model_width // head_count
    score_scale = head_dim ** (-0.5)
    ctx_count = lax.axis_size("ctx")
    ctx_index = lax.axis_index("ctx")
    total_rows = row_count * ctx_count
    lengths = doc_lengths[0]
    local_pos = dealt_position(
        ctx_index * row_count + jnp.arange(row_count, dtype=jnp.int32), row_count, ctx_count
    )
    local_doc, local_inner = document_info(local_pos, lengths)
    stream_pos = dealt_position(jnp.arange(total_rows, dtype=jnp.int32), row_count, ctx_count)
    stream_doc, stream_inner = document_info(stream_pos, lengths)
    block_rows = math.gcd(total_rows, 512)
    block_count = total_rows // block_rows
    block_ids = jnp.arange(block_count, dtype=jnp.int32)
    gain_one, qkv_weight, gain_query, gain_key, out_weight = (
        lax.all_gather(attn_gain, "fsdp", axis=0, tiled=True),
        lax.all_gather(w_qkv, "fsdp", axis=0, tiled=True),
        lax.all_gather(q_gain, "fsdp", axis=0, tiled=True),
        lax.all_gather(k_gain, "fsdp", axis=0, tiled=True),
        lax.all_gather(w_out, "fsdp", axis=0, tiled=True),
    )
    gain_two, router_weight, gate_weight, up_weight, down_weight = (
        lax.all_gather(ffn_gain, "fsdp", axis=0, tiled=True),
        lax.all_gather(w_router, "fsdp", axis=0, tiled=True),
        lax.all_gather(w_gate, "fsdp", axis=2, tiled=True),
        lax.all_gather(w_up, "fsdp", axis=2, tiled=True),
        lax.all_gather(w_down, "fsdp", axis=1, tiled=True),
    )
    inputs = tokens[0].astype(jnp.float32)
    normed_f, norm_one_pull = jax.vjp(rms_scale, inputs, gain_one.astype(jnp.float32))
    normed_low = normed_f.astype(jnp.bfloat16)
    projected = jnp.dot(normed_low, qkv_weight, preferred_element_type=jnp.float32)
    query_lin = projected[:, :model_width]
    key_lin = projected[:, model_width : 2 * model_width]
    value_low = (
        projected[:, 2 * model_width :]
        .astype(jnp.bfloat16)
        .reshape(row_count, head_count, head_dim)
    )

    def head_shape(values, gain_vector):
        return rotate(
            rms_scale(values, gain_vector).reshape(row_count, head_count, head_dim), local_inner
        )

    query_f, query_pull = jax.vjp(head_shape, query_lin, gain_query.astype(jnp.float32))
    key_f, key_pull = jax.vjp(head_shape, key_lin, gain_key.astype(jnp.float32))
    query_low = query_f.astype(jnp.bfloat16)
    key_low = key_f.astype(jnp.bfloat16)
    keys_all, values_all = (
        lax.all_gather(key_low, "ctx", axis=0, tiled=True),
        lax.all_gather(value_low, "ctx", axis=0, tiled=True),
    )

    def key_slice(block_index):
        first_row = block_index * block_rows
        return (
            lax.dynamic_slice_in_dim(keys_all, first_row, block_rows, 0),
            lax.dynamic_slice_in_dim(values_all, first_row, block_rows, 0),
            lax.dynamic_slice_in_dim(stream_pos, first_row, block_rows, 0),
            lax.dynamic_slice_in_dim(stream_doc, first_row, block_rows, 0),
        )

    def stats_step(carry, block_index):
        running_top, running_total = carry
        key_block, value_block, key_pos, key_doc = key_slice(block_index)
        scores = masked_scores(
            query_low, key_block, local_pos, local_doc, key_pos, key_doc, score_scale
        )
        new_top = jnp.maximum(running_top, jnp.max(scores, axis=-1))
        running_total = running_total * jnp.exp(running_top - new_top) + jnp.sum(
            jnp.exp(scores - new_top[..., None]), axis=-1
        )
        return ((new_top, running_total), None)

    start_stats = (
        jnp.full((head_count, row_count), MASKED, jnp.float32),
        jnp.zeros((head_count, row_count), jnp.float32),
    )
    (score_top, score_total), _ = lax.scan(stats_step, start_stats, block_ids)
    log_total = score_top + jnp.log(score_total)

    def output_step(accum, block_index):
        key_block, value_block, key_pos, key_doc = key_slice(block_index)
        scores = masked_scores(
            query_low, key_block, local_pos, local_doc, key_pos, key_doc, score_scale
        )
        prob_block = jnp.exp(scores - log_total[..., None]).astype(jnp.bfloat16)
        return (
            accum
            + jnp.einsum(
                "hqk,khd->qhd", prob_block, value_block, preferred_element_type=jnp.float32
            ),
            None,
        )

    attended_f, _ = lax.scan(
        output_step, jnp.zeros((row_count, head_count, head_dim), jnp.float32), block_ids
    )
    attended_low = attended_f.reshape(row_count, model_width).astype(jnp.bfloat16)
    mixed = inputs + jnp.dot(attended_low, out_weight, preferred_element_type=jnp.float32)
    normed_two_f, norm_two_pull = jax.vjp(rms_scale, mixed, gain_two.astype(jnp.float32))
    normed_two = normed_two_f.astype(jnp.bfloat16)
    expert_count = gate_weight.shape[0]
    route_ids = routes[0]
    top_count = route_ids.shape[1]
    pair_count = row_count * top_count
    capacity = pair_count // expert_count
    logits = jnp.dot(normed_two, router_weight, preferred_element_type=jnp.float32)
    router_probs = jax.nn.softmax(logits, axis=-1)
    chosen = (
        route_ids[:, :, None] == jnp.arange(expert_count, dtype=jnp.int32)[None, None, :]
    ).astype(jnp.float32)
    gate_values = jnp.sum(chosen * router_probs[:, None, :], axis=-1)
    placed, source = slot_table(route_ids, slot_order[0], capacity, expert_count)
    padded_in = jnp.concatenate([normed_two, jnp.zeros((1, model_width), jnp.bfloat16)], axis=0)
    expert_in = padded_in[source // top_count].reshape(expert_count, capacity, model_width)
    gate_pre = jnp.einsum(
        "ecd,edh->ech", expert_in, gate_weight, preferred_element_type=jnp.float32
    )
    up_pre = jnp.einsum("ecd,edh->ech", expert_in, up_weight, preferred_element_type=jnp.float32)
    hidden_low = (jax.nn.silu(gate_pre) * up_pre).astype(jnp.bfloat16)
    expert_out = jnp.einsum(
        "ech,ehd->ecd", hidden_low, down_weight, preferred_element_type=jnp.float32
    )
    out_padded = jnp.concatenate(
        [
            expert_out.reshape(expert_count * capacity, model_width),
            jnp.zeros((1, model_width), jnp.float32),
        ],
        axis=0,
    )
    per_pair = out_padded[placed].reshape(row_count, top_count, model_width)
    layer_out = mixed + jnp.sum(gate_values[:, :, None] * per_pair, axis=1)
    out_grad = cotangent[0].astype(jnp.float32)
    gate_grad = jnp.sum(out_grad[:, None, :] * per_pair, axis=-1)
    pair_grad = (gate_values[:, :, None] * out_grad[:, None, :]).reshape(pair_count, model_width)
    pair_padded = jnp.concatenate([pair_grad, jnp.zeros((1, model_width), jnp.float32)], axis=0)
    slot_grad = (
        pair_padded[source].reshape(expert_count, capacity, model_width).astype(jnp.bfloat16)
    )

    def expert_step(carry, pieces):
        slot_in, slot_hidden, slot_dy, slot_gate, slot_up, gate_matrix, up_matrix, down_matrix = (
            pieces
        )
        hidden_grad = jnp.einsum(
            "cd,hd->ch", slot_dy, down_matrix, preferred_element_type=jnp.float32
        )
        gate_grad_low, up_grad_low = silu_parts(hidden_grad, slot_gate, slot_up)
        in_grad = jnp.einsum(
            "ch,dh->cd", gate_grad_low, gate_matrix, preferred_element_type=jnp.float32
        ) + jnp.einsum("ch,dh->cd", up_grad_low, up_matrix, preferred_element_type=jnp.float32)
        gate_term = jnp.einsum(
            "cd,ch->dh", slot_in, gate_grad_low, preferred_element_type=jnp.float32
        )
        up_term = jnp.einsum("cd,ch->dh", slot_in, up_grad_low, preferred_element_type=jnp.float32)
        down_term = jnp.einsum(
            "ch,cd->hd", slot_hidden, slot_dy, preferred_element_type=jnp.float32
        )
        gate_shard, up_shard, down_shard = (
            lax.psum_scatter(
                gate_term.astype(jnp.bfloat16), "fsdp", scatter_dimension=1, tiled=True
            ).astype(jnp.float32),
            lax.psum_scatter(
                up_term.astype(jnp.bfloat16), "fsdp", scatter_dimension=1, tiled=True
            ).astype(jnp.float32),
            lax.psum_scatter(
                down_term.astype(jnp.bfloat16), "fsdp", scatter_dimension=0, tiled=True
            ).astype(jnp.float32),
        )
        gate_part, up_part, down_part = (
            lax.psum_scatter(
                gate_shard.astype(jnp.bfloat16), "ctx", scatter_dimension=0, tiled=True
            ).astype(jnp.float32),
            lax.psum_scatter(
                up_shard.astype(jnp.bfloat16), "ctx", scatter_dimension=0, tiled=True
            ).astype(jnp.float32),
            lax.psum_scatter(
                down_shard.astype(jnp.bfloat16), "ctx", scatter_dimension=1, tiled=True
            ).astype(jnp.float32),
        )
        return (carry, (in_grad, gate_part, up_part, down_part))

    _, (expert_in_grad, gate_parts, up_parts, down_parts) = lax.scan(
        expert_step,
        None,
        (expert_in, hidden_low, slot_grad, gate_pre, up_pre, gate_weight, up_weight, down_weight),
    )
    in_padded = jnp.concatenate(
        [
            expert_in_grad.reshape(expert_count * capacity, model_width),
            jnp.zeros((1, model_width), jnp.float32),
        ],
        axis=0,
    )
    normed_two_grad = jnp.sum(in_padded[placed].reshape(row_count, top_count, model_width), axis=1)
    prob_grad_router = jnp.sum(chosen * gate_grad[:, :, None], axis=1)
    logit_grad = (
        router_probs
        * (prob_grad_router - jnp.sum(router_probs * prob_grad_router, axis=-1, keepdims=True))
    ).astype(jnp.bfloat16)
    normed_two_grad = normed_two_grad + jnp.einsum(
        "te,de->td", logit_grad, router_weight, preferred_element_type=jnp.float32
    )
    router_grad = jnp.einsum(
        "td,te->de", normed_two, logit_grad, preferred_element_type=jnp.float32
    )
    mixed_norm_grad, gain_two_grad = norm_two_pull(normed_two_grad)
    mixed_grad = out_grad + mixed_norm_grad
    mixed_low = mixed_grad.astype(jnp.bfloat16)
    out_weight_grad = jnp.einsum(
        "td,te->de", attended_low, mixed_low, preferred_element_type=jnp.float32
    )
    output_grad = (
        jnp.einsum("te,de->td", mixed_low, out_weight, preferred_element_type=jnp.float32)
        .astype(jnp.bfloat16)
        .reshape(row_count, head_count, head_dim)
    )
    row_delta = jnp.sum(output_grad.astype(jnp.float32) * attended_f, axis=-1).T

    def query_grad_step(accum, block_index):
        key_block, value_block, key_pos, key_doc = key_slice(block_index)
        scores = masked_scores(
            query_low, key_block, local_pos, local_doc, key_pos, key_doc, score_scale
        )
        prob_block = jnp.exp(scores - log_total[..., None])
        prob_grad = jnp.einsum(
            "qhd,khd->hqk", output_grad, value_block, preferred_element_type=jnp.float32
        )
        score_grad = (prob_block * (prob_grad - row_delta[..., None])).astype(jnp.bfloat16)
        return (
            accum
            + jnp.einsum("hqk,khd->qhd", score_grad, key_block, preferred_element_type=jnp.float32)
            * score_scale,
            None,
        )

    query_grad, _ = lax.scan(
        query_grad_step, jnp.zeros((row_count, head_count, head_dim), jnp.float32), block_ids
    )
    inner_rows = math.gcd(row_count * lax.axis_size("ctx"), 512)

    def piece_step(carry, piece_index):
        first_row = piece_index * inner_rows
        key_block = lax.dynamic_slice_in_dim(keys_all, first_row, inner_rows, 0)
        value_block = lax.dynamic_slice_in_dim(values_all, first_row, inner_rows, 0)
        key_pos = lax.dynamic_slice_in_dim(stream_pos, first_row, inner_rows, 0)
        key_doc = lax.dynamic_slice_in_dim(stream_doc, first_row, inner_rows, 0)
        scores = masked_scores(
            query_low, key_block, local_pos, local_doc, key_pos, key_doc, score_scale
        )
        prob_block = jnp.exp(scores - log_total[..., None])
        prob_grad = jnp.einsum(
            "qhd,khd->hqk", output_grad, value_block, preferred_element_type=jnp.float32
        )
        score_grad = (prob_block * (prob_grad - row_delta[..., None])).astype(jnp.bfloat16)
        value_part = jnp.einsum(
            "hqk,qhd->khd",
            prob_block.astype(jnp.bfloat16),
            output_grad,
            preferred_element_type=jnp.float32,
        )
        key_part = (
            jnp.einsum("hqk,qhd->khd", score_grad, query_low, preferred_element_type=jnp.float32)
            * score_scale
        )
        return (
            carry,
            jnp.concatenate(
                [
                    key_part.reshape(inner_rows, model_width),
                    value_part.reshape(inner_rows, model_width),
                ],
                axis=1,
            ),
        )

    _, stacked = lax.scan(
        piece_step,
        None,
        jnp.arange(row_count * lax.axis_size("ctx") // inner_rows, dtype=jnp.int32),
    )
    key_value_grad = lax.psum_scatter(
        stacked.reshape(row_count * lax.axis_size("ctx"), 2 * model_width).astype(jnp.bfloat16),
        "ctx",
        scatter_dimension=0,
        tiled=True,
    ).astype(jnp.float32)
    key_grad = key_value_grad[:, :model_width].reshape(row_count, head_count, head_dim)
    value_grad = key_value_grad[:, model_width:]
    query_lin_grad, gain_query_grad = query_pull(query_grad)
    key_lin_grad, gain_key_grad = key_pull(key_grad)
    proj_grad = jnp.concatenate(
        [
            query_lin_grad.astype(jnp.bfloat16),
            key_lin_grad.astype(jnp.bfloat16),
            value_grad.astype(jnp.bfloat16),
        ],
        axis=1,
    )
    qkv_weight_grad = jnp.einsum(
        "td,te->de", normed_low, proj_grad, preferred_element_type=jnp.float32
    )
    normed_grad = jnp.einsum("te,de->td", proj_grad, qkv_weight, preferred_element_type=jnp.float32)
    input_norm_grad, gain_one_grad = norm_one_pull(normed_grad)
    input_grad = mixed_grad + input_norm_grad
    qkv_shard, out_shard = (
        lax.psum_scatter(
            qkv_weight_grad.astype(jnp.bfloat16), "fsdp", scatter_dimension=0, tiled=True
        ).astype(jnp.float32),
        lax.psum_scatter(
            out_weight_grad.astype(jnp.bfloat16), "fsdp", scatter_dimension=0, tiled=True
        ).astype(jnp.float32),
    )
    qkv_part, out_part = (
        lax.psum_scatter(
            qkv_shard.astype(jnp.bfloat16), "ctx", scatter_dimension=1, tiled=True
        ).astype(jnp.float32),
        lax.psum_scatter(
            out_shard.astype(jnp.bfloat16), "ctx", scatter_dimension=1, tiled=True
        ).astype(jnp.float32),
    )
    gain_one_sum, gain_query_sum, gain_key_sum, gain_two_sum, router_sum = lax.psum(
        (gain_one_grad, gain_query_grad, gain_key_grad, gain_two_grad, router_grad), ("ctx", "fsdp")
    )
    shard_rows = model_width // lax.axis_size("fsdp")
    shard_start = lax.axis_index("fsdp") * shard_rows

    def own_rows(full_array):
        return lax.dynamic_slice_in_dim(full_array, shard_start, shard_rows, 0)

    return (
        layer_out.astype(jnp.bfloat16)[None],
        input_grad[None],
        own_rows(gain_one_sum),
        qkv_part,
        own_rows(gain_query_sum),
        own_rows(gain_key_sum),
        out_part,
        own_rows(gain_two_sum),
        own_rows(router_sum),
        gate_parts,
        up_parts,
        down_parts,
    )


def rms_unit(values):
    return lax.rsqrt(jnp.mean(values * values, axis=-1, keepdims=True) + EPSILON)


def rope_tables(inner_pos, head_dim):
    half_dim = head_dim // 2
    freq_table = ROPE_BASE ** (-2.0 * jnp.arange(half_dim, dtype=jnp.float32) / head_dim)
    angles = inner_pos.astype(jnp.float32)[:, None] * freq_table[None, :]
    return (jnp.cos(angles), jnp.sin(angles))


def dot32(spec, left, right):
    return jnp.einsum(spec, left, right, preferred_element_type=jnp.float32)


def greet(peers):
    barrier = pltpu.get_barrier_semaphore()
    for peer in peers:
        pl.semaphore_signal(barrier, inc=1, device_id=peer, device_id_type=MESH)
    pl.semaphore_wait(barrier, len(peers))


def send(source, target, send_sem, recv_sem, peer):
    copy = pltpu.make_async_remote_copy(
        source, target, send_sem, recv_sem, device_id=peer, device_id_type=MESH
    )
    copy.start()
    return copy


def comm_call(
    kernel, name, collective_id, out_shape, in_specs, out_specs, scratch_shapes, cost, vmem=16
):
    return pl.pallas_call(
        kernel,
        out_shape=out_shape,
        in_specs=in_specs,
        out_specs=out_specs,
        scratch_shapes=scratch_shapes,
        compiler_params=pltpu.CompilerParams(
            collective_id=collective_id, has_side_effects=True, vmem_limit_bytes=vmem * 2**20
        ),
        cost_estimate=pl.CostEstimate(flops=0, bytes_accessed=cost, transcendentals=0),
        name=name,
    )


def ctx_sum(values, collective_id):
    ctx = lax.axis_size("ctx")

    def kernel(own_ref, out_ref, held, send_sems, recv_sems):
        me, mine = lax.axis_index("ctx"), lax.axis_index("fsdp")
        peers = [(lax.rem(me + step, ctx), mine) for step in range(1, ctx)]
        greet(peers)
        copies = [
            send(own_ref, held.at[i], send_sems.at[i], recv_sems.at[i], peer)
            for i, peer in enumerate(peers)
        ]
        total = own_ref[...]
        for i, copy in enumerate(copies):
            copy.wait_recv()
            total = total + held[i]
        out_ref[...] = total
        for copy in copies:
            copy.wait_send()

    return comm_call(
        kernel,
        "ctx_sum",
        collective_id,
        jax.ShapeDtypeStruct(values.shape, values.dtype),
        [VMEM],
        VMEM,
        [
            pltpu.VMEM((ctx - 1,) + values.shape, values.dtype),
            DMA((ctx - 1,)),
            DMA((ctx - 1,)),
        ],
        20 * 2**20,
    )(values)


def heads_to_rows(values, collective_id):
    ctx, fsdp = lax.axis_size("ctx"), lax.axis_size("fsdp")
    rows, cols = values.shape[0] // ctx, values.shape[1]
    share = ctx // fsdp

    def kernel(own_ref, out_ref, send_sems, recv_sems):
        me, mine = lax.axis_index("ctx"), lax.axis_index("fsdp")
        keeper, place = me // share, lax.rem(me, share)
        own_keeper = (keeper == mine).astype(jnp.int32)
        barrier = pltpu.get_barrier_semaphore()
        for step in range(share * fsdp):
            source, stream = mine * share + step // fsdp, step % fsdp

            @pl.when(jnp.logical_or(source != me, stream != mine))
            def _():
                pl.semaphore_signal(
                    barrier, inc=1, device_id=(source, stream), device_id_type=MESH
                )

        pl.semaphore_wait(barrier, ctx - own_keeper)

        def block(index):
            return own_ref.at[pl.ds(pl.multiple_of(index * rows, rows), rows), :]

        def landing(stream, position):
            return out_ref.at[
                pl.ds(pl.multiple_of(stream * rows, rows), rows),
                pl.ds(pl.multiple_of(position * cols, cols), cols),
            ]

        slot = place * fsdp + mine

        def copy_to(step):
            other = lax.rem(me + step, ctx)
            return pltpu.make_async_remote_copy(
                block(other),
                landing(mine, place),
                send_sems.at[step],
                recv_sems.at[slot],
                device_id=(other, keeper),
                device_id_type=MESH,
            )

        kept = pltpu.make_async_copy(block(me), landing(mine, place), send_sems.at[0])
        for step in range(1, ctx):
            copy_to(step).start()

        @pl.when(own_keeper == 0)
        def _():
            copy_to(0).start()

        @pl.when(own_keeper == 1)
        def _():
            kept.start()
            kept.wait()

        for step in range(share * fsdp):

            @pl.when(
                jnp.logical_or(mine * share + step // fsdp != me, step % fsdp != mine)
            )
            def _():
                pltpu.make_async_copy(
                    block(0), landing(step % fsdp, step // fsdp), recv_sems.at[step]
                ).wait()

        for step in range(1, ctx):
            copy_to(step).wait_send()

        @pl.when(own_keeper == 0)
        def _():
            copy_to(0).wait_send()

    return comm_call(
        kernel,
        "heads_to_rows",
        collective_id,
        jax.ShapeDtypeStruct((fsdp * rows, share * cols), values.dtype),
        [ANY],
        ANY,
        [DMA((ctx,)), DMA((share * fsdp,))],
        40 * 2**20,
    )(values)


def rows_to_heads(values, collective_id):
    ctx, fsdp = lax.axis_size("ctx"), lax.axis_size("fsdp")
    share = ctx // fsdp
    rows, cols = values.shape[0] // fsdp, values.shape[1] // share

    def kernel(own_ref, out_ref, stage, stage_send, stage_recv, send_sems, recv_sems, done_sem):
        me, mine = lax.axis_index("ctx"), lax.axis_index("fsdp")
        ctx_peers = [(lax.rem(me + step, ctx), mine) for step in range(1, ctx)]
        greet(ctx_peers + [(me, lax.rem(mine + step, fsdp)) for step in range(1, fsdp)])

        def block(stream):
            return own_ref.at[pl.ds(pl.multiple_of(stream * rows, rows), rows), :]

        def landing(index):
            return out_ref.at[pl.ds(pl.multiple_of(index * rows, rows), rows), :]

        steps = [2, 3, 1]
        staged = {
            step: send(
                block(lax.rem(mine + step, fsdp)),
                stage.at[fsdp - step],
                stage_send.at[step],
                stage_recv.at[fsdp - step],
                (me, lax.rem(mine + step, fsdp)),
            )
            for step in steps
        }

        def piece(step, place):
            span = pl.ds(place * cols, cols)
            if step == 0:
                return own_ref.at[pl.ds(pl.multiple_of(mine * rows, rows), rows), span]
            return stage.at[step, :, span]

        def target(step, place):
            return lax.rem(mine + step, fsdp) * share + place

        def copy_to(step, place):
            return pltpu.make_async_remote_copy(
                piece(step, place),
                landing(me),
                send_sems.at[step * share + place],
                recv_sems.at[me],
                device_id=(target(step, place), mine),
                device_id_type=MESH,
            )

        def keep(step, place):
            return pltpu.make_async_copy(
                piece(step, place), landing(me), send_sems.at[step * share + place]
            )

        for step in [0, 1, 2, 3]:
            if step > 0:
                staged[fsdp - step].wait_recv()
            for place in range(share):
                far = target(step, place) != me
                pl.when(far)(copy_to(step, place).start)
                pl.when(jnp.logical_not(far))(keep(step, place).start)
        for step in range(1, ctx):
            source = lax.rem(me + step, ctx)
            pltpu.make_async_copy(
                piece(0, 0), landing(source), recv_sems.at[source]
            ).wait()
        for step in range(fsdp):
            for place in range(share):
                far = target(step, place) != me
                pl.when(far)(copy_to(step, place).wait_send)
                pl.when(jnp.logical_not(far))(keep(step, place).wait)
        for copy in staged.values():
            copy.wait_send()
        for peer in ctx_peers:
            pl.semaphore_signal(done_sem, inc=1, device_id=peer, device_id_type=MESH)
        pl.semaphore_wait(done_sem, ctx - 1)

    return comm_call(
        kernel,
        "rows_to_heads",
        collective_id,
        jax.ShapeDtypeStruct((ctx * rows, cols), values.dtype),
        [ANY],
        ANY,
        [
            pltpu.VMEM((fsdp, rows, share * cols), values.dtype),
            DMA((fsdp,)),
            DMA((fsdp,)),
            DMA((ctx,)),
            DMA((ctx,)),
            pltpu.SemaphoreType.REGULAR,
        ],
        2**20,
    )(values)


def swap(values, flip):
    return lax.ppermute(values, "ctx", [(i, i ^ flip) for i in range(lax.axis_size("ctx"))])


def reduce_then_gather(partial, extras, out_shapes, chunk_math, name, collective_id, crossed, bulk):
    ctx, fsdp = lax.axis_size("ctx"), lax.axis_size("fsdp")
    rows, width = partial.shape[0] // fsdp, partial.shape[1]
    chunks = 4
    size = rows // chunks
    count = len(extras)
    cols = width // ctx
    if crossed:
        out_shapes = out_shapes + [jax.ShapeDtypeStruct((rows, width // 2), jnp.bfloat16)]
    bulk_count, out_count = len(bulk), len(out_shapes)

    def kernel(*refs):
        part_ref, extra_refs = refs[0], refs[1 : 1 + count]
        bulk_refs, refs = refs[1 + count : 1 + count + bulk_count], refs[1 + count + bulk_count :]
        all_ref, out_refs = refs[0], refs[1 : 1 + out_count]
        bulk_out_refs, refs = refs[1 + out_count : 1 + out_count + bulk_count], refs[1 + out_count :]
        near_own, near_far, far_sum, far_own, sems, cross_sems, bulk_sems = refs[bulk_count:]
        me, mine = lax.axis_index("ctx"), lax.axis_index("fsdp")
        flip = 1 - 2 * lax.rem(mine, 2)
        core = mine + flip
        chip = lax.rem(mine + 2, fsdp)
        diagonal = lax.rem(core + 2, fsdp)
        to_x = (flipped(me, 1), mine)
        greet([(me, core), (me, chip)] + ([to_x] if crossed or bulk else []))

        def span(block, i):
            return pl.ds(pl.multiple_of(block * rows + i * size, size), size)

        def sem(kind, i):
            return sems.at[2 * kind, i], sems.at[2 * kind + 1, i]

        copies = []
        from_core_far, from_core_own, from_chip = [], [], []
        exchanged = [
            send(source, target, bulk_sems.at[0, i], bulk_sems.at[1, i], to_x)
            for i, (source, target) in enumerate(zip(bulk_refs, bulk_out_refs))
        ]
        for i in range(chunks):
            copy = send(
                part_ref.at[span(diagonal, i), :], near_far.at[i], *sem(0, i), (me, core)
            )
            from_core_far.append(copy)
        for i in range(chunks):
            copy = send(part_ref.at[span(core, i), :], near_own.at[i], *sem(1, i), (me, core))
            from_core_own.append(copy)
        for i in range(chunks):
            from_core_far[i].wait_recv()
            both = part_ref[span(chip, i), :].astype(jnp.float32) + near_far[i].astype(jnp.float32)
            far_sum[i] = both.astype(jnp.bfloat16)
            from_chip.append(send(far_sum.at[i], far_own.at[i], *sem(2, i), (me, chip)))
        to_chip = []
        for i in range(chunks):
            from_core_own[i].wait_recv()
            from_chip[i].wait_recv()
            total = (
                part_ref[span(mine, i), :].astype(jnp.float32)
                + near_own[i].astype(jnp.float32)
                + far_own[i].astype(jnp.float32)
            )
            all_ref[span(mine, i), :] = chunk_math(
                i, pl.ds(i * size, size), total, extra_refs, out_refs
            ).astype(jnp.bfloat16)
            own = all_ref.at[span(mine, i), :]
            to_chip.append(send(own, own, *sem(3, i), (me, chip)))
            copies.append(send(own, own, *sem(4, i), (me, core)))
            for run in range(ctx // 2 if crossed else 0):
                start = pl.multiple_of((2 * run + 1 - lax.rem(me, 2)) * cols, cols)
                copies.append(
                    send(
                        all_ref.at[span(mine, i), pl.ds(start, cols)],
                        out_refs[-1].at[pl.ds(i * size, size), pl.ds(run * cols, cols)],
                        cross_sems.at[0, i, run],
                        cross_sems.at[1, i, run],
                        to_x,
                    )
                )
        for i in range(chunks):
            to_chip[i].wait_recv()
            other = all_ref.at[span(chip, i), :]
            copies.append(send(other, other, *sem(5, i), (me, core)))
        for copy in copies + exchanged:
            copy.wait_recv()
        for copy in from_core_far + from_core_own + from_chip + to_chip + copies + exchanged:
            copy.wait_send()

    return comm_call(
        kernel,
        name,
        collective_id,
        [jax.ShapeDtypeStruct(partial.shape, jnp.bfloat16)]
        + out_shapes
        + [jax.ShapeDtypeStruct(values.shape, values.dtype) for values in bulk],
        [VMEM] * (1 + count) + [ANY] * bulk_count,
        [VMEM] * (1 + out_count) + [ANY] * bulk_count,
        [
            pltpu.VMEM((chunks, size, width), jnp.bfloat16),
            pltpu.VMEM((chunks, size, width), jnp.bfloat16),
            pltpu.VMEM((chunks, size, width), jnp.bfloat16),
            pltpu.VMEM((chunks, size, width), jnp.bfloat16),
            DMA((12, chunks)),
            DMA((2, chunks, ctx // 2)),
            DMA((2, max(1, bulk_count))),
        ],
        100 * 2**20,
    )(partial, *extras, *bulk)


def norm_chunk(index, span, total, extra_refs, out_refs):
    tokens_ref, gain_ref = extra_refs
    mixed = tokens_ref[span, :].astype(jnp.float32) + total
    out_refs[0][span, :] = mixed
    return mixed * rms_unit(mixed) * gain_ref[...]


def norm_back_chunk(index, span, total, extra_refs, out_refs):
    mixed_ref, gain_ref, dy_ref = extra_refs
    mixed = mixed_ref[span, :]
    scale = rms_unit(mixed)
    unit = mixed * scale
    pulled = total * gain_ref[...]
    grad = dy_ref[span, :].astype(jnp.float32) + scale * (
        pulled - unit * jnp.mean(unit * pulled, axis=-1, keepdims=True)
    )
    out_refs[0][span, :] = grad
    gain_grad = jnp.sum(total * unit, axis=0, keepdims=True)
    if index == 0:
        out_refs[1][...] = gain_grad
    else:
        out_refs[1][...] += gain_grad
    return grad


ROUTER_ROWS = 16


def one_hot(slots, capacity):
    return lax.broadcasted_iota(jnp.int32, (capacity, slots.shape[1]), 0) == slots


def slots_of(pairs, experts, top):
    count = len(pairs)
    blocks, _, rows = pairs[0].shape
    absent = float(rows * top)

    def kernel(*refs):
        for pairs_ref, out_ref in zip(refs[:count], refs[count:]):
            out_ref[...] = jnp.full(out_ref.shape, -1, jnp.int32)
            for b in range(blocks):
                rank_rows = []
                for expert in range(experts):
                    rank = jnp.full((1, rows), absent, jnp.float32)
                    for k in range(top):
                        rank = jnp.where(
                            pairs_ref[b, k : k + 1, :] == expert,
                            pairs_ref[b, top + k : top + k + 1, :].astype(jnp.float32),
                            rank,
                        )
                    rank_rows.append(rank)
                filler = jnp.full((rows - experts, rows), absent, jnp.float32)
                by_column = jnp.concatenate(rank_rows + [filler], axis=0).T
                for expert, rank in enumerate(rank_rows):
                    earlier = jnp.where(by_column[:, expert : expert + 1] < rank, 1.0, 0.0)
                    slot = jnp.where(rank < absent, jnp.sum(earlier, axis=0, keepdims=True), -1.0)
                    out_ref[expert : expert + 1, b * rows : (b + 1) * rows] = slot.astype(jnp.int32)

    shape = jax.ShapeDtypeStruct((ROUTER_ROWS, blocks * rows), jnp.int32)
    return pl.pallas_call(
        kernel,
        out_shape=[shape] * count,
        in_specs=[VMEM] * count,
        out_specs=[VMEM] * count,
        cost_estimate=pl.CostEstimate(flops=10**7, bytes_accessed=2**20, transcendentals=0),
        name="slots_of",
    )(*pairs)


def run_experts(group, dy_all, slots, router, w_gate, w_up, w_down, blocks, capacity):
    experts, width, units = w_gate.shape
    total = group.shape[0]
    rows = total // blocks
    held = blocks * capacity
    f32, bf16 = jnp.float32, jnp.bfloat16

    def kernel(
        group_ref,
        dy_ref,
        slots_ref,
        router_ref,
        gate_ref,
        up_ref,
        down_ref,
        moved_ref,
        grad_ref,
        g_router_ref,
        scaled_ref,
        gate_low_ref,
        up_low_ref,
        disp,
        ins,
        dys,
        probs,
        prob_grad,
    ):
        expert = pl.program_id(0)

        def block_rows(b):
            return pl.ds(b * rows, rows)

        @pl.when(expert == 0)
        def _():
            logits = lax.dot_general(
                router_ref[...],
                group_ref[...],
                (((1,), (1,)), ((), ())),
                preferred_element_type=f32,
            )
            real = lax.broadcasted_iota(jnp.int32, logits.shape, 0) < experts
            logits = jnp.where(real, logits, MASKED)
            weights = jnp.exp(logits - jnp.max(logits, axis=0, keepdims=True))
            probs[...] = weights / jnp.sum(weights, axis=0, keepdims=True)
            prob_grad[...] = jnp.zeros_like(prob_grad)
            for b in range(blocks):
                for e in range(experts):
                    disp[b, pl.ds(e * capacity, capacity), :] = (
                        one_hot(slots_ref[pl.ds(e, 1), block_rows(b)], capacity)
                        .astype(f32)
                        .astype(bf16)
                    )
                for source, target in ((group_ref, ins), (dy_ref, dys)):
                    picked = jnp.dot(
                        disp[b], source[block_rows(b), :], preferred_element_type=f32
                    ).astype(bf16)
                    for e in range(experts):
                        target[e, pl.ds(b * capacity, capacity), :] = picked[
                            e * capacity : (e + 1) * capacity
                        ]

        expert_in, slot_dy = ins[expert], dys[expert]
        gate_matrix, up_matrix, down_matrix = gate_ref[0], up_ref[0], down_ref[0]
        gate_pre = jnp.dot(expert_in, gate_matrix, preferred_element_type=f32)
        up_pre = jnp.dot(expert_in, up_matrix, preferred_element_type=f32)
        raw_grad = lax.dot_general(
            slot_dy, down_matrix, (((1,), (1,)), ((), ())), preferred_element_type=f32
        )
        own_probs = probs[pl.ds(expert, 1), :]
        own_slots = slots_ref[pl.ds(expert, 1), :]
        hots = [
            one_hot(own_slots[:, b * rows : (b + 1) * rows], capacity) for b in range(blocks)
        ]
        value = jnp.concatenate(
            [
                jnp.sum(
                    jnp.where(hots[b], own_probs[:, b * rows : (b + 1) * rows], 0.0),
                    axis=1,
                    keepdims=True,
                )
                for b in range(blocks)
            ],
            axis=0,
        )
        sigma = 1.0 / (1.0 + jnp.exp(-gate_pre))
        silu = gate_pre * sigma
        hidden = (silu * up_pre).astype(bf16)
        hidden_f = hidden.astype(f32)
        value_grad = jnp.sum(hidden_f * raw_grad, axis=1, keepdims=True)
        hidden_grad = raw_grad * value
        gate_low = (hidden_grad * up_pre * sigma * (1.0 + gate_pre * (1.0 - sigma))).astype(bf16)
        up_low = (hidden_grad * silu).astype(bf16)
        scaled = (hidden_f * value).astype(bf16)
        scaled_ref[0] = scaled
        gate_low_ref[0] = gate_low
        up_low_ref[0] = up_low
        for b in range(blocks):
            prob_grad[expert, :, block_rows(b)] = jnp.sum(
                jnp.where(hots[b], value_grad[b * capacity : (b + 1) * capacity], 0.0),
                axis=0,
                keepdims=True,
            )
        dys[expert] = jnp.dot(scaled, down_matrix, preferred_element_type=f32).astype(bf16)
        ins[expert] = (
            lax.dot_general(
                gate_low, gate_matrix, (((1,), (1,)), ((), ())), preferred_element_type=f32
            )
            + lax.dot_general(
                up_low, up_matrix, (((1,), (1,)), ((), ())), preferred_element_type=f32
            )
        ).astype(bf16)

        @pl.when(expert == experts - 1)
        def _():
            grads = jnp.concatenate([prob_grad[e] for e in range(ROUTER_ROWS)], axis=0)
            weights = probs[...]
            logit_grad = (
                weights * (grads - jnp.sum(weights * grads, axis=0, keepdims=True))
            ).astype(bf16)
            g_router_ref[...] = jnp.dot(logit_grad, group_ref[...], preferred_element_type=f32)
            for b in range(blocks):
                for source, target in ((dys, moved_ref), (ins, grad_ref)):
                    gathered = jnp.concatenate(
                        [source[e, pl.ds(b * capacity, capacity), :] for e in range(experts)],
                        axis=0,
                    )
                    back = lax.dot_general(
                        disp[b], gathered, (((0,), (0,)), ((), ())), preferred_element_type=f32
                    )
                    if target is grad_ref:
                        back = back + lax.dot_general(
                            logit_grad[:, b * rows : (b + 1) * rows],
                            router_ref[...],
                            (((0,), (0,)), ((), ())),
                            preferred_element_type=f32,
                        )
                    target[block_rows(b), :] = back.astype(bf16)

    def whole(shape):
        return pl.BlockSpec(shape, lambda e: (0,) * len(shape))

    def by_expert(shape):
        return pl.BlockSpec((1,) + shape, lambda e: (e, 0, 0))

    return pl.pallas_call(
        kernel,
        grid=(experts,),
        out_shape=[
            jax.ShapeDtypeStruct((total, width), bf16),
            jax.ShapeDtypeStruct((total, width), bf16),
            jax.ShapeDtypeStruct((ROUTER_ROWS, width), f32),
        ]
        + [jax.ShapeDtypeStruct((experts, held, units), bf16)] * 3,
        in_specs=[
            whole((total, width)),
            whole((total, width)),
            whole((ROUTER_ROWS, total)),
            whole((ROUTER_ROWS, width)),
            by_expert((width, units)),
            by_expert((width, units)),
            by_expert((units, width)),
        ],
        out_specs=[
            whole((total, width)),
            whole((total, width)),
            whole((ROUTER_ROWS, width)),
        ]
        + [by_expert((held, units))] * 3,
        scratch_shapes=[
            pltpu.VMEM((blocks, experts * capacity, rows), bf16),
            pltpu.VMEM((experts, held, width), bf16),
            pltpu.VMEM((experts, held, width), bf16),
            pltpu.VMEM((ROUTER_ROWS, total), f32),
            pltpu.VMEM((ROUTER_ROWS, 1, total), f32),
        ],
        compiler_params=pltpu.CompilerParams(vmem_limit_bytes=56 * 2**20),
        cost_estimate=pl.CostEstimate(
            flops=30 * 10**9, bytes_accessed=30 * 2**20, transcendentals=10**6
        ),
        name="run_experts",
    )(group, dy_all, slots, router, w_gate, w_up, w_down)


def expert_grads(slot_own, slot_other, rows_own, rows_other, slots_own, slots_other, capacity):
    kinds = len(slot_own)
    experts, held, units = slot_own[0].shape
    total, half = rows_other.shape
    blocks = held // capacity
    rows = total // blocks
    ctx = lax.axis_size("ctx")
    cols = 2 * half // ctx
    f32, bf16 = jnp.float32, jnp.bfloat16

    def kernel(*refs):
        own_refs, other_refs = refs[:kinds], refs[kinds : 2 * kinds]
        rows_own_ref, rows_other_ref, slots_own_ref, slots_other_ref = refs[2 * kinds : 2 * kinds + 4]
        out_ref, held_rows = refs[2 * kinds + 4 :]
        expert = pl.program_id(0)
        me = lax.axis_index("ctx")

        def columns(side, run):
            if side == 1:
                return pl.ds(run * cols, cols)
            return pl.ds(pl.multiple_of((2 * run + lax.rem(me, 2)) * cols, cols), cols)

        @pl.when(expert == 0)
        def _():
            for side, slots_ref, source in (
                (0, slots_own_ref, rows_own_ref),
                (1, slots_other_ref, rows_other_ref),
            ):
                for b in range(blocks):
                    span = pl.ds(b * rows, rows)
                    disp = jnp.concatenate(
                        [
                            one_hot(slots_ref[pl.ds(e, 1), span], capacity).astype(f32)
                            for e in range(experts)
                        ],
                        axis=0,
                    ).astype(bf16)
                    for run in range(ctx // 2):
                        picked = jnp.dot(
                            disp, source[span, columns(side, run)], preferred_element_type=f32
                        ).astype(bf16)
                        for e in range(experts):
                            held_rows[
                                e,
                                pl.ds(side * held + b * capacity, capacity),
                                pl.ds(run * cols, cols),
                            ] = picked[e * capacity : (e + 1) * capacity]

        low, high = lax.rem(me // 2, 2), me // 4
        stacked = [
            jnp.concatenate([own[0], other[0]], axis=0) for own, other in zip(own_refs, other_refs)
        ]
        contract = (((0,), (0,)), ((), ()))
        for run in range(ctx // 2):
            kept = jnp.where(low == run % 2, 1, 0)
            far = jnp.where(high == run // 2, 0, 1)
            features = held_rows[expert, :, pl.ds(run * cols, cols)]
            for kind in range(kinds):
                out_ref[kind, pl.ds(kept, 1), pl.ds(far, 1), 0] = lax.dot_general(
                    features, stacked[kind], contract, preferred_element_type=f32
                ).astype(bf16)[None, None]

    def whole(shape):
        return pl.BlockSpec(shape, lambda e: (0,) * len(shape))

    slot_spec = pl.BlockSpec((1, held, units), lambda e: (e, 0, 0))
    return pl.pallas_call(
        kernel,
        grid=(experts,),
        out_shape=jax.ShapeDtypeStruct((kinds, 2, 2, experts, units, cols), bf16),
        in_specs=[slot_spec] * (2 * kinds)
        + [whole((total, 2 * half)), whole((total, half))]
        + [whole((ROUTER_ROWS, total))] * 2,
        out_specs=pl.BlockSpec((kinds, 2, 2, 1, units, cols), lambda e: (0, 0, 0, e, 0, 0)),
        scratch_shapes=[pltpu.VMEM((experts, 2 * held, half), bf16)],
        compiler_params=pltpu.CompilerParams(vmem_limit_bytes=60 * 2**20),
        cost_estimate=pl.CostEstimate(flops=0, bytes_accessed=2**20, transcendentals=0),
        name="expert_grads",
    )(*slot_own, *slot_other, rows_own, rows_other, slots_own, slots_other)


def down_grads(scaled, dy_parts, slots, capacity):
    count = len(scaled)
    experts, held, units = scaled[0].shape
    blocks, _, rows, wide = dy_parts.shape
    cols = wide // 2
    f32, bf16 = jnp.float32, jnp.bfloat16

    def kernel(*refs):
        scaled_refs, dy_ref, slots_refs = refs[:count], refs[count], refs[count + 1 : 2 * count + 1]
        out_ref, held_rows = refs[2 * count + 1 :]
        expert = pl.program_id(0)

        @pl.when(expert == 0)
        def _():
            for i, slots_ref in enumerate(slots_refs):
                for b in range(blocks):
                    span = pl.ds(b * rows, rows)
                    disp = jnp.concatenate(
                        [
                            one_hot(slots_ref[pl.ds(e, 1), span], capacity).astype(f32)
                            for e in range(experts)
                        ],
                        axis=0,
                    ).astype(bf16)
                    picked = jnp.dot(disp, dy_ref[b, i], preferred_element_type=f32).astype(bf16)
                    for e in range(experts):
                        held_rows[e, pl.ds(i * held + b * capacity, capacity), :] = picked[
                            e * capacity : (e + 1) * capacity
                        ]

        stacked = jnp.concatenate([ref[0] for ref in scaled_refs], axis=0)
        total = lax.dot_general(
            stacked, held_rows[expert], (((0,), (0,)), ((), ())), preferred_element_type=f32
        ).astype(bf16)
        side = lax.rem(lax.axis_index("ctx"), 2)
        for x in range(2):
            kept = jnp.where(side == x, 1, 0)
            out_ref[pl.ds(kept, 1), 0] = total[:, x * cols : (x + 1) * cols][None]

    def whole(shape):
        return pl.BlockSpec(shape, lambda e: (0,) * len(shape))

    return pl.pallas_call(
        kernel,
        grid=(experts,),
        out_shape=jax.ShapeDtypeStruct((2, experts, units, cols), bf16),
        in_specs=[pl.BlockSpec((1, held, units), lambda e: (e, 0, 0))] * count
        + [whole(dy_parts.shape)]
        + [whole(slots[0].shape)] * count,
        out_specs=pl.BlockSpec((2, 1, units, cols), lambda e: (0, e, 0, 0)),
        scratch_shapes=[pltpu.VMEM((experts, count * held, wide), bf16)],
        compiler_params=pltpu.CompilerParams(vmem_limit_bytes=60 * 2**20),
        cost_estimate=pl.CostEstimate(flops=0, bytes_accessed=2**20, transcendentals=0),
        name="down_grads",
    )(*scaled, dy_parts, *slots)


def roll_half(values):
    return pltpu.roll(values, values.shape[1] // 2, 1)


def allowed_keys(first_ref, last_ref, span, places):
    return (places >= first_ref[span, :]) & (places <= last_ref[span, :])


def attend(projected, scales, gains, cosine, sine_part, first, last, places, cols):
    total = projected.shape[0]
    head_dim = cosine.shape[1]
    heads = cols // head_dim
    size = math.gcd(total, 256)
    score_scale = head_dim ** (-0.5)
    f32, bf16 = jnp.float32, jnp.bfloat16

    def kernel(
        lin_ref,
        scales_ref,
        gains_ref,
        cos_ref,
        sin_ref,
        first_ref,
        last_ref,
        places_ref,
        low_ref,
        attended_ref,
        attended_low_ref,
        top_ref,
    ):
        for kind in range(3):
            for h in range(heads):
                span = pl.ds(kind * cols + h * head_dim, head_dim)
                values = lin_ref[:, span]
                if kind < 2:
                    values = values * scales_ref[:, kind : kind + 1] * gains_ref[:, span]
                    values = values * cos_ref[...] + roll_half(values) * sin_ref[...]
                low_ref[:, span] = values.astype(bf16)
        for h in range(heads):
            head = pl.ds(h * head_dim, head_dim)
            keys = low_ref[:, pl.ds(cols + h * head_dim, head_dim)]
            values = low_ref[:, pl.ds(2 * cols + h * head_dim, head_dim)]

            def step(b, carry):
                span = pl.ds(pl.multiple_of(b * size, size), size)
                scores = lax.dot_general(
                    low_ref[span, head],
                    keys,
                    (((1,), (1,)), ((), ())),
                    preferred_element_type=f32,
                )
                allowed = allowed_keys(first_ref, last_ref, span, places_ref[...])
                scores = jnp.where(allowed, scores * score_scale, MASKED)
                top = jnp.max(scores, axis=1, keepdims=True)
                weights = jnp.exp(scores - top)
                sums = jnp.sum(weights, axis=1, keepdims=True)
                probs = (weights * (1.0 / sums)).astype(bf16)
                attended = jnp.dot(probs, values, preferred_element_type=f32)
                attended_ref[span, head] = attended
                attended_low_ref[span, head] = attended.astype(bf16)
                top_ref[span, head] = jnp.broadcast_to(top + jnp.log(sums), (size, head_dim))
                return carry

            lax.fori_loop(0, total // size, step, 0)

    return pl.pallas_call(
        kernel,
        out_shape=[
            jax.ShapeDtypeStruct((total, 3 * cols), bf16),
            jax.ShapeDtypeStruct((total, cols), f32),
            jax.ShapeDtypeStruct((total, cols), bf16),
            jax.ShapeDtypeStruct((total, cols), f32),
        ],
        in_specs=[VMEM] * 8,
        out_specs=[VMEM] * 4,
        compiler_params=pltpu.CompilerParams(vmem_limit_bytes=24 * 2**20),
        cost_estimate=pl.CostEstimate(
            flops=2 * 10**9, bytes_accessed=20 * 2**20, transcendentals=2 * 10**6
        ),
        name="attend",
    )(projected, scales, gains, cosine, sine_part, first, last, places)


def attend_back(
    output_grad, low, attended, top, projected, scales, gains, cosine, sine_part, first, last, places
):
    total, cols = output_grad.shape
    head_dim = cosine.shape[1]
    heads = cols // head_dim
    size = math.gcd(total, 256)
    score_scale = head_dim ** (-0.5)
    f32, bf16 = jnp.float32, jnp.bfloat16
    contract_rows = (((0,), (0,)), ((), ()))

    def kernel(
        grad_ref,
        low_ref,
        attended_ref,
        top_ref,
        lin_ref,
        scales_ref,
        gains_ref,
        cos_ref,
        sin_ref,
        first_ref,
        last_ref,
        places_ref,
        back_ref,
        value_ref,
        gain_ref,
        sums_ref,
        query_grad,
        key_grad,
        value_grad,
    ):
        totals = [jnp.zeros((total, 1), f32) for _ in range(2)]
        for h in range(heads):
            head = pl.ds(h * head_dim, head_dim)
            keys = low_ref[:, pl.ds(cols + h * head_dim, head_dim)]
            values = low_ref[:, pl.ds(2 * cols + h * head_dim, head_dim)]
            key_grad[...] = jnp.zeros_like(key_grad)
            value_grad[...] = jnp.zeros_like(value_grad)

            def step(b, carry):
                span = pl.ds(pl.multiple_of(b * size, size), size)
                queries, grads = low_ref[span, head], grad_ref[span, head]
                scores = lax.dot_general(
                    queries, keys, (((1,), (1,)), ((), ())), preferred_element_type=f32
                )
                allowed = allowed_keys(first_ref, last_ref, span, places_ref[...])
                scores = jnp.where(allowed, scores * score_scale, MASKED)
                probs = jnp.exp(scores - top_ref[span, head][:, :1])
                prob_grad = lax.dot_general(
                    grads, values, (((1,), (1,)), ((), ())), preferred_element_type=f32
                )
                delta = jnp.sum(
                    grads.astype(f32) * attended_ref[span, head], axis=1, keepdims=True
                )
                score_grad = (probs * (prob_grad - delta)).astype(bf16)
                query_grad[span, :] = (
                    jnp.dot(score_grad, keys, preferred_element_type=f32) * score_scale
                )
                key_grad[...] += lax.dot_general(
                    score_grad, queries, contract_rows, preferred_element_type=f32
                )
                value_grad[...] += lax.dot_general(
                    probs.astype(bf16), grads, contract_rows, preferred_element_type=f32
                )
                return carry

            lax.fori_loop(0, total // size, step, 0)
            value_ref[:, head] = value_grad[...].astype(bf16)
            for kind, grad in ((0, query_grad[...]), (1, key_grad[...] * score_scale)):
                span = pl.ds(kind * cols + h * head_dim, head_dim)
                unit = lin_ref[:, span] * scales_ref[:, kind : kind + 1]
                grad = grad * cos_ref[...] - roll_half(grad) * sin_ref[...]
                gain_ref[kind, :, head] = jnp.sum(grad * unit, axis=0, keepdims=True)
                grad = grad * gains_ref[:, span]
                back_ref[kind, :, head] = grad
                totals[kind] = totals[kind] + jnp.sum(grad * unit, axis=1, keepdims=True)
        for kind in range(2):
            sums_ref[:, kind : kind + 1] = totals[kind]

    return pl.pallas_call(
        kernel,
        out_shape=[
            jax.ShapeDtypeStruct((2, total, cols), f32),
            jax.ShapeDtypeStruct((total, cols), bf16),
            jax.ShapeDtypeStruct((2, 1, cols), f32),
            jax.ShapeDtypeStruct((total, 2), f32),
        ],
        in_specs=[VMEM] * 12,
        out_specs=[VMEM] * 4,
        scratch_shapes=[pltpu.VMEM((total, head_dim), f32)] * 3,
        compiler_params=pltpu.CompilerParams(vmem_limit_bytes=60 * 2**20),
        cost_estimate=pl.CostEstimate(flops=0, bytes_accessed=2**20, transcendentals=0),
        name="attend_back",
    )(
        output_grad,
        low,
        attended,
        top,
        projected,
        scales,
        gains,
        cosine,
        sine_part,
        first,
        last,
        places,
    )


def flipped(index, bit):
    return index + bit * (1 - 2 * lax.rem(index // bit, 2))


def flipped_by(index, flip):
    for bit in (1, 2, 4):
        index = flipped(index, bit) if flip & bit else index
    return index


def add_into(target, *sources):
    step = target.shape[0] if len(target.shape) == 3 else target.shape[0] // 64

    def body(i, carry):
        span = i if len(target.shape) == 3 else pl.ds(pl.multiple_of(i * 64, 64), 64)
        total = sources[0][span].astype(jnp.float32)
        for source in sources[1:]:
            total = total + source[span].astype(jnp.float32)
        target[span] = total.astype(target.dtype)
        return carry

    lax.fori_loop(0, step, body, 0)


def finish_sums(downs, ups, gate_far, gate_own, up_far, normed_part, out_part, qkv_part, small, tokens, mixed_grad, gain, mixed, moved, collective_id):
    ctx, fsdp = lax.axis_size("ctx"), lax.axis_size("fsdp")
    experts, units, cols = gate_far.shape
    kinds = 3
    rows, width = tokens.shape
    part = out_part.shape[0]
    f32, bf16 = jnp.float32, jnp.bfloat16
    small_rows, small_cols = small.shape[0], small.shape[1] // fsdp
    copies_most = 64

    def kernel(
        downs_ref,
        ups_ref,
        gate_far_ref,
        gate_own_ref,
        up_far_ref,
        normed_ref,
        g_out_ref,
        g_qkv_ref,
        small_ref,
        tokens_ref,
        mixed_ref,
        gain_ref,
        forward_ref,
        moved_ref,
        down_ref,
        gate_ref,
        up_ref,
        input_ref,
        out_ref,
        qkv_ref,
        sums_ref,
        result_ref,
        kept,
        kept_low,
        kept_high,
        normed_own,
        normed_x,
        normed_low,
        normed_high,
        out_own,
        out_x,
        out_low,
        out_high,
        qkv_own,
        qkv_core,
        qkv_chip,
        qkv_sum,
        dealt,
        small_parts,
        small_sum,
        small_held,
        sends,
        recvs,
        locals_,
        deal_sems,
    ):
        me, mine = lax.axis_index("ctx"), lax.axis_index("fsdp")
        x, low, high = lax.rem(me, 2), lax.rem(me // 2, 2), me // 4
        to_x, to_low, to_high = ((flipped(me, bit), mine) for bit in (1, 2, 4))
        core, chip = flipped(mine, 1), flipped(mine, 2)
        diagonal = flipped(core, 2)
        ctx_peers = [(lax.rem(me + step, ctx), mine) for step in range(1, ctx)]
        near = [lax.rem(mine + step, fsdp) for step in range(1, fsdp)]
        greet(ctx_peers + [(me, other) for other in near])
        used, used_local, all_sends, loads = [0], [0], [], {}

        def push(source, target, peer):
            i = used[0]
            used[0] += 1
            copy = send(source, target, sends.at[i], recvs.at[i], peer)
            all_sends.append(copy)
            return copy

        def load(source, target):
            i = used_local[0]
            used_local[0] += 1
            copy = pltpu.make_async_copy(source, target, locals_.at[i])
            copy.start()
            return copy

        def normed_block(a, b, other):
            side = 1 - x if other else x
            block = (high + a - 2 * a * high) * 4 + (low + b - 2 * b * low) * 2 + side
            return normed_ref.at[pl.ds(pl.multiple_of(block * rows, rows), rows), :]

        def out_block(a, b, other):
            side = 1 - x if other else x
            block = (high + a - 2 * a * high) * 4 + (low + b - 2 * b * low) * 2 + side
            return g_out_ref.at[:, pl.ds(pl.multiple_of(block * cols, cols), cols)]

        def qkv_block(index):
            return g_qkv_ref.at[pl.ds(pl.multiple_of(index * part, part), part), :]

        def columns(index):
            return pl.ds(pl.multiple_of(index * small_cols, small_cols), small_cols)

        order = ((1, 1), (0, 1), (1, 0), (0, 0))
        small_copies = [
            push(small_ref.at[:, columns(other)], small_parts.at[i], (me, other))
            for i, other in enumerate(near)
        ]
        normed_copies = {
            ab: push(normed_block(*ab, True), normed_x.at[ab[0], ab[1]], to_x) for ab in order
        }

        def push_low(kind, a):
            return push(ups_ref.at[kind - 1, 0, a], kept_low.at[kind, a], to_low)

        low_copies = {
            (2, 0): push_low(2, 0),
            (0, 0): push(downs_ref.at[0], kept_low.at[0, 0], to_x),
        }
        early = {
            (1, 1): load(gate_far_ref, kept_low.at[1, 1]),
            (2, 1): load(up_far_ref, kept_low.at[2, 1]),
            (1, 0): load(gate_own_ref, kept_low.at[1, 0]),
        }
        kept_loads = {
            (kind, a): load(
                downs_ref.at[1] if kind == 0 else ups_ref.at[kind - 1, 1, a], kept.at[kind, a]
            )
            for kind, a in ((1, 1), (2, 1), (0, 0), (1, 0), (2, 0))
        }
        qkv_copies = [
            push(qkv_block(diagonal), qkv_core.at[1], (me, core)),
            push(qkv_block(core), qkv_core.at[0], (me, core)),
        ]
        qkv_loads = [
            load(qkv_block(chip), qkv_own.at[1]),
            load(qkv_block(mine), qkv_own.at[0]),
        ]
        normed_loads = {
            ab: load(normed_block(*ab, False), normed_own.at[ab[0], ab[1]]) for ab in order
        }
        out_loads = {ab: load(out_block(*ab, False), out_own.at[ab[0], ab[1]]) for ab in order}

        total = small_ref[:, columns(mine)]
        for i, copy in enumerate(small_copies):
            copy.wait_recv()
            total = total + small_parts[i]
        small_sum[...] = total
        small_wide = [push(small_sum, small_held.at[i], peer) for i, peer in enumerate(ctx_peers)]

        qkv_copies[0].wait_recv()
        qkv_loads[0].wait()
        add_into(qkv_core.at[1], qkv_own.at[1], qkv_core.at[1])
        chip_copy = push(qkv_core.at[1], qkv_chip, (me, chip))

        def to_low_side(copies, loads, own, from_x, from_low, a):
            copies[a, 1].wait_recv()
            loads[a, 1].wait()
            add_into(from_x.at[a, 1], own.at[a, 1], from_x.at[a, 1])
            return push(from_x.at[a, 1], from_low.at[a], to_low)

        def to_high_side(copies, loads, lows, own, from_x, from_low, from_high):
            copies[1, 0].wait_recv()
            loads[1, 0].wait()
            lows[1].wait_recv()
            add_into(from_x.at[1, 0], own.at[1, 0], from_x.at[1, 0], from_low.at[1])
            return push(from_x.at[1, 0], from_high, to_high)

        def arrived(kind, a):
            if (kind, a) in early:
                early[kind, a].wait()
            else:
                low_copies[kind, a].wait_recv()

        def experts_high(kind):
            arrived(kind, 1)
            kept_loads[kind, 1].wait()
            add_into(kept_low.at[kind, 1], kept.at[kind, 1], kept_low.at[kind, 1])
            return push(kept_low.at[kind, 1], kept_high.at[kind], to_high)

        high_copies = {1: experts_high(1)}
        normed_args = (normed_copies, normed_loads)
        normed_lows = {1: to_low_side(*normed_args, normed_own, normed_x, normed_low, 1)}
        high_copies[2] = experts_high(2)
        normed_lows[0] = to_low_side(*normed_args, normed_own, normed_x, normed_low, 0)
        out_copies = {ab: push(out_block(*ab, True), out_x.at[ab[0], ab[1]], to_x) for ab in order}

        qkv_copies[1].wait_recv()
        qkv_loads[1].wait()
        chip_copy.wait_recv()
        add_into(qkv_sum, qkv_own.at[0], qkv_core.at[0], qkv_chip)

        def deal(kind):
            index = kind * ctx + me
            return pltpu.make_async_remote_copy(
                qkv_sum.at[:, pl.ds(kind * cols, cols)],
                dealt.at[lax.rem(index, kinds)],
                deal_sems.at[0, kind],
                deal_sems.at[1, lax.rem(index, kinds)],
                device_id=(index // kinds, mine),
                device_id_type=MESH,
            )

        def keep(kind):
            return pltpu.make_async_copy(
                qkv_sum.at[:, pl.ds(kind * cols, cols)],
                dealt.at[lax.rem(kind * ctx + me, kinds)],
                deal_sems.at[0, kind],
            )

        def is_far(kind):
            return (kind * ctx + me) // kinds != me

        for kind in range(kinds):
            pl.when(is_far(kind))(deal(kind).start)
            pl.when(jnp.logical_not(is_far(kind)))(keep(kind).start)

        normed_high_copy = to_high_side(
            *normed_args, normed_lows, normed_own, normed_x, normed_low, normed_high
        )
        out_args = (out_copies, out_loads)
        out_lows = {a: to_low_side(*out_args, out_own, out_x, out_low, a) for a in (1, 0)}

        def experts_end(kind):
            arrived(kind, 0)
            kept_loads[kind, 0].wait()
            sources = [kept.at[kind, 0], kept_low.at[kind, 0]]
            if kind > 0:
                high_copies[kind].wait_recv()
                sources.append(kept_high.at[kind])
            add_into((down_ref, gate_ref, up_ref)[kind], *sources)

        experts_end(0)

        normed_copies[0, 0].wait_recv()
        normed_loads[0, 0].wait()
        normed_lows[0].wait_recv()
        normed_high_copy.wait_recv()

        def norm_step(i, carry):
            span = pl.ds(pl.multiple_of(i * 16, 16), 16)
            grad = (
                normed_own[0, 0, span, :].astype(f32)
                + normed_x[0, 0, span, :].astype(f32)
                + normed_low[0, span, :].astype(f32)
                + normed_high[span, :].astype(f32)
            )
            values = tokens_ref[span, :].astype(f32)
            scale = rms_unit(values)
            unit = values * scale
            pulled = grad * gain_ref[...]
            input_ref[span, :] = mixed_ref[span, :] + scale * (
                pulled - unit * jnp.mean(unit * pulled, axis=-1, keepdims=True)
            )
            result_ref[span, :] = (forward_ref[span, :] + moved_ref[span, :].astype(f32)).astype(bf16)
            return carry

        lax.fori_loop(0, rows // 16, norm_step, 0)

        out_high_copy = to_high_side(*out_args, out_lows, out_own, out_x, out_low, out_high)
        experts_end(1)

        total = small_sum[...]
        for i, copy in enumerate(small_wide):
            copy.wait_recv()
            total = total + small_held[i]
        sums_ref[...] = total

        for kind in range(kinds):
            pl.when(is_far(kind))(deal(kind).wait_send)
            pl.when(jnp.logical_not(is_far(kind)))(keep(kind).wait)
        for slot in range(kinds):

            @pl.when(lax.rem(me * kinds + slot, ctx) != me)
            def _():
                pltpu.make_async_copy(
                    dealt.at[slot], dealt.at[slot], deal_sems.at[1, slot]
                ).wait()

            add_into(qkv_ref.at[:, pl.ds(slot * cols, cols)], dealt.at[slot])

        out_copies[0, 0].wait_recv()
        out_loads[0, 0].wait()
        out_lows[0].wait_recv()
        out_high_copy.wait_recv()
        add_into(out_ref, out_own.at[0, 0], out_x.at[0, 0], out_low.at[0], out_high)
        experts_end(2)
        for copy in all_sends:
            copy.wait_send()

    def block(*shape):
        return pltpu.VMEM(shape, bf16)

    gradient = (experts, units, cols)
    return comm_call(
        kernel,
        "finish_sums",
        collective_id,
        [
            jax.ShapeDtypeStruct(gradient, f32),
            jax.ShapeDtypeStruct(gradient, f32),
            jax.ShapeDtypeStruct(gradient, f32),
            jax.ShapeDtypeStruct((rows, width), f32),
            jax.ShapeDtypeStruct((part, cols), f32),
            jax.ShapeDtypeStruct((part, kinds * cols), f32),
            jax.ShapeDtypeStruct((small_rows, small_cols), f32),
            jax.ShapeDtypeStruct((rows, width), bf16),
        ],
        [ANY] * 8 + [VMEM] * 6,
        [VMEM] * 8,
        [
            block(kinds, 2, *gradient),
            block(kinds, 2, *gradient),
            block(kinds, *gradient),
            block(2, 2, rows, width),
            block(2, 2, rows, width),
            block(2, rows, width),
            block(rows, width),
            block(2, 2, part, cols),
            block(2, 2, part, cols),
            block(2, part, cols),
            block(part, cols),
            block(2, part, kinds * cols),
            block(2, part, kinds * cols),
            block(part, kinds * cols),
            block(part, kinds * cols),
            block(kinds, part, cols),
            pltpu.VMEM((fsdp - 1, small_rows, small_cols), f32),
            pltpu.VMEM((small_rows, small_cols), f32),
            pltpu.VMEM((ctx - 1, small_rows, small_cols), f32),
            DMA((copies_most,)),
            DMA((copies_most,)),
            DMA((32,)),
            DMA((2, kinds)),
        ],
        700 * 2**20,
        56,
    )(
        downs,
        ups,
        gate_far,
        gate_own,
        up_far,
        normed_part,
        out_part,
        qkv_part,
        small,
        tokens,
        mixed_grad,
        gain,
        mixed,
        moved,
    )


def gather_inputs(tokens, w_qkv, dy, row_arrays, block, flips, collective_id):
    ctx, fsdp = lax.axis_size("ctx"), lax.axis_size("fsdp")
    rows, width = tokens.shape
    part = w_qkv.shape[0]
    kinds = 3
    cols = width // ctx
    line = ctx // 2
    chunks = 2
    size = rows // chunks
    row_count, flip_count = len(row_arrays), len(flips)
    small_count = row_count + 1

    def kernel(*refs):
        tokens_ref, w_qkv_ref, dy_ref = refs[:3]
        small_refs = refs[3 : 3 + small_count]
        all_ref, weight_ref, dy_all_ref = refs[3 + small_count : 6 + small_count]
        small_all_refs = refs[6 + small_count : 6 + 2 * small_count]
        refs = refs[6 + 2 * small_count :]
        run_kernel(
            tokens_ref,
            w_qkv_ref,
            dy_ref,
            small_refs,
            all_ref,
            weight_ref,
            dy_all_ref,
            small_all_refs,
            *refs,
        )

    def run_kernel(
        tokens_ref,
        w_qkv_ref,
        dy_ref,
        small_refs,
        all_ref,
        weight_ref,
        dy_all_ref,
        small_all_refs,
        *refs,
    ):
        flip_refs, dy_line_ref, refs = refs[:flip_count], refs[flip_count], refs[flip_count + 1 :]
        sends, recvs, line_send, line_recv, cross_send, cross_recv, local_sems = refs
        me, mine = lax.axis_index("ctx"), lax.axis_index("fsdp")
        z, x = me // 2, lax.rem(me, 2)
        to_x = (flipped(me, 1), mine)
        core, chip = (me, flipped(mine, 1)), (me, flipped(mine, 2))
        others = [flipped_by(me, flip) for flip in flips]
        greet(
            [(lax.rem(me + step, ctx), mine) for step in range(1, ctx)]
            + [(me, lax.rem(mine + step, fsdp)) for step in range(1, fsdp)]
            + [(other, lax.rem(mine + step, fsdp)) for other in others for step in range(1, fsdp)]
        )
        used, used_local, started, kept = [0], [0], [], []

        def push(source, target, peer):
            i = used[0]
            used[0] += 1
            copy = send(source, target, sends.at[i], recvs.at[i], peer)
            started.append(copy)
            return copy

        def load(source, target):
            i = used_local[0]
            used_local[0] += 1
            copy = pltpu.make_async_copy(source, target, local_sems.at[i])
            copy.start()
            kept.append(copy)

        def token_block(index):
            return all_ref.at[pl.ds(pl.multiple_of(index * rows, rows), rows), :]

        def token_chunk(index, chunk):
            start = pl.multiple_of(index * rows + chunk * size, size)
            return all_ref.at[pl.ds(start, size), :]

        def taken(own, index, chunk):
            return tokens_ref.at[pl.ds(chunk * size, size), :] if own else token_chunk(index, chunk)

        def by_part(ref, index, count):
            return ref.at[pl.ds(pl.multiple_of(index * count, count), count), :]

        def cross(away, side, chunk):
            index = 2 * (z - away if side == 0 else z + away) + x
            i = side * line + away
            return pltpu.make_async_remote_copy(
                taken(away == 0, index, chunk),
                token_chunk(index, chunk),
                cross_send.at[i, chunk],
                cross_recv.at[i, chunk],
                device_id=to_x,
                device_id_type=MESH,
            )

        def along(away, side, chunk):
            index = 2 * (z - away if side == 0 else z + away) + x
            i = side * line + away
            return pltpu.make_async_remote_copy(
                taken(away == 0, index, chunk),
                token_chunk(index, chunk),
                line_send.at[i, chunk],
                line_recv.at[i, chunk],
                device_id=(me + 2 if side == 0 else me - 2, mine),
                device_id_type=MESH,
            )

        def has(away, side):
            return z >= away if side == 0 else z + away < line

        def goes_on(away, side):
            return jnp.logical_and(has(away, side), z < line - 1 if side == 0 else z > 0)

        for chunk in range(chunks):
            for side in range(2):
                pl.when(goes_on(0, side))(along(0, side, chunk).start)
            cross(0, 0, chunk).start()
        load(tokens_ref, token_block(me))

        weight_chip = []
        for kind in range(kinds):
            column = pl.ds(pl.multiple_of(kind * width + me * cols, cols), cols)
            target = by_part(weight_ref, mine, part).at[:, pl.ds(kind * cols, cols)]
            source = w_qkv_ref.at[:, column]
            weight_chip.append(push(source, target, chip))
            push(source, target, core)
            load(source, target)
        columns = pl.ds(pl.multiple_of(mine * part, part), part)
        for i, (source, target) in enumerate(zip(small_refs, small_all_refs)):
            if i < row_count:
                target = target.at[:, columns]
            else:
                target = target.at[mine]
            for step in range(1, fsdp):
                push(source, target, (me, lax.rem(mine + step, fsdp)))
            load(source, target)
        dy_chip = push(dy_ref, by_part(dy_all_ref, mine, rows), chip)
        push(dy_ref, by_part(dy_all_ref, mine, rows), core)
        load(dy_ref, by_part(dy_all_ref, mine, rows))

        for away in range(1, line):
            for chunk in range(chunks):
                for side in range(2):

                    @pl.when(has(away, side))
                    def _():
                        index = 2 * (z - away if side == 0 else z + away) + x
                        pltpu.make_async_copy(
                            taken(True, index, chunk),
                            token_chunk(index, chunk),
                            line_recv.at[side * line + away - 1, chunk],
                        ).wait()
                        cross(away, side, chunk).start()

                    if away < line - 1:
                        pl.when(goes_on(away, side))(along(away, side, chunk).start)
            if away == 1:
                for copy in weight_chip:
                    copy.wait_recv()
                far = by_part(weight_ref, flipped(mine, 2), part)
                push(far, far, core)
            if away == 2:
                dy_chip.wait_recv()
                far = by_part(dy_all_ref, flipped(mine, 2), rows)
                push(far, far, core)
        for other, target in zip(others, flip_refs):
            for step in range(fsdp):
                push(small_refs[-1], target.at[mine], (other, lax.rem(mine + step, fsdp)))
        for i in range(line):
            wide = 2 * cols
            to = flipped_by(me, 2 * i)
            source = dy_ref.at[:, pl.ds(pl.multiple_of(to // 2 * wide, wide), wide)]
            if i == 0:
                load(source, dy_line_ref.at[0])
            else:
                push(source, dy_line_ref.at[i], (to, mine))

        every = [(side, chunk) for side in range(2) for chunk in range(chunks)]
        for chunk in range(chunks):
            cross(0, 0, chunk).wait_recv()
        for away in range(1, line):
            for side, chunk in every:
                pl.when(has(away, side))(cross(away, side, chunk).wait_recv)
        for copy in started:
            if copy is not dy_chip and not any(copy is other for other in weight_chip):
                copy.wait_recv()
        for copy in kept:
            copy.wait()
        for copy in started:
            copy.wait_send()
        for chunk in range(chunks):
            cross(0, 0, chunk).wait_send()
        for away in range(line - 1):
            for side, chunk in every:
                pl.when(goes_on(away, side))(along(away, side, chunk).wait_send)
        for away in range(1, line):
            for side, chunk in every:
                pl.when(has(away, side))(cross(away, side, chunk).wait_send)

    return comm_call(
        kernel,
        "gather_inputs",
        collective_id,
        [
            jax.ShapeDtypeStruct((ctx * rows, width), tokens.dtype),
            jax.ShapeDtypeStruct((fsdp * part, kinds * cols), w_qkv.dtype),
            jax.ShapeDtypeStruct((fsdp * rows, width), dy.dtype),
        ]
        + [jax.ShapeDtypeStruct((row.shape[0], fsdp * part), row.dtype) for row in row_arrays]
        + [jax.ShapeDtypeStruct((fsdp,) + block.shape, block.dtype)] * (1 + flip_count)
        + [jax.ShapeDtypeStruct((line, rows, 2 * cols), dy.dtype)],
        [HBM] * (3 + small_count),
        [HBM] * (4 + small_count + flip_count),
        [
            DMA((64,)),
            DMA((64,)),
            DMA((2 * line, chunks)),
            DMA((2 * line, chunks)),
            DMA((2 * line, chunks)),
            DMA((2 * line, chunks)),
            DMA((16,)),
        ],
        150 * 2**20,
    )(tokens, w_qkv, dy, *row_arrays, block)


def project(tokens, gain, weight):
    total, width = tokens.shape
    wide = weight.shape[1]
    cols = wide // 3
    size = math.gcd(total, 256)
    f32 = jnp.float32

    def kernel(tokens_ref, gain_ref, weight_ref, normed_ref, lin_ref, squares_ref):
        values = tokens_ref[...].astype(f32)
        normed = (values * rms_unit(values) * gain_ref[...]).astype(jnp.bfloat16)
        normed_ref[...] = normed
        lin = jnp.dot(normed, weight_ref[...], preferred_element_type=f32)
        lin_ref[...] = lin
        for kind in range(2):
            piece = lin[:, kind * cols : (kind + 1) * cols]
            squares_ref[:, kind : kind + 1] = jnp.sum(piece * piece, axis=1, keepdims=True)

    def by_rows(columns):
        return pl.BlockSpec((size, columns), lambda i: (i, 0))

    return pl.pallas_call(
        kernel,
        grid=(total // size,),
        out_shape=[
            jax.ShapeDtypeStruct((total, width), jnp.bfloat16),
            jax.ShapeDtypeStruct((total, wide), f32),
            jax.ShapeDtypeStruct((total, 2), f32),
        ],
        in_specs=[
            by_rows(width),
            pl.BlockSpec((1, width), lambda i: (0, 0)),
            pl.BlockSpec((width, wide), lambda i: (0, 0)),
        ],
        out_specs=[by_rows(width), by_rows(wide), by_rows(2)],
        compiler_params=pltpu.CompilerParams(vmem_limit_bytes=24 * 2**20),
        cost_estimate=pl.CostEstimate(
            flops=3 * 10**9, bytes_accessed=15 * 2**20, transcendentals=0
        ),
        name="project",
    )(tokens, gain, weight)


def project_back(back, projected, scales, inner_sums, value_grad, weight, normed, tokens):
    total, width = tokens.shape
    wide = weight.shape[1]
    cols = wide // 3
    size = math.gcd(total, 256)
    steps, runs = total // size, 4
    f32, bf16 = jnp.float32, jnp.bfloat16

    def kernel(
        back_ref,
        lin_ref,
        scales_ref,
        sums_ref,
        value_ref,
        weight_ref,
        normed_ref,
        tokens_ref,
        part_ref,
        g_qkv_ref,
        gain_ref,
        proj,
    ):
        i = pl.program_id(0)

        @pl.when(i == 0)
        def _():
            gain_ref[...] = jnp.zeros_like(gain_ref)

        @pl.when(i < steps)
        def _():
            pieces = []
            for kind in range(2):
                scale = scales_ref[:, kind : kind + 1]
                unit = lin_ref[:, kind * cols : (kind + 1) * cols] * scale
                grad = scale * (back_ref[kind] - unit * sums_ref[:, kind : kind + 1])
                pieces.append(grad.astype(bf16))
            grads = jnp.concatenate(pieces + [value_ref[...]], axis=1)
            proj[pl.ds(pl.multiple_of(i * size, size), size), :] = grads
            part = lax.dot_general(
                grads, weight_ref[...], (((1,), (1,)), ((), ())), preferred_element_type=f32
            )
            values = tokens_ref[...].astype(f32)
            gain_ref[...] += jnp.sum(part * (values * rms_unit(values)), axis=0, keepdims=True)
            part_ref[...] = part.astype(bf16)

        @pl.when(i >= steps)
        def _():
            g_qkv_ref[...] = lax.dot_general(
                normed_ref[...], proj[...], (((0,), (0,)), ((), ())), preferred_element_type=f32
            ).astype(bf16)

    def by_rows(columns):
        return pl.BlockSpec((size, columns), lambda i: (jnp.minimum(i, steps - 1), 0))

    def later(i):
        return jnp.maximum(i - steps, 0)

    return pl.pallas_call(
        kernel,
        grid=(steps + runs,),
        out_shape=[
            jax.ShapeDtypeStruct((total, width), bf16),
            jax.ShapeDtypeStruct((width, wide), bf16),
            jax.ShapeDtypeStruct((1, width), f32),
        ],
        in_specs=[
            pl.BlockSpec((2, size, cols), lambda i: (0, jnp.minimum(i, steps - 1), 0)),
            by_rows(wide),
            by_rows(2),
            by_rows(2),
            by_rows(cols),
            pl.BlockSpec((width, wide), lambda i: (0, 0)),
            pl.BlockSpec((total, width // runs), lambda i: (0, later(i))),
            by_rows(width),
        ],
        out_specs=[
            by_rows(width),
            pl.BlockSpec((width // runs, wide), lambda i: (later(i), 0)),
            pl.BlockSpec((1, width), lambda i: (0, 0)),
        ],
        scratch_shapes=[pltpu.VMEM((total, wide), bf16)],
        compiler_params=pltpu.CompilerParams(vmem_limit_bytes=60 * 2**20),
        cost_estimate=pl.CostEstimate(flops=0, bytes_accessed=2**20, transcendentals=0),
        name="project_back",
    )(back, projected, scales, inner_sums, value_grad, weight, normed, tokens)


def on_device_heads(
    tokens,
    doc_lengths,
    routes,
    slot_order,
    attn_gain,
    w_qkv,
    q_gain,
    k_gain,
    w_out,
    ffn_gain,
    w_router,
    w_gate,
    w_up,
    w_down,
    cotangent,
):
    rows, width = tokens.shape[1], tokens.shape[2]
    ctx, fsdp = lax.axis_size("ctx"), lax.axis_size("fsdp")
    me = lax.axis_index("ctx")
    head_dim = width // HEADS
    cols = HEADS // ctx * head_dim
    part = width // fsdp
    total = rows * ctx
    lengths = doc_lengths[0]
    bf16, f32 = jnp.bfloat16, jnp.float32

    experts, top = w_gate.shape[0], routes.shape[2]
    gains = jnp.concatenate([attn_gain, q_gain, k_gain, ffn_gain]).reshape(4, part)
    router_rows = jnp.pad(w_router.T, ((0, ROUTER_ROWS - experts), (0, 0)))
    pairs = jnp.concatenate([routes[0].T, slot_order[0].T], axis=0)
    pairs = jnp.pad(pairs, ((0, -pairs.shape[0] % 8), (0, 0)))
    tokens_all, qkv_weight, dy_all, gains, router_rows, *pairs, dy_parts = gather_inputs(
        tokens[0], w_qkv, cotangent[0], [gains, router_rows], pairs, [1, 2, 4, 6], 9
    )
    row_gain_one, gain_query, gain_key, row_gain_two = (
        gains[i : i + 1].astype(f32) for i in range(4)
    )
    flips = [0, 2, 4, 6]
    dy_parts = lax.all_gather(dy_parts, "fsdp", axis=0)

    stream_pos = dealt_position(jnp.arange(total, dtype=jnp.int32), rows, ctx)
    stream_doc, stream_inner = document_info(stream_pos, lengths)
    cosine, sine_part = rope_tables(stream_inner, head_dim)
    turn_tables = (
        jnp.concatenate([cosine, cosine], axis=1),
        jnp.concatenate([-sine_part, sine_part], axis=1),
    )
    sight = (
        (stream_pos - stream_inner).reshape(total, 1),
        stream_pos.reshape(total, 1),
        stream_pos.reshape(1, total),
    )
    normed_all, projected, squares = project(tokens_all, row_gain_one, qkv_weight)
    squares = squares.T
    squares = ctx_sum(squares.reshape(-1, 128), 1).reshape(2, total)
    scales = lax.rsqrt(squares / width + EPSILON).T
    own_gains = [
        lax.dynamic_slice_in_dim(gain, me * cols, cols, 1) for gain in (gain_query, gain_key)
    ]
    own_gains = jnp.concatenate(own_gains, axis=1)
    low, attended, attended_low, tops = attend(
        projected, scales, own_gains, *turn_tables, *sight, cols
    )

    attended_part = heads_to_rows(attended_low, 2)
    mixed_part = dot32("td,de->te", attended_part, w_out).astype(bf16)
    inputs = tokens[0].astype(f32)
    group, mixed, crossed = reduce_then_gather(
        mixed_part,
        [tokens[0], row_gain_two],
        [jax.ShapeDtypeStruct((rows, width), f32)],
        norm_chunk,
        "mix_and_norm",
        6,
        True,
        [],
    )

    capacity = rows * top // experts
    slot_by_expert, slots_other, *slots_line = slots_of(pairs, experts, top)
    moved_part, group_grad, g_router, scaled, gate_low, up_low = run_experts(
        group, dy_all, slot_by_expert, router_rows, w_gate, w_up, w_down, fsdp, capacity
    )
    scaled_line = [scaled] + [swap(scaled, flip) for flip in flips[1:]]
    mixed_all, mixed_grad, g_ffn_gain, gate_other, up_other = reduce_then_gather(
        group_grad,
        [mixed, row_gain_two, cotangent[0]],
        [jax.ShapeDtypeStruct((rows, width), f32), jax.ShapeDtypeStruct((1, width), f32)],
        norm_back_chunk,
        "norm_back",
        7,
        False,
        [gate_low, up_low],
    )
    g_ffn_gain = g_ffn_gain[0]
    crossed = lax.all_gather(crossed, "fsdp", axis=0, tiled=True)
    ups = expert_grads(
        [gate_low, up_low], [gate_other, up_other], group, crossed, slot_by_expert, slots_other, capacity
    )
    ups, mixed_all = lax.optimization_barrier((ups, mixed_all))
    output_part = dot32("te,de->td", mixed_all, w_out).astype(bf16)
    output_grad = rows_to_heads(output_part, 3)
    output_grad, moved_part, ups, mixed_all, *scaled_line = lax.optimization_barrier(
        (output_grad, moved_part, ups, mixed_all, *scaled_line)
    )
    moved = lax.psum_scatter(moved_part, "fsdp", scatter_dimension=0, tiled=True)
    gate_far, gate_own = swap(ups[0, 0, 1], 2), swap(ups[0, 0, 0], 2)
    downs = down_grads(scaled_line, dy_parts, [slot_by_expert] + slots_line, capacity)
    g_out = dot32("td,te->de", attended_part, mixed_all).astype(bf16)
    output_grad, ups, downs, g_out = lax.optimization_barrier((output_grad, ups, downs, g_out))

    back, value_grad, own_g_gains, inner_sums = attend_back(
        output_grad, low, attended, tops, projected, scales, own_gains, *turn_tables, *sight
    )
    inner_sums, gate_far, gate_own = lax.optimization_barrier((inner_sums, gate_far, gate_own))
    inner_sums = ctx_sum(inner_sums.T.reshape(-1, 128), 1)
    inner_sums, ups = lax.optimization_barrier((inner_sums, ups))
    up_far = swap(ups[1, 0, 1], 2)
    inner_sums = inner_sums.reshape(2, total).T / width

    normed_grad_part, g_qkv, g_attn_gain = project_back(
        back, projected, scales, inner_sums, value_grad, qkv_weight, normed_all, tokens_all
    )
    g_attn_gain = g_attn_gain[0]

    def placed_cols(values):
        return lax.dynamic_update_slice_in_dim(jnp.zeros((width,), f32), values, me * cols, 0)

    sums = jnp.concatenate(
        [
            jnp.stack([g_attn_gain, placed_cols(own_g_gains[0, 0]), placed_cols(own_g_gains[1, 0]), g_ffn_gain]),
            g_router[:experts],
        ],
        axis=0,
    )
    down_parts, gate_parts, up_parts, input_grad, out_part, qkv_part, sums, activations = finish_sums(
        downs,
        ups,
        gate_far,
        gate_own,
        up_far,
        normed_grad_part,
        g_out,
        g_qkv,
        jnp.pad(sums, ((0, -sums.shape[0] % 8), (0, 0))),
        tokens[0],
        mixed_grad,
        row_gain_one,
        mixed,
        moved,
        8,
    )
    return (
        activations[None],
        input_grad[None],
        sums[0],
        qkv_part,
        sums[1],
        sums[2],
        out_part,
        sums[3],
        sums[4 : 4 + experts].T,
        gate_parts,
        up_parts,
        down_parts,
    )


def solution(mesh):
    in_specs = (
        P("fsdp", "ctx", None),
        P("fsdp", None),
        P("fsdp", "ctx", None),
        P("fsdp", "ctx", None),
        P("fsdp"),
        P("fsdp", None),
        P("fsdp"),
        P("fsdp"),
        P("fsdp", None),
        P("fsdp"),
        P("fsdp", None),
        P(None, None, "fsdp"),
        P(None, None, "fsdp"),
        P(None, "fsdp", None),
        P("fsdp", "ctx", None),
    )
    out_specs = (
        P("fsdp", "ctx", None),
        P("fsdp", "ctx", None),
        P("fsdp"),
        P("fsdp", "ctx"),
        P("fsdp"),
        P("fsdp"),
        P("fsdp", "ctx"),
        P("fsdp"),
        P("fsdp", None),
        P(None, "ctx", "fsdp"),
        P(None, "ctx", "fsdp"),
        P(None, "fsdp", "ctx"),
    )
    ctx, fsdp = mesh.shape["ctx"], mesh.shape["fsdp"]
    by_heads = HEADS % ctx == 0 and ctx == 8 and fsdp == 4
    body = on_device_heads if by_heads else on_device
    return jax.shard_map(
        body, mesh=mesh, in_specs=in_specs, out_specs=out_specs, check_vma=False
    )
```

profile of v0, /device:TPU:5, one launch (start us, length us, event | category | flops | bytes accessed | tf_op | source)
XLA Modules:
  0.0 511.2 jit_solution(3198664920590458276)
XLA Ops:
  7.4 1.1 pad_maximum_fusion.2
  8.5 0.7 copy_bitcast_fusion
  9.2 0.7 pad.12.refs_4_
  9.9 2.8 copy-done.3
  12.7 1.0 copy-done.5
  13.8 1.0 copy-done.17
  14.8 54.7 %gather_inputs.1 = (bf16[1024,2048]{1,0:T(8,128)(2,1)S(1)}, bf16[2048,768]{1,0:T(8,128)(2,1)S(1)}, bf16[512,2048]{1,0:T(8,128)(2,1)S(1)}, bf16[4,2048]{1,0:T(4,1...) custom-call(bf16[128,2048]{1,0:T(8,128)(2,1)S(1)} %bitcast.46, ...), custom_call_target="tpu_custom_call" | custom-call | bytes 157286400 | tf_op jit(solution)/shard_map/gather_inputs/pallas_call | solution.py:1998
  69.5 2.0 copy-done.7
  71.5 1.7 copy-done.12
  76.2 1.3 copy-done.41
  78.2 2.2 copy-done.8
  80.4 1.9 copy-done.13
  82.3 5.3 %project.1 = (bf16[1024,2048]{1,0:T(8,128)(2,1)S(1)}, f32[1024,768]{1,0:T(8,128)S(1)}, f32[1024,2]{1,0:T(8,128)S(1)}) custom-call(bf16[1024,2048]{1,0:T(8,128)(2,1)S(1)} %copy-done.8, f32[1,2048]{1,0:T(1,128)S(1)} %get-tuple-element.163.gain_ref, bf16[2048,768]{1,0:T(8,128)(2,1)S(1)} %copy-done.13), custom_call_target="tpu_custom_call" | custom-call | flops 3000000000 | bytes 15728640 | tf_op jit(solution)/shard_map/project/pallas_call | solution.py:2045
  87.6 1.6 copy-done.1
  89.2 2.0 copy-done.9
  91.4 5.4 %ctx_sum.2 = f32[16,128]{1,0:T(8,128)S(1)} custom-call(f32[16,128]{1,0:T(8,128)S(1)} %reshape.211.own_ref), custom_call_target="tpu_custom_call" | custom-call | bytes 20971520 | tf_op jit(solution)/shard_map/ctx_sum/pallas_call | solution.py:538
  97.3 1.0 copy.43.first_ref
  98.4 1.9 fusion.15
  100.7 8.2 %attend.1 = (bf16[1024,768]{1,0:T(8,128)(2,1)S(1)}, f32[1024,256]{1,0:T(8,128)S(1)}, bf16[1024,256]{1,0:T(8,128)(2,1)S(1)}, f32[1024,256]{1,0:T(8,128)S(1)}) custom-call(f32[1024,768]{1,0:T(8,128)S(1)} %copy-done.2, f32[1024,2]{1,0:T(8,128)S(1)} %bitcast.42, f32[1,512]{1,0:T(1,128)S(1)} %pad_maximum_fusion.3.gains_ref, ...), custom_call_target="tpu_custom_call" | custom-call | flops 2000000000 | bytes 20971520 | tf_op jit(solution)/shard_map/attend/pallas_call | solution.py:1299
  109.0 15.5 %heads_to_rows.1 = bf16[512,512]{1,0:T(8,128)(2,1)S(1)} custom-call(bf16[1024,256]{1,0:T(8,128)(2,1)S(1)} %get-tuple-element.88.own_ref), custom_call_target="tpu_custom_call" | custom-call | bytes 41943040 | tf_op jit(solution)/shard_map/heads_to_rows/pallas_call | solution.py:627
  124.5 1.3 convolution_convert_fusion.1.refs_0_
  125.9 29.1 %mix_and_norm.1 = (bf16[512,2048]{1,0:T(8,128)(2,1)S(1)}, f32[128,2048]{1,0:T(8,128)S(1)}, bf16[128,1024]{1,0:T(8,128)(2,1)}) custom-call(bf16[512,2048]{1,0:T(8,128)(2,1)S(1)} %convolution_convert_fusion.1.refs_0_, bf16[128,2048]{1,0:T(8,128)(2,1)S(1)} %bitcast.47, f32[1,2048]{1,0:T(1,128)S(1)} %get-tuple-element.160.refs_2_), custom_call_target="tpu_custom_call" | custom-call | bytes 104857600 | tf_op jit(solution)/shard_map/mix_and_norm/pallas_call | solution.py:822
  155.0 1.0 copy-done.10
  156.0 1.4 copy-done.24
  158.5 4.0 slots_of.1
  162.5 25.3 %run_experts.1 = (bf16[512,2048]{1,0:T(8,128)(2,1)}, bf16[512,2048]{1,0:T(8,128)(2,1)}, f32[16,2048]{1,0:T(8,128)}, bf16[6,256,256]{2,1,0:T(8,128)(2,1)}, bf16[6...) custom-call(bf16[512,2048]{1,0:T(8,128)(2,1)} %copy-done.24, bf16[512,2048]{1,0:T(8,128)(2,1)} %copy-done.41, ...), custom_call_target="tpu_custom_call" | custom-call | flops 30000001024 | bytes 31457280 | tf_op jit(solution)/shard_map/run_experts/pallas_call | solution.py:1057
  187.8 0.9 collective-permute-start
  188.7 4.6 collective-permute-start.1
  193.3 1.1 copy-done.14
  194.5 1.1 copy-done.15
  195.6 1.6 copy-done.16
  197.2 36.1 %norm_back.1 = (bf16[512,2048]{1,0:T(8,128)(2,1)S(1)}, f32[128,2048]{1,0:T(8,128)S(1)}, f32[1,2048]{1,0:T(1,128)S(1)}, bf16[6,256,256]{2,1,0:T(8,128)(2,1)S(1)}, bf16[6,256,256]{2,1,0:T(8,128)(2,1)S(1)}) custom-call(bf16[512,2048]{1,0:T(8,128)(2,1)S(1)} %copy-done.16, f32[128,2048]{1,0:T(8,128)S(1)} %copy-done.11, f32[1,2048]{1,0:T(1,128)S(1)} %get-tuple-element.160.refs_2_, ...), custom_call_target="tpu_custom_call" | custom-call | bytes 104857600 | tf_op jit(solution)/shard_map/norm_back/pallas_call | solution.py:822
  233.3 1.0 copy-done.28
  234.3 0.9 copy-done.29
  235.2 0.9 copy-done.30
  236.1 1.3 copy-done.42
  237.4 22.4 %expert_grads.1.ups_ref = bf16[2,2,2,6,256,256]{5,4,3,2,1,0:T(8,128)(2,1)} custom-call(bf16[6,256,256]{2,1,0:T(8,128)(2,1)} %get-tuple-element.98.refs_4_.refs_0_, bf16[6,256,256]{2,1,0:T(8,128)(2,1)} %get-tuple-element.99.refs_5_.refs_1_, bf16[6,256,256]{2,1,0:T(8,128)(2,1)} %copy-done.29, bf16[6,256,256]{2,1,0:T(8,128)(2,1)} %copy-done.30, ...), custom_call_target="tpu_custom_call" | custom-call | bytes 1048576 | tf_op jit(solution)/shard_map/expert_grads/pallas_call | solution.py:1162
  259.8 2.9 convolution_convert_fusion.2.own_ref
  262.7 24.9 %rows_to_heads.1.grad_ref = bf16[1024,256]{1,0:T(8,128)(2,1)S(1)} custom-call(bf16[512,512]{1,0:T(8,128)(2,1)S(1)} %convolution_convert_fusion.2.own_ref), custom_call_target="tpu_custom_call" | custom-call | bytes 1048576 | tf_op jit(solution)/shard_map/rows_to_heads/pallas_call | solution.py:714
  287.6 0.8 copy-done.23
  288.5 0.9 copy-done.49
  289.4 2.5 slice_bitcast_fusion.1
  292.2 1.2 collective-permute-start.4
  293.4 2.6 convolution_convert_fusion.g_out_ref
  296.0 9.2 %down_grads.1.downs_ref = bf16[2,6,256,256]{3,2,1,0:T(8,128)(2,1)} custom-call(bf16[6,256,256]{2,1,0:T(8,128)(2,1)} %get-tuple-element.113.refs_0_, bf16[6,256,256]{2,1,0:T(8,128)(2,1)} %copy-done.49, bf16[6,256,256]{2,1,0:T(8,128)(2,1)} %collective-permute-done.1.refs_2_, bf16[6,256,256]{2,1,0:T(8,128)(2,1)} %collective-permute-done.2.refs_3_, ...), custom_call_target="tpu_custom_call" | custom-call | bytes 1048576 | tf_op jit(solution)/shard_map/down_grads/pallas_call | solution.py:1219
  305.2 16.9 %attend_back.1 = (f32[2,1024,256]{2,1,0:T(8,128)}, bf16[1024,256]{1,0:T(8,128)(2,1)}, f32[2,1,256]{2,1,0:T(1,128)}, f32[1024,2]{1,0:T(8,128)}) custom-call(bf16[1024,256]{1,0:T(8,128)(2,1)} %copy-done.23, bf16[1024,768]{1,0:T(8,128)(2,1)} %copy-done.25, f32[1024,256]{1,0:T(8,128)} %copy-done.26, f32[1024,256]{1,0:T(8,128)} %copy-done.27, ...), custom_call_target="tpu_custom_call" | custom-call | bytes 1048576 | tf_op jit(solution)/shard_map/attend_back/pallas_call | solution.py:1397
  322.1 5.4 %collective-permute-done.4.gate_own_ref = bf16[6,256,256]{2,1,0:T(8,128)(2,1)} collective-permute-done((bf16[6,256,256]{2,1,0:T(8,128)(2,1)S(1)}, bf16[6,256,256]{2,1,0:T(8,128)(2,1)}, u32[]{:S(2)}, u32[]{:S(2)}) %collective-permute-start.4) | collective-permute-done | bytes 786464 | tf_op jit(solution)/shard_map/ppermute | solution.py:734
  327.5 1.2 copy.45
  328.8 5.4 %ctx_sum.3 = f32[16,128]{1,0:T(8,128)S(1)} custom-call(f32[16,128]{1,0:T(8,128)S(1)} %reshape.212.own_ref), custom_call_target="tpu_custom_call" | custom-call | bytes 20971520 | tf_op jit(solution)/shard_map/ctx_sum/pallas_call | solution.py:538
  334.2 1.2 slice_bitcast_fusion
  336.0 1.0 copy.46
  337.0 15.1 %project_back.1 = (bf16[1024,2048]{1,0:T(8,128)(2,1)}, bf16[2048,768]{1,0:T(8,128)(2,1)}, f32[1,2048]{1,0:T(1,128)}) custom-call(f32[2,1024,256]{2,1,0:T(8,128)} %get-tuple-element.133.back_ref, f32[1024,768]{1,0:T(8,128)} %copy-done.1, f32[1024,2]{1,0:T(8,128)} %bitcast.44, f32[1024,2]{1,0:T(8,128)} %bitcast.51, ...), custom_call_target="tpu_custom_call" | custom-call | bytes 1048576 | tf_op jit(solution)/shard_map/project_back/pallas_call | solution.py:2124
  352.2 0.9 concatenate.23
  353.7 137.2 %finish_sums.1 = (f32[6,256,256]{2,1,0:T(8,128)}, f32[6,256,256]{2,1,0:T(8,128)}, f32[6,256,256]{2,1,0:T(8,128)}, f32[128,2048]{1,0:T(8,128)}, f32[512,256]{1,0:...) custom-call(bf16[2,6,256,256]{3,2,1,0:T(8,128)(2,1)} %down_grads.1.downs_ref, ...), custom_call_target="tpu_custom_call" | custom-call | bytes 734003200 | tf_op jit(solution)/shard_map/finish_sums/pallas_call | solution.py:1739
  490.9 1.5 slice_bitcast_fusion.3
  492.4 1.5 fusion.31
  493.8 1.9 copy.61
  495.7 2.3 copy.62
  498.0 1.1 copy.63
  499.4 0.8 copy.64
  500.2 1.1 copy.65
  501.3 1.1 copy.66
  502.5 0.8 copy-done.45
  503.3 1.1 copy.67
  (132 shorter events, 7.9 us)
Async XLA Ops:
  7.2 117.3 %copy-start = (bf16[512,2048]{1,0:T(8,128)(2,1)S(1)}, bf16[512,2048]{1,0:T(8,128)(2,1)}, u32[]{:S(2)}) copy-start(bf16[512,2048]{1,0:T(8,128)(2,1)} %param.23) | copy-start | bytes 6291460
  7.2 230.2 %all-gather.4.cloned.1.call-start = ((), (), s32[]{:S(2)}) async-start(), calls=%async_computation.1 | async-start | bytes 1310720 | tf_op jit(solution)/shard_map/all_gather | solution.py:2250
  7.4 93.3 %copy-start.21 = (s32[1024,1]{1,0:T(8,128)}, s32[1024,1]{1,0:T(8,128)S(1)}, u32[]{:S(2)}) copy-start(s32[1024,1]{1,0:T(8,128)S(1)} %fusion.9.last_ref) | copy-start | bytes 12292
  7.4 93.2 %copy-start.34 = (s32[1,1024]{1,0:T(1,128)}, s32[1,1024]{1,0:T(1,128)S(1)}, u32[]{:S(2)}) copy-start(s32[1,1024]{1,0:T(1,128)S(1)} %compare_select_fusion.places_ref) | copy-start | bytes 12292
  9.9 2.8 copy-start.3
  12.7 1.0 copy-start.5
  13.8 1.0 copy-start.17
  69.5 2.0 copy-start.7
  71.5 1.7 copy-start.12
  73.2 0.6 copy-start.35
  73.8 0.6 copy-start.36
  74.4 0.6 copy-start.37
  75.0 0.6 copy-start.38
  75.6 0.6 copy-start.39
  76.2 1.3 copy-start.41
  77.5 0.6 copy-start.44
  78.1 9.4 %copy-start.33 = (f32[1,2048]{1,0:T(1,128)}, f32[1,2048]{1,0:T(1,128)S(1)}, u32[]{:S(2)}) copy-start(f32[1,2048]{1,0:T(1,128)S(1)} %get-tuple-element.163.gain_ref) | copy-start | bytes 24580
  78.2 2.2 copy-start.8
  80.4 1.9 copy-start.13
  82.3 14.8 %copy-start.53 = (s32[1,16]{1,0:T(1,128)S(1)}, s32[1,16]{1,0:T(1,128)}, u32[]{:S(2)}) copy-start(s32[1,16]{1,0:T(1,128)} %param.16) | copy-start | bytes 196
  87.6 1.6 copy-start.1
  89.2 2.0 copy-start.9
  97.1 3.6 copy-start.4
  98.3 2.3 copy-start.40
  98.3 2.3 copy-start.2
  98.4 2.3 copy-start.22
  100.6 8.3 %copy-start.19 = (f32[1024,128]{1,0:T(8,128)}, f32[1024,128]{1,0:T(8,128)S(1)}, u32[]{:S(2)}) copy-start(f32[1024,128]{1,0:T(8,128)S(1)} %get-tuple-element.169.cos_ref) | copy-start | bytes 1572868
  100.6 8.3 %copy-start.20 = (f32[1024,128]{1,0:T(8,128)}, f32[1024,128]{1,0:T(8,128)S(1)}, u32[]{:S(2)}) copy-start(f32[1024,128]{1,0:T(8,128)S(1)} %get-tuple-element.170.sin_ref) | copy-start | bytes 1572868
  108.9 16.9 %copy-start.25 = (bf16[1024,768]{1,0:T(8,128)(2,1)}, bf16[1024,768]{1,0:T(8,128)(2,1)S(1)}, u32[]{:S(2)}) copy-start(bf16[1024,768]{1,0:T(8,128)(2,1)S(1)} %get-tuple-element.124.low_ref) | copy-start | bytes 4718596
  108.9 16.9 %copy-start.26 = (f32[1024,256]{1,0:T(8,128)}, f32[1024,256]{1,0:T(8,128)S(1)}, u32[]{:S(2)}) copy-start(f32[1024,256]{1,0:T(8,128)S(1)} %get-tuple-element.125.attended_ref) | copy-start | bytes 3145732
  108.9 16.9 %copy-start.27 = (f32[1024,256]{1,0:T(8,128)}, f32[1024,256]{1,0:T(8,128)S(1)}, u32[]{:S(2)}) copy-start(f32[1024,256]{1,0:T(8,128)S(1)} %get-tuple-element.126.top_ref) | copy-start | bytes 3145732
  124.5 1.3 copy-start.31
  124.5 1.3 copy-start.6
  155.0 1.0 copy-start.10
  156.0 1.4 copy-start.24
  157.4 138.5 %all-gather.6.cloned.1.call-start = ((), (), s32[]{:S(2)}) async-start(), calls=%async_computation.3 | async-start | bytes 2621440 | tf_op jit(solution)/shard_map/all_gather | solution.py:2193
  158.2 195.5 %reduce-scatter.2.cloned.1.call-start = ((), (), s32[]{:S(2)}) async-start(), calls=%async_computation.2 | async-start | bytes 2621440 | tf_op jit(solution)/shard_map/reduce_scatter | solution.py:2260
  162.5 30.8 %copy-start.11 = (f32[128,2048]{1,0:T(8,128)S(1)}, f32[128,2048]{1,0:T(8,128)}, u32[]{:S(2)}) copy-start(f32[128,2048]{1,0:T(8,128)} %copy-done.10) | copy-start | bytes 3145732
  162.5 30.8 %copy-start.18 = (bf16[1,128,2048]{2,1,0:T(8,128)(2,1)S(1)}, bf16[1,128,2048]{2,1,0:T(8,128)(2,1)}, u32[]{:S(2)}) copy-start(bf16[1,128,2048]{2,1,0:T(8,128)(2,1)} %param.29) | copy-start | bytes 1572868
  187.8 100.6 %collective-permute-start = (bf16[6,256,256]{2,1,0:T(8,128)(2,1)}, bf16[6,256,256]{2,1,0:T(8,128)(2,1)S(1)}, u32[]{:S(2)}, u32[]{:S(2)}) collective-permute-start(bf16[6,256,256]{2,1,0:T(8,128)(2,1)} %get-tuple-element.113.refs_0_), channel_id=1, source_target_pairs={{0,8},{4,12},{8,0},{12,4},{16,24},{20,28},{24,16},{28,20},{1,9},{5... | collective-permute-start | bytes 2359304 | tf_op jit(solution)/shard_map/ppermute | solution.py:734
  188.7 99.7 %collective-permute-start.1 = (bf16[6,256,256]{2,1,0:T(8,128)(2,1)}, bf16[6,256,256]{2,1,0:T(8,128)(2,1)}, u32[]{:S(2)}, u32[]{:S(2)}) collective-permute-start(bf16[6,256,256]{2,1,0:T(8,128)(2,1)} %get-tuple-element.113.refs_0_), channel_id=1, source_target_pairs={{0,16},{4,20},{8,24},{12,28},{16,0},{20,4},{24,8},{28,12},{1,17},{... | collective-permute-start | bytes 2359304 | tf_op jit(solution)/shard_map/ppermute | solution.py:734
  193.3 95.1 %collective-permute-start.2 = (bf16[6,256,256]{2,1,0:T(8,128)(2,1)}, bf16[6,256,256]{2,1,0:T(8,128)(2,1)}, u32[]{:S(2)}, u32[]{:S(2)}) collective-permute-start(bf16[6,256,256]{2,1,0:T(8,128)(2,1)} %get-tuple-element.113.refs_0_), channel_id=1, source_target_pairs={{0,24},{4,28},{8,16},{12,20},{16,8},{20,12},{24,0},{28,4},{1,25},{... | collective-permute-start | bytes 2359304 | tf_op jit(solution)/shard_map/ppermute | solution.py:734
  193.3 1.1 copy-start.14
  194.5 1.1 copy-start.15
  195.6 1.6 copy-start.16
  233.3 1.0 copy-start.28
  234.3 0.9 copy-start.29
  235.2 0.9 copy-start.30
  236.1 1.3 copy-start.42
  287.6 0.8 copy-start.23
  288.4 0.9 copy-start.49
  289.4 4.0 copy-start.32
  289.4 4.0 copy-start.43
  291.9 30.2 %collective-permute-start.3 = (bf16[6,256,256]{2,1,0:T(8,128)(2,1)}, bf16[6,256,256]{2,1,0:T(8,128)(2,1)}, u32[]{:S(2)}, u32[]{:S(2)}) collective-permute-start(bf16[6,256,256]{2,1,0:T(8,128)(2,1)} %get-tuple-element.155), channel_id=1, source_target_pairs={{0,8},{4,12},{8,0},{12,4},{16,24},{20,28},{24,16},{28,20},{1,9},{5... | collective-permute-start | bytes 2359304 | tf_op jit(solution)/shard_map/ppermute | solution.py:734
  292.2 35.3 %collective-permute-start.4 = (bf16[6,256,256]{2,1,0:T(8,128)(2,1)S(1)}, bf16[6,256,256]{2,1,0:T(8,128)(2,1)}, u32[]{:S(2)}, u32[]{:S(2)}) collective-permute-start(bf16[6,256,256]{2,1,0:T(8,128)(2,1)S(1)} %get-tuple-element.154), channel_id=1, source_target_pairs={{0,8},{4,12},{8,0},{12,4},{16,24},{20,28},{24,16},{28,20},{1,9},{5... | collective-permute-start | bytes 2359304 | tf_op jit(solution)/shard_map/ppermute | solution.py:734
  322.1 13.9 %copy-start.51 = (f32[16,2048]{1,0:T(8,128)S(1)}, f32[16,2048]{1,0:T(8,128)}, u32[]{:S(2)}) copy-start(f32[16,2048]{1,0:T(8,128)} %get-tuple-element.143) | copy-start | bytes 393220
  335.4 18.3 %collective-permute-start.5 = (bf16[6,256,256]{2,1,0:T(8,128)(2,1)S(1)}, bf16[6,256,256]{2,1,0:T(8,128)(2,1)}, u32[]{:S(2)}, u32[]{:S(2)}) collective-permute-start(bf16[6,256,256]{2,1,0:T(8,128)(2,1)S(1)} %slice_bitcast_fusion), channel_id=1, source_target_pairs={{0,8},{4,12},{8,0},{12,4},{16,24},{20,28},{24,16},{28,20},{1,9},{5... | collective-permute-start | bytes 2359304 | tf_op jit(solution)/shard_map/ppermute | solution.py:734
  337.0 15.1 %copy-start.52 = (f32[2,1,256]{2,1,0:T(1,128)S(1)}, f32[2,1,256]{2,1,0:T(1,128)}, u32[]{:S(2)}) copy-start(f32[2,1,256]{2,1,0:T(1,128)} %get-tuple-element.141) | copy-start | bytes 6148
  490.9 7.1 %copy-start.48 = (f32[512,768]{1,0:T(8,128)S(1)}, f32[512,768]{1,0:T(8,128)}, u32[]{:S(2)}) copy-start(f32[512,768]{1,0:T(8,128)} %get-tuple-element.186) | copy-start | bytes 4718596
  498.0 1.4 copy-start.50
  498.0 2.2 copy-start.47
  499.4 1.9 copy-start.46
  501.3 2.0 copy-start.45
Sparse Core Ops, SparseCore 0:
  157.5 18.1 all-gather.3
  177.3 22.5 all-gather.5
  289.5 29.4 reduce-scatter.1
where the time goes:
time: 515 us; the launch traced here: 511 us
  Pallas kernels  415 us (81%)
  local copies, waits for them, and re-layouts  57.2 us (11%)
  between operations  14.6 us (3%)
  starting transfers between devices  7.86 us (2%)
  matrix products  6.7 us (1%)
  waiting for transfers between devices  6.19 us (1%)
    pallas_call x1, Pallas kernels, finish_sums(): comm_call(kernel, 'finish_sums', collective_id, [jax.ShapeDtypeStruct(gra...  137 us
    pallas_call x2, Pallas kernels, reduce_then_gather(): comm_call(kernel, name, collective_id, [jax.ShapeDtypeStruct(partial.shap...  65.3 us
    pallas_call x1, Pallas kernels, gather_inputs(): comm_call(kernel, 'gather_inputs', collective_id, [jax.ShapeDtypeStruct((...  54.7 us
    unnamed x115, local copies, waits for them, and re-layouts  43.8 us
    pallas_call x1, Pallas kernels, run_experts(): pl.pallas_call(kernel, grid=(experts,), out_shape=[jax.ShapeDtypeStruct((...  25.3 us
    pallas_call x1, Pallas kernels, rows_to_heads(): comm_call(kernel, 'rows_to_heads', collective_id, jax.ShapeDtypeStruct((c...  24.9 us
    pallas_call x1, Pallas kernels, expert_grads(): pl.pallas_call(kernel, grid=(experts,), out_shape=jax.ShapeDtypeStruct((k...  22.4 us
    pallas_call x1, Pallas kernels, attend_back(): pl.pallas_call(kernel, out_shape=[jax.ShapeDtypeStruct((2, total, cols),...  16.9 us
  transfers between devices with their start and end apart: 9, of which 1 were waited for; matrix products, arithmetic and copies ran while one was open for 3% of the time, Pallas kernels for 31%

commit v1 on v0

--- a/solution.py
+++ b/solution.py
@@ -10,7 +10,6 @@
 HEADS = 16
 MESH = pl.DeviceIdType.MESH
 ANY = pl.BlockSpec(memory_space=pl.ANY)
-HBM = pl.BlockSpec(memory_space=pltpu.HBM)
 VMEM = pl.BlockSpec(memory_space=pltpu.VMEM)
 DMA = pltpu.SemaphoreType.DMA
 
@@ -1085,7 +1084,7 @@
             pltpu.VMEM((ROUTER_ROWS, total), f32),
             pltpu.VMEM((ROUTER_ROWS, 1, total), f32),
         ],
-        compiler_params=pltpu.CompilerParams(vmem_limit_bytes=56 * 2**20),
+        compiler_params=pltpu.CompilerParams(vmem_limit_bytes=60 * 2**20),
         cost_estimate=pl.CostEstimate(
             flops=30 * 10**9, bytes_accessed=30 * 2**20, transcendentals=10**6
         ),
@@ -1106,7 +1105,7 @@
     def kernel(*refs):
         own_refs, other_refs = refs[:kinds], refs[kinds : 2 * kinds]
         rows_own_ref, rows_other_ref, slots_own_ref, slots_other_ref = refs[2 * kinds : 2 * kinds + 4]
-        out_ref, held_rows = refs[2 * kinds + 4 :]
+        out_refs, held_rows = refs[2 * kinds + 4 : -1], refs[-1]
         expert = pl.program_id(0)
         me = lax.axis_index("ctx")
 
@@ -1147,13 +1146,18 @@
         ]
         contract = (((0,), (0,)), ((), ()))
         for run in range(ctx // 2):
-            kept = jnp.where(low == run % 2, 1, 0)
-            far = jnp.where(high == run // 2, 0, 1)
+            given = jnp.where(low == run % 2, 0, 2)
+            place = given + jnp.where(high == run // 2, 0, 1)
             features = held_rows[expert, :, pl.ds(run * cols, cols)]
             for kind in range(kinds):
-                out_ref[kind, pl.ds(kept, 1), pl.ds(far, 1), 0] = lax.dot_general(
+                total = lax.dot_general(
                     features, stacked[kind], contract, preferred_element_type=f32
-                ).astype(bf16)[None, None]
+                ).astype(bf16)
+                for i in range(4):
+
+                    @pl.when(place == i)
+                    def _():
+                        out_refs[4 * kind + i][0] = total
 
     def whole(shape):
         return pl.BlockSpec(shape, lambda e: (0,) * len(shape))
@@ -1162,11 +1166,11 @@
     return pl.pallas_call(
         kernel,
         grid=(experts,),
-        out_shape=jax.ShapeDtypeStruct((kinds, 2, 2, experts, units, cols), bf16),
+        out_shape=[jax.ShapeDtypeStruct((experts, units, cols), bf16)] * (4 * kinds),
         in_specs=[slot_spec] * (2 * kinds)
         + [whole((total, 2 * half)), whole((total, half))]
         + [whole((ROUTER_ROWS, total))] * 2,
-        out_specs=pl.BlockSpec((kinds, 2, 2, 1, units, cols), lambda e: (0, 0, 0, e, 0, 0)),
+        out_specs=[pl.BlockSpec((1, units, cols), lambda e: (e, 0, 0))] * (4 * kinds),
         scratch_shapes=[pltpu.VMEM((experts, 2 * held, half), bf16)],
         compiler_params=pltpu.CompilerParams(vmem_limit_bytes=60 * 2**20),
         cost_estimate=pl.CostEstimate(flops=0, bytes_accessed=2**20, transcendentals=0),
@@ -1460,7 +1464,11 @@
 
     def kernel(
         downs_ref,
-        ups_ref,
+        gate_near_ref,
+        gate_high_ref,
+        up_near_ref,
+        up_high_ref,
+        up_low_ref,
         gate_far_ref,
         gate_own_ref,
         up_far_ref,
@@ -1554,11 +1562,8 @@
             ab: push(normed_block(*ab, True), normed_x.at[ab[0], ab[1]], to_x) for ab in order
         }
 
-        def push_low(kind, a):
-            return push(ups_ref.at[kind - 1, 0, a], kept_low.at[kind, a], to_low)
-
         low_copies = {
-            (2, 0): push_low(2, 0),
+            (2, 0): push(up_low_ref, kept_low.at[2, 0], to_low),
             (0, 0): push(downs_ref.at[0], kept_low.at[0, 0], to_x),
         }
         early = {
@@ -1567,10 +1572,14 @@
             (1, 0): load(gate_own_ref, kept_low.at[1, 0]),
         }
         kept_loads = {
-            (kind, a): load(
-                downs_ref.at[1] if kind == 0 else ups_ref.at[kind - 1, 1, a], kept.at[kind, a]
+            place: load(source, kept.at[place])
+            for place, source in (
+                ((1, 1), gate_high_ref),
+                ((2, 1), up_high_ref),
+                ((0, 0), downs_ref.at[1]),
+                ((1, 0), gate_near_ref),
+                ((2, 0), up_near_ref),
             )
-            for kind, a in ((1, 1), (2, 1), (0, 0), (1, 0), (2, 0))
         }
         qkv_copies = [
             push(qkv_block(diagonal), qkv_core.at[1], (me, core)),
@@ -1750,7 +1759,7 @@
             jax.ShapeDtypeStruct((small_rows, small_cols), f32),
             jax.ShapeDtypeStruct((rows, width), bf16),
         ],
-        [ANY] * 8 + [VMEM] * 6,
+        [ANY] * 12 + [VMEM] * 6,
         [VMEM] * 8,
         [
             block(kinds, 2, *gradient),
@@ -1781,7 +1790,7 @@
         56,
     )(
         downs,
-        ups,
+        *ups,
         gate_far,
         gate_own,
         up_far,
@@ -1839,7 +1848,8 @@
         *refs,
     ):
         flip_refs, dy_line_ref, refs = refs[:flip_count], refs[flip_count], refs[flip_count + 1 :]
-        sends, recvs, line_send, line_recv, cross_send, cross_recv, local_sems = refs
+        stage, weight_stage, dy_stage, sends, recvs, line_send, line_recv, cross_send, cross_recv, *refs = refs
+        local_sems, line_out, cross_out = refs
         me, mine = lax.axis_index("ctx"), lax.axis_index("fsdp")
         z, x = me // 2, lax.rem(me, 2)
         to_x = (flipped(me, 1), mine)
@@ -1871,7 +1881,16 @@
 
         def token_chunk(index, chunk):
             start = pl.multiple_of(index * rows + chunk * size, size)
-            return all_ref.at[pl.ds(start, size), :]
+            return stage.at[pl.ds(start, size), :]
+
+        def put(away, side, chunk, crossed):
+            index = 2 * (z - away if side == 0 else z + away) + (1 - x if crossed else x)
+            start = pl.multiple_of(index * rows + chunk * size, size)
+            return pltpu.make_async_copy(
+                stage.at[pl.ds(start, size), :],
+                all_ref.at[pl.ds(start, size), :],
+                (cross_out if crossed else line_out).at[side * line + away, chunk],
+            )
 
         def taken(own, index, chunk):
             return tokens_ref.at[pl.ds(chunk * size, size), :] if own else token_chunk(index, chunk)
@@ -1915,14 +1934,22 @@
             cross(0, 0, chunk).start()
         load(tokens_ref, token_block(me))
 
-        weight_chip = []
+        own_weight = by_part(weight_stage, mine, part)
+        pieces = []
         for kind in range(kinds):
             column = pl.ds(pl.multiple_of(kind * width + me * cols, cols), cols)
-            target = by_part(weight_ref, mine, part).at[:, pl.ds(kind * cols, cols)]
-            source = w_qkv_ref.at[:, column]
-            weight_chip.append(push(source, target, chip))
-            push(source, target, core)
-            load(source, target)
+            target = own_weight.at[:, pl.ds(kind * cols, cols)]
+            pieces.append(
+                pltpu.make_async_copy(w_qkv_ref.at[:, column], target, local_sems.at[23 - kind])
+            )
+            pieces[-1].start()
+        load(dy_ref, dy_stage)
+        dy_loaded = kept.pop()
+        for piece in pieces:
+            piece.wait()
+        weight_chip = [push(own_weight, own_weight, chip)]
+        weight_core = [push(own_weight, own_weight, core)]
+        load(own_weight, by_part(weight_ref, mine, part))
         columns = pl.ds(pl.multiple_of(mine * part, part), part)
         for i, (source, target) in enumerate(zip(small_refs, small_all_refs)):
             if i < row_count:
@@ -1949,38 +1976,52 @@
                             line_recv.at[side * line + away - 1, chunk],
                         ).wait()
                         cross(away, side, chunk).start()
+                        put(away, side, chunk, False).start()
 
                     if away < line - 1:
                         pl.when(goes_on(away, side))(along(away, side, chunk).start)
-            if away == 1:
-                for copy in weight_chip:
-                    copy.wait_recv()
-                far = by_part(weight_ref, flipped(mine, 2), part)
-                push(far, far, core)
-            if away == 2:
-                dy_chip.wait_recv()
-                far = by_part(dy_all_ref, flipped(mine, 2), rows)
-                push(far, far, core)
         for other, target in zip(others, flip_refs):
             for step in range(fsdp):
                 push(small_refs[-1], target.at[mine], (other, lax.rem(mine + step, fsdp)))
+        dy_loaded.wait()
         for i in range(line):
             wide = 2 * cols
             to = flipped_by(me, 2 * i)
-            source = dy_ref.at[:, pl.ds(pl.multiple_of(to // 2 * wide, wide), wide)]
+            source = dy_stage.at[:, pl.ds(pl.multiple_of(to // 2 * wide, wide), wide)]
             if i == 0:
                 load(source, dy_line_ref.at[0])
             else:
                 push(source, dy_line_ref.at[i], (to, mine))
 
+        for copy in weight_chip:
+            copy.wait_recv()
+        far = by_part(weight_stage, flipped(mine, 2), part)
+        weight_far = push(far, far, core)
+        load(far, by_part(weight_ref, flipped(mine, 2), part))
+        for copy in weight_core:
+            copy.wait_recv()
+        near = flipped(mine, 1)
+        load(by_part(weight_stage, near, part), by_part(weight_ref, near, part))
+        dy_chip.wait_recv()
+        far = by_part(dy_all_ref, flipped(mine, 2), rows)
+        push(far, far, core)
         every = [(side, chunk) for side in range(2) for chunk in range(chunks)]
+        weight_far.wait_recv()
+        far = flipped_by(mine, 3)
+        load(by_part(weight_stage, far, part), by_part(weight_ref, far, part))
         for chunk in range(chunks):
             cross(0, 0, chunk).wait_recv()
+            put(0, 0, chunk, True).start()
         for away in range(1, line):
             for side, chunk in every:
-                pl.when(has(away, side))(cross(away, side, chunk).wait_recv)
+
+                @pl.when(has(away, side))
+                def _():
+                    cross(away, side, chunk).wait_recv()
+                    put(away, side, chunk, True).start()
+
         for copy in started:
-            if copy is not dy_chip and not any(copy is other for other in weight_chip):
+            if not any(copy is other for other in [dy_chip, weight_far] + weight_chip + weight_core):
                 copy.wait_recv()
         for copy in kept:
             copy.wait()
@@ -1988,6 +2029,16 @@
             copy.wait_send()
         for chunk in range(chunks):
             cross(0, 0, chunk).wait_send()
+        for chunk in range(chunks):
+            put(0, 0, chunk, True).wait()
+        for away in range(1, line):
+            for side, chunk in every:
+
+                @pl.when(has(away, side))
+                def _():
+                    put(away, side, chunk, False).wait()
+                    put(away, side, chunk, True).wait()
+
         for away in range(line - 1):
             for side, chunk in every:
                 pl.when(goes_on(away, side))(along(away, side, chunk).wait_send)
@@ -2007,18 +2058,24 @@
         + [jax.ShapeDtypeStruct((row.shape[0], fsdp * part), row.dtype) for row in row_arrays]
         + [jax.ShapeDtypeStruct((fsdp,) + block.shape, block.dtype)] * (1 + flip_count)
         + [jax.ShapeDtypeStruct((line, rows, 2 * cols), dy.dtype)],
-        [HBM] * (3 + small_count),
-        [HBM] * (4 + small_count + flip_count),
+        [ANY] * (3 + small_count),
+        [ANY] * (4 + small_count + flip_count),
         [
+            pltpu.VMEM((ctx * rows, width), tokens.dtype),
+            pltpu.VMEM((fsdp * part, kinds * cols), w_qkv.dtype),
+            pltpu.VMEM((rows, width), dy.dtype),
             DMA((64,)),
             DMA((64,)),
             DMA((2 * line, chunks)),
             DMA((2 * line, chunks)),
             DMA((2 * line, chunks)),
             DMA((2 * line, chunks)),
-            DMA((16,)),
+            DMA((24,)),
+            DMA((2 * line, chunks)),
+            DMA((2 * line, chunks)),
         ],
         150 * 2**20,
+        60,
     )(tokens, w_qkv, dy, *row_arrays, block)
 
 
@@ -2056,7 +2113,7 @@
             pl.BlockSpec((width, wide), lambda i: (0, 0)),
         ],
         out_specs=[by_rows(width), by_rows(wide), by_rows(2)],
-        compiler_params=pltpu.CompilerParams(vmem_limit_bytes=24 * 2**20),
+        compiler_params=pltpu.CompilerParams(vmem_limit_bytes=60 * 2**20),
         cost_estimate=pl.CostEstimate(
             flops=3 * 10**9, bytes_accessed=15 * 2**20, transcendentals=0
         ),
@@ -2254,11 +2311,11 @@
     ups, mixed_all = lax.optimization_barrier((ups, mixed_all))
     output_part = dot32("te,de->td", mixed_all, w_out).astype(bf16)
     output_grad = rows_to_heads(output_part, 3)
-    output_grad, moved_part, ups, mixed_all, *scaled_line = lax.optimization_barrier(
-        (output_grad, moved_part, ups, mixed_all, *scaled_line)
+    output_grad, moved_part, ups, mixed_all, scaled_line = lax.optimization_barrier(
+        (output_grad, moved_part, ups, mixed_all, scaled_line)
     )
     moved = lax.psum_scatter(moved_part, "fsdp", scatter_dimension=0, tiled=True)
-    gate_far, gate_own = swap(ups[0, 0, 1], 2), swap(ups[0, 0, 0], 2)
+    gate_far, gate_own = swap(ups[3], 2), swap(ups[2], 2)
     downs = down_grads(scaled_line, dy_parts, [slot_by_expert] + slots_line, capacity)
     g_out = dot32("td,te->de", attended_part, mixed_all).astype(bf16)
     output_grad, ups, downs, g_out = lax.optimization_barrier((output_grad, ups, downs, g_out))
@@ -2269,7 +2326,7 @@
     inner_sums, gate_far, gate_own = lax.optimization_barrier((inner_sums, gate_far, gate_own))
     inner_sums = ctx_sum(inner_sums.T.reshape(-1, 128), 1)
     inner_sums, ups = lax.optimization_barrier((inner_sums, ups))
-    up_far = swap(ups[1, 0, 1], 2)
+    up_far = swap(ups[7], 2)
     inner_sums = inner_sums.reshape(2, total).T / width
 
     normed_grad_part, g_qkv, g_attn_gain = project_back(
@@ -2289,7 +2346,7 @@
     )
     down_parts, gate_parts, up_parts, input_grad, out_part, qkv_part, sums, activations = finish_sums(
         downs,
-        ups,
+        ups[0:2] + ups[4:7],
         gate_far,
         gate_own,
         up_far,

time: 515 us -> 503 us (0.977); the launches traced: 511 us -> 493 us
  local copies, waits for them, and re-layouts: 57.2 us -> 34.3 us
    unnamed x115 -> x79, local copies, waits for them, and re-layouts: 43.8 us -> 21.8 us
  transfers between devices with their start and end apart: 9 -> 9, of which waited for: 1 -> 1; matrix products, arithmetic and copies ran while one was open for 3% -> 2% of each run, Pallas kernels for 31% -> 32%
where the time goes in v1:
time: 503 us; the launch traced here: 493 us
  Pallas kernels  418 us (83%)
  local copies, waits for them, and re-layouts  34.3 us (7%)
  between operations  14.7 us (3%)
  matrix products  8.31 us (2%)
  starting transfers between devices  7.9 us (2%)
  other arithmetic  5.65 us (1%)
    pallas_call x1, Pallas kernels, finish_sums(): comm_call(kernel, 'finish_sums', collective_id, [jax.ShapeDtypeStruct(gra...  137 us
    pallas_call x2, Pallas kernels, reduce_then_gather(): comm_call(kernel, name, collective_id, [jax.ShapeDtypeStruct(partial.shap...  65.2 us
    pallas_call x1, Pallas kernels, gather_inputs(): comm_call(kernel, 'gather_inputs', collective_id, [jax.ShapeDtypeStruct((...  55.3 us
    pallas_call x1, Pallas kernels, run_experts(): pl.pallas_call(kernel, grid=(experts,), out_shape=[jax.ShapeDtypeStruct((...  25.3 us
    pallas_call x1, Pallas kernels, rows_to_heads(): comm_call(kernel, 'rows_to_heads', collective_id, jax.ShapeDtypeStruct((c...  24.8 us
    unnamed x79, local copies, waits for them, and re-layouts  21.8 us
    pallas_call x1, Pallas kernels, expert_grads(): pl.pallas_call(kernel, grid=(experts,), out_shape=[jax.ShapeDtypeStruct((...  20.4 us
    pallas_call x1, Pallas kernels, attend_back(): pl.pallas_call(kernel, out_shape=[jax.ShapeDtypeStruct((2, total, cols),...  16.9 us
  transfers between devices with their start and end apart: 9, of which 1 were waited for; matrix products, arithmetic and copies ran while one was open for 2% of the time, Pallas kernels for 32%

profile of v1, /device:TPU:5, one launch (start us, length us, event | category | flops | bytes accessed | tf_op | source)
XLA Modules:
  0.0 493.1 jit_solution(977095131034558096)
XLA Ops:
  7.3 0.9 fusion.9.last_ref
  8.2 0.7 pad_maximum_fusion.2
  8.9 0.6 reshape.210.refs_3_
  9.5 0.7 copy_bitcast_fusion
  10.3 0.6 pad.13.refs_5_
  10.9 1.3 pad.12.refs_4_
  12.2 55.3 %gather_inputs.1 = (bf16[1024,2048]{1,0:T(8,128)(2,1)}, bf16[2048,768]{1,0:T(8,128)(2,1)}, bf16[512,2048]{1,0:T(8,128)(2,1)}, bf16[4,2048]{1,0:T(4,128)(2,1)}, b...) custom-call(bf16[128,2048]{1,0:T(8,128)(2,1)} %bitcast.36, ...), custom_call_target="tpu_custom_call" | custom-call | bytes 157286400 | tf_op jit(solution)/shard_map/gather_inputs/pallas_call | solution.py:2049
  67.5 1.5 slice_convert_fusion
  69.0 9.3 %project.1 = (bf16[1024,2048]{1,0:T(8,128)(2,1)}, f32[1024,768]{1,0:T(8,128)}, f32[1024,2]{1,0:T(8,128)}) custom-call(bf16[1024,2048]{1,0:T(8,128)(2,1)} %get-tuple-element.115.tokens_ref, f32[1,2048]{1,0:T(1,128)} %get-tuple-element.225.gain_ref, bf16[2048,768]{1,0:T(8,128)(2,1)} %get-tuple-element.117.weight_ref), custom_call_target="tpu_custom_call" | custom-call | flops 3000000000 | bytes 15728640 | tf_op jit(solution)/shard_map/project/pallas_call | solution.py:2102
  78.4 1.2 copy.41
  79.6 5.4 %ctx_sum.2 = f32[16,128]{1,0:T(8,128)S(1)} custom-call(f32[16,128]{1,0:T(8,128)S(1)} %reshape.211.own_ref), custom_call_target="tpu_custom_call" | custom-call | bytes 20971520 | tf_op jit(solution)/shard_map/ctx_sum/pallas_call | solution.py:537
  85.1 0.2 copy.42
  85.6 1.0 copy.43.first_ref
  86.6 1.9 fusion.15
  88.5 0.3 pad_maximum_fusion
  88.9 8.1 %attend.1 = (bf16[1024,768]{1,0:T(8,128)(2,1)S(1)}, f32[1024,256]{1,0:T(8,128)S(1)}, bf16[1024,256]{1,0:T(8,128)(2,1)S(1)}, f32[1024,256]{1,0:T(8,128)S(1)}) custom-call(f32[1024,768]{1,0:T(8,128)S(1)} %copy-done.1, f32[1024,2]{1,0:T(8,128)S(1)} %bitcast.39, f32[1,512]{1,0:T(1,128)S(1)} %pad_maximum_fusion.3.gains_ref, ...), custom_call_target="tpu_custom_call" | custom-call | flops 2000000000 | bytes 20971520 | tf_op jit(solution)/shard_map/attend/pallas_call | solution.py:1303
  97.1 16.0 %heads_to_rows.1 = bf16[512,512]{1,0:T(8,128)(2,1)S(1)} custom-call(bf16[1024,256]{1,0:T(8,128)(2,1)S(1)} %get-tuple-element.120.own_ref), custom_call_target="tpu_custom_call" | custom-call | bytes 41943040 | tf_op jit(solution)/shard_map/heads_to_rows/pallas_call | solution.py:626
  113.1 1.3 convolution_convert_fusion.1.refs_0_
  114.5 29.1 %mix_and_norm.1 = (bf16[512,2048]{1,0:T(8,128)(2,1)S(1)}, f32[128,2048]{1,0:T(8,128)S(1)}, bf16[128,1024]{1,0:T(8,128)(2,1)}) custom-call(bf16[512,2048]{1,0:T(8,128)(2,1)S(1)} %convolution_convert_fusion.1.refs_0_, bf16[128,2048]{1,0:T(8,128)(2,1)S(1)} %bitcast.38, f32[1,2048]{1,0:T(1,128)S(1)} %get-tuple-element.222.refs_2_), custom_call_target="tpu_custom_call" | custom-call | bytes 104857600 | tf_op jit(solution)/shard_map/mix_and_norm/pallas_call | solution.py:821
  143.6 1.0 copy-done.4
  144.6 1.3 copy-done.8
  146.0 0.7 all-gather.6.cloned.1.call-update
  146.7 0.2 reduce-scatter.2.cloned.1.call-start
  146.9 4.0 slots_of.1
  150.9 25.3 %run_experts.1 = (bf16[512,2048]{1,0:T(8,128)(2,1)}, bf16[512,2048]{1,0:T(8,128)(2,1)}, f32[16,2048]{1,0:T(8,128)}, bf16[6,256,256]{2,1,0:T(8,128)(2,1)}, bf16[6...) custom-call(bf16[512,2048]{1,0:T(8,128)(2,1)} %copy-done.8, bf16[512,2048]{1,0:T(8,128)(2,1)} %get-tuple-element.122.dy_ref, ...), custom_call_target="tpu_custom_call" | custom-call | flops 30000001024 | bytes 31457280 | tf_op jit(solution)/shard_map/run_experts/pallas_call | solution.py:1056
  176.2 0.9 collective-permute-start
  177.1 4.7 collective-permute-start.1
  181.8 1.1 copy-done.6
  182.9 1.1 copy-done.7
  184.1 1.6 copy-done.9
  185.7 36.1 %norm_back.1 = (bf16[512,2048]{1,0:T(8,128)(2,1)S(1)}, f32[128,2048]{1,0:T(8,128)S(1)}, f32[1,2048]{1,0:T(1,128)S(1)}, bf16[6,256,256]{2,1,0:T(8,128)(2,1)S(1)}, bf16[6,256,256]{2,1,0:T(8,128)(2,1)S(1)}) custom-call(bf16[512,2048]{1,0:T(8,128)(2,1)S(1)} %copy-done.9, f32[128,2048]{1,0:T(8,128)S(1)} %copy-done.5, f32[1,2048]{1,0:T(1,128)S(1)} %get-tuple-element.222.refs_2_, ...), custom_call_target="tpu_custom_call" | custom-call | bytes 104857600 | tf_op jit(solution)/shard_map/norm_back/pallas_call | solution.py:821
  221.8 1.0 copy-done.17
  222.8 0.9 copy-done.20
  223.7 0.9 copy-done.21
  224.6 1.3 copy-done.26
  225.9 20.4 %expert_grads.1 = (bf16[6,256,256]{2,1,0:T(8,128)(2,1)}, bf16[6,256,256]{2,1,0:T(8,128)(2,1)}, bf16[6,256,256]{2,1,0:T(8,128)(2,1)}, bf16[6,256,256]{2,1,0:T(8,1...) custom-call(bf16[6,256,256]{2,1,0:T(8,128)(2,1)} %get-tuple-element., ...), custom_call_target="tpu_custom_call" | custom-call | bytes 1048576 | tf_op jit(solution)/shard_map/expert_grads/pallas_call | solution.py:1166
  246.3 2.9 convolution_convert_fusion.2.own_ref
  249.2 24.8 %rows_to_heads.1.grad_ref = bf16[1024,256]{1,0:T(8,128)(2,1)S(1)} custom-call(bf16[512,512]{1,0:T(8,128)(2,1)S(1)} %convolution_convert_fusion.2.own_ref), custom_call_target="tpu_custom_call" | custom-call | bytes 1048576 | tf_op jit(solution)/shard_map/rows_to_heads/pallas_call | solution.py:713
  274.1 0.8 copy-done.15
  274.9 0.4 collective-permute-start.3
  275.3 1.2 collective-permute-start.4
  276.5 4.2 convolution_convert_fusion.g_out_ref
  280.6 9.4 %down_grads.1.downs_ref = bf16[2,6,256,256]{3,2,1,0:T(8,128)(2,1)} custom-call(bf16[6,256,256]{2,1,0:T(8,128)(2,1)} %get-tuple-element.167.refs_0_, bf16[6,256,256]{2,1,0:T(8,128)(2,1)} %collective-permute-done.refs_1_, bf16[6,256,256]{2,1,0:T(8,128)(2,1)} %collective-permute-done.1.refs_2_, bf16[6,256,256]{2,1,0:T(8,128)(2,1)} %collective-permute-done.2.refs_3_, ...), custom_call_target="tpu_custom_call" | custom-call | bytes 1048576 | tf_op jit(solution)/shard_map/down_grads/pallas_call | solution.py:1223
  290.1 16.9 %attend_back.1 = (f32[2,1024,256]{2,1,0:T(8,128)}, bf16[1024,256]{1,0:T(8,128)(2,1)}, f32[2,1,256]{2,1,0:T(1,128)}, f32[1024,2]{1,0:T(8,128)}) custom-call(bf16[1024,256]{1,0:T(8,128)(2,1)} %copy-done.15, bf16[1024,768]{1,0:T(8,128)(2,1)} %copy-done.16, f32[1024,256]{1,0:T(8,128)} %copy-done.18, f32[1024,256]{1,0:T(8,128)} %copy-done.19, ...), custom_call_target="tpu_custom_call" | custom-call | bytes 1048576 | tf_op jit(solution)/shard_map/attend_back/pallas_call | solution.py:1401
  307.0 3.6 collective-permute-done.4.gate_own_ref
  310.6 1.2 copy.45
  311.9 5.4 %ctx_sum.3 = f32[16,128]{1,0:T(8,128)S(1)} custom-call(f32[16,128]{1,0:T(8,128)S(1)} %reshape.212.own_ref), custom_call_target="tpu_custom_call" | custom-call | bytes 20971520 | tf_op jit(solution)/shard_map/ctx_sum/pallas_call | solution.py:537
  317.3 0.5 collective-permute-start.5
  317.9 1.0 copy.46
  318.9 15.1 %project_back.1 = (bf16[1024,2048]{1,0:T(8,128)(2,1)}, bf16[2048,768]{1,0:T(8,128)(2,1)}, f32[1,2048]{1,0:T(1,128)}) custom-call(f32[2,1024,256]{2,1,0:T(8,128)} %get-tuple-element.197.back_ref, f32[1024,768]{1,0:T(8,128)} %get-tuple-element.118.lin_ref, f32[1024,2]{1,0:T(8,128)} %bitcast.41, f32[1024,2]{1,0:T(8,128)} %bitcast.44, ...), custom_call_target="tpu_custom_call" | custom-call | bytes 1048576 | tf_op jit(solution)/shard_map/project_back/pallas_call | solution.py:2181
  334.1 0.9 concatenate.23
  335.0 0.7 pad.14.small_ref
  335.6 136.9 %finish_sums.1 = (f32[6,256,256]{2,1,0:T(8,128)}, f32[6,256,256]{2,1,0:T(8,128)}, f32[6,256,256]{2,1,0:T(8,128)}, f32[128,2048]{1,0:T(8,128)}, f32[512,256]{1,0:...) custom-call(bf16[2,6,256,256]{3,2,1,0:T(8,128)(2,1)} %down_grads.1.downs_ref, ...), custom_call_target="tpu_custom_call" | custom-call | bytes 734003200 | tf_op jit(solution)/shard_map/finish_sums/pallas_call | solution.py:1748
  472.5 1.5 slice_bitcast_fusion
  474.0 1.5 fusion.31
  475.5 1.9 copy.61
  477.4 2.3 copy.62
  479.7 1.1 copy.63
  480.8 0.2 copy-done.32
  481.0 0.8 copy.64
  481.8 1.1 copy.65
  483.0 1.1 copy.66
  484.1 0.8 copy-done.27
  485.0 1.1 copy.67
  (94 shorter events, 0.6 us)
Async XLA Ops:
  7.2 105.9 %copy-start = (bf16[512,2048]{1,0:T(8,128)(2,1)S(1)}, bf16[512,2048]{1,0:T(8,128)(2,1)}, u32[]{:S(2)}) copy-start(bf16[512,2048]{1,0:T(8,128)(2,1)} %param.23) | copy-start | bytes 6291460
  7.2 218.7 %all-gather.4.cloned.1.call-start = ((), (), s32[]{:S(2)}) async-start(), calls=%async_computation.1 | async-start | bytes 1310720 | tf_op jit(solution)/shard_map/all_gather | solution.py:2307
  8.2 80.7 %copy-start.24 = (s32[1,1024]{1,0:T(1,128)}, s32[1,1024]{1,0:T(1,128)S(1)}, u32[]{:S(2)}) copy-start(s32[1,1024]{1,0:T(1,128)S(1)} %compare_select_fusion.places_ref) | copy-start | bytes 12292
  69.0 16.3 %copy-start.35 = (s32[1,16]{1,0:T(1,128)S(1)}, s32[1,16]{1,0:T(1,128)}, u32[]{:S(2)}) copy-start(s32[1,16]{1,0:T(1,128)} %param.16) | copy-start | bytes 196
  85.3 3.6 copy-start.3
  86.6 2.3 copy-start.25
  86.6 2.3 copy-start.1
  86.6 2.3 copy-start.13
  86.6 2.3 copy-start.14
  88.9 8.2 %copy-start.11 = (f32[1024,128]{1,0:T(8,128)}, f32[1024,128]{1,0:T(8,128)S(1)}, u32[]{:S(2)}) copy-start(f32[1024,128]{1,0:T(8,128)S(1)} %get-tuple-element.231.cos_ref) | copy-start | bytes 1572868
  88.9 8.2 %copy-start.12 = (f32[1024,128]{1,0:T(8,128)}, f32[1024,128]{1,0:T(8,128)S(1)}, u32[]{:S(2)}) copy-start(f32[1024,128]{1,0:T(8,128)S(1)} %get-tuple-element.232.sin_ref) | copy-start | bytes 1572868
  97.1 17.3 %copy-start.16 = (bf16[1024,768]{1,0:T(8,128)(2,1)}, bf16[1024,768]{1,0:T(8,128)(2,1)S(1)}, u32[]{:S(2)}) copy-start(bf16[1024,768]{1,0:T(8,128)(2,1)S(1)} %get-tuple-element.178.low_ref) | copy-start | bytes 4718596
  97.1 17.3 %copy-start.18 = (f32[1024,256]{1,0:T(8,128)}, f32[1024,256]{1,0:T(8,128)S(1)}, u32[]{:S(2)}) copy-start(f32[1024,256]{1,0:T(8,128)S(1)} %get-tuple-element.179.attended_ref) | copy-start | bytes 3145732
  97.1 17.3 %copy-start.19 = (f32[1024,256]{1,0:T(8,128)}, f32[1024,256]{1,0:T(8,128)S(1)}, u32[]{:S(2)}) copy-start(f32[1024,256]{1,0:T(8,128)S(1)} %get-tuple-element.180.top_ref) | copy-start | bytes 3145732
  113.1 1.3 copy-start.22
  113.1 1.3 copy-start.2
  143.6 1.0 copy-start.4
  144.6 1.3 copy-start.8
  145.9 134.7 %all-gather.6.cloned.1.call-start = ((), (), s32[]{:S(2)}) async-start(), calls=%async_computation.3 | async-start | bytes 2621440 | tf_op jit(solution)/shard_map/all_gather | solution.py:2250
  146.7 189.0 %reduce-scatter.2.cloned.1.call-start = ((), (), s32[]{:S(2)}) async-start(), calls=%async_computation.2 | async-start | bytes 2621440 | tf_op jit(solution)/shard_map/reduce_scatter | solution.py:2317
  150.9 30.8 %copy-start.5 = (f32[128,2048]{1,0:T(8,128)S(1)}, f32[128,2048]{1,0:T(8,128)}, u32[]{:S(2)}) copy-start(f32[128,2048]{1,0:T(8,128)} %copy-done.4) | copy-start | bytes 3145732
  150.9 30.8 %copy-start.10 = (bf16[1,128,2048]{2,1,0:T(8,128)(2,1)S(1)}, bf16[1,128,2048]{2,1,0:T(8,128)(2,1)}, u32[]{:S(2)}) copy-start(bf16[1,128,2048]{2,1,0:T(8,128)(2,1)} %param.29) | copy-start | bytes 1572868
  176.2 98.7 %collective-permute-start = (bf16[6,256,256]{2,1,0:T(8,128)(2,1)}, bf16[6,256,256]{2,1,0:T(8,128)(2,1)}, u32[]{:S(2)}, u32[]{:S(2)}) collective-permute-start(bf16[6,256,256]{2,1,0:T(8,128)(2,1)} %get-tuple-element.167.refs_0_), channel_id=1, source_target_pairs={{0,8},{4,12},{8,0},{12,4},{16,24},{20,28},{24,16},{28,20},{1,9},{5... | collective-permute-start | bytes 2359304 | tf_op jit(solution)/shard_map/ppermute | solution.py:733
  177.1 97.8 %collective-permute-start.1 = (bf16[6,256,256]{2,1,0:T(8,128)(2,1)}, bf16[6,256,256]{2,1,0:T(8,128)(2,1)}, u32[]{:S(2)}, u32[]{:S(2)}) collective-permute-start(bf16[6,256,256]{2,1,0:T(8,128)(2,1)} %get-tuple-element.167.refs_0_), channel_id=1, source_target_pairs={{0,16},{4,20},{8,24},{12,28},{16,0},{20,4},{24,8},{28,12},{1,17},{... | collective-permute-start | bytes 2359304 | tf_op jit(solution)/shard_map/ppermute | solution.py:733
  181.8 93.1 %collective-permute-start.2 = (bf16[6,256,256]{2,1,0:T(8,128)(2,1)}, bf16[6,256,256]{2,1,0:T(8,128)(2,1)}, u32[]{:S(2)}, u32[]{:S(2)}) collective-permute-start(bf16[6,256,256]{2,1,0:T(8,128)(2,1)} %get-tuple-element.167.refs_0_), channel_id=1, source_target_pairs={{0,24},{4,28},{8,16},{12,20},{16,8},{20,12},{24,0},{28,4},{1,25},{... | collective-permute-start | bytes 2359304 | tf_op jit(solution)/shard_map/ppermute | solution.py:733
  181.8 1.1 copy-start.6
  182.9 1.1 copy-start.7
  184.1 1.6 copy-start.9
  221.8 1.0 copy-start.17
  222.8 0.9 copy-start.20
  223.7 0.9 copy-start.21
  224.6 1.3 copy-start.26
  249.2 27.2 %copy-start.23 = (bf16[512,512]{1,0:T(8,128)(2,1)S(1)}, bf16[512,512]{1,0:T(8,128)(2,1)}, u32[]{:S(2)}) copy-start(bf16[512,512]{1,0:T(8,128)(2,1)} %copy-done.22) | copy-start | bytes 1572868
  274.1 0.8 copy-start.15
  274.9 32.1 %collective-permute-start.3 = (bf16[6,256,256]{2,1,0:T(8,128)(2,1)}, bf16[6,256,256]{2,1,0:T(8,128)(2,1)S(1)}, u32[]{:S(2)}, u32[]{:S(2)}) collective-permute-start(bf16[6,256,256]{2,1,0:T(8,128)(2,1)} %get-tuple-element.162), channel_id=1, source_target_pairs={{0,8},{4,12},{8,0},{12,4},{16,24},{20,28},{24,16},{28,20},{1,9},{5... | collective-permute-start | bytes 2359304 | tf_op jit(solution)/shard_map/ppermute | solution.py:733
  275.3 35.3 %collective-permute-start.4 = (bf16[6,256,256]{2,1,0:T(8,128)(2,1)}, bf16[6,256,256]{2,1,0:T(8,128)(2,1)}, u32[]{:S(2)}, u32[]{:S(2)}) collective-permute-start(bf16[6,256,256]{2,1,0:T(8,128)(2,1)} %get-tuple-element.161), channel_id=1, source_target_pairs={{0,8},{4,12},{8,0},{12,4},{16,24},{20,28},{24,16},{28,20},{1,9},{5... | collective-permute-start | bytes 2359304 | tf_op jit(solution)/shard_map/ppermute | solution.py:733
  290.1 27.8 %copy-start.33 = (f32[16,2048]{1,0:T(8,128)S(1)}, f32[16,2048]{1,0:T(8,128)}, u32[]{:S(2)}) copy-start(f32[16,2048]{1,0:T(8,128)} %get-tuple-element.207) | copy-start | bytes 393220
  307.0 27.0 %copy-start.31 = (bf16[6,256,256]{2,1,0:T(8,128)(2,1)}, bf16[6,256,256]{2,1,0:T(8,128)(2,1)S(1)}, u32[]{:S(2)}) copy-start(bf16[6,256,256]{2,1,0:T(8,128)(2,1)S(1)} %collective-permute-done.3.gate_far_ref) | copy-start | bytes 2359300
  317.3 18.3 %collective-permute-start.5 = (bf16[6,256,256]{2,1,0:T(8,128)(2,1)}, bf16[6,256,256]{2,1,0:T(8,128)(2,1)}, u32[]{:S(2)}, u32[]{:S(2)}) collective-permute-start(bf16[6,256,256]{2,1,0:T(8,128)(2,1)} %get-tuple-element.196), channel_id=1, source_target_pairs={{0,8},{4,12},{8,0},{12,4},{16,24},{20,28},{24,16},{28,20},{1,9},{5... | collective-permute-start | bytes 2359304 | tf_op jit(solution)/shard_map/ppermute | solution.py:733
  318.9 15.1 %copy-start.34 = (f32[2,1,256]{2,1,0:T(1,128)S(1)}, f32[2,1,256]{2,1,0:T(1,128)}, u32[]{:S(2)}) copy-start(f32[2,1,256]{2,1,0:T(1,128)} %get-tuple-element.205) | copy-start | bytes 6148
  472.5 7.1 %copy-start.30 = (f32[512,768]{1,0:T(8,128)S(1)}, f32[512,768]{1,0:T(8,128)}, u32[]{:S(2)}) copy-start(f32[512,768]{1,0:T(8,128)} %get-tuple-element.248) | copy-start | bytes 4718596
  479.7 1.4 copy-start.32
  479.7 2.2 copy-start.29
  481.0 1.9 copy-start.28
  483.0 2.0 copy-start.27
Sparse Core Ops, SparseCore 0:
  146.1 18.1 all-gather.3
  165.8 22.6 all-gather.5
  275.0 29.3 reduce-scatter.1

commit v2 on v1

--- a/solution.py
+++ b/solution.py
@@ -733,7 +733,7 @@
     return lax.ppermute(values, "ctx", [(i, i ^ flip) for i in range(lax.axis_size("ctx"))])
 
 
-def reduce_then_gather(partial, extras, out_shapes, chunk_math, name, collective_id, crossed, bulk):
+def reduce_then_gather(partial, extras, out_shapes, chunk_math, name, collective_id, crossed, bulk, vmem):
     ctx, fsdp = lax.axis_size("ctx"), lax.axis_size("fsdp")
     rows, width = partial.shape[0] // fsdp, partial.shape[1]
     chunks = 4
@@ -837,6 +837,7 @@
             DMA((2, max(1, bulk_count))),
         ],
         100 * 2**20,
+        vmem,
     )(partial, *extras, *bulk)
 
 
@@ -873,40 +874,36 @@
 
 
 def slots_of(pairs, experts, top):
-    count = len(pairs)
-    blocks, _, rows = pairs[0].shape
+    lines, rows = pairs.shape
     absent = float(rows * top)
 
-    def kernel(*refs):
-        for pairs_ref, out_ref in zip(refs[:count], refs[count:]):
-            out_ref[...] = jnp.full(out_ref.shape, -1, jnp.int32)
-            for b in range(blocks):
-                rank_rows = []
-                for expert in range(experts):
-                    rank = jnp.full((1, rows), absent, jnp.float32)
-                    for k in range(top):
-                        rank = jnp.where(
-                            pairs_ref[b, k : k + 1, :] == expert,
-                            pairs_ref[b, top + k : top + k + 1, :].astype(jnp.float32),
-                            rank,
-                        )
-                    rank_rows.append(rank)
-                filler = jnp.full((rows - experts, rows), absent, jnp.float32)
-                by_column = jnp.concatenate(rank_rows + [filler], axis=0).T
-                for expert, rank in enumerate(rank_rows):
-                    earlier = jnp.where(by_column[:, expert : expert + 1] < rank, 1.0, 0.0)
-                    slot = jnp.where(rank < absent, jnp.sum(earlier, axis=0, keepdims=True), -1.0)
-                    out_ref[expert : expert + 1, b * rows : (b + 1) * rows] = slot.astype(jnp.int32)
-
-    shape = jax.ShapeDtypeStruct((ROUTER_ROWS, blocks * rows), jnp.int32)
+    def kernel(pairs_ref, out_ref):
+        out_ref[...] = jnp.full(out_ref.shape, -1, jnp.int32)
+        rank_rows = []
+        for expert in range(experts):
+            rank = jnp.full((1, rows), absent, jnp.float32)
+            for k in range(top):
+                rank = jnp.where(
+                    pairs_ref[k : k + 1, :] == expert,
+                    pairs_ref[top + k : top + k + 1, :].astype(jnp.float32),
+                    rank,
+                )
+            rank_rows.append(rank)
+        filler = jnp.full((rows - experts, rows), absent, jnp.float32)
+        by_column = jnp.concatenate(rank_rows + [filler], axis=0).T
+        for expert, rank in enumerate(rank_rows):
+            earlier = jnp.where(by_column[:, expert : expert + 1] < rank, 1.0, 0.0)
+            slot = jnp.where(rank < absent, jnp.sum(earlier, axis=0, keepdims=True), -1.0)
+            out_ref[expert : expert + 1, :] = slot.astype(jnp.int32)
+
     return pl.pallas_call(
         kernel,
-        out_shape=[shape] * count,
-        in_specs=[VMEM] * count,
-        out_specs=[VMEM] * count,
+        out_shape=jax.ShapeDtypeStruct((lines, rows), jnp.int32),
+        in_specs=[VMEM],
+        out_specs=VMEM,
         cost_estimate=pl.CostEstimate(flops=10**7, bytes_accessed=2**20, transcendentals=0),
         name="slots_of",
-    )(*pairs)
+    )(pairs)
 
 
 def run_experts(group, dy_all, slots, router, w_gate, w_up, w_down, blocks, capacity):
@@ -957,7 +954,7 @@
             for b in range(blocks):
                 for e in range(experts):
                     disp[b, pl.ds(e * capacity, capacity), :] = (
-                        one_hot(slots_ref[pl.ds(e, 1), block_rows(b)], capacity)
+                        one_hot(slots_ref[b, pl.ds(e, 1), :], capacity)
                         .astype(f32)
                         .astype(bf16)
                     )
@@ -978,10 +975,7 @@
             slot_dy, down_matrix, (((1,), (1,)), ((), ())), preferred_element_type=f32
         )
         own_probs = probs[pl.ds(expert, 1), :]
-        own_slots = slots_ref[pl.ds(expert, 1), :]
-        hots = [
-            one_hot(own_slots[:, b * rows : (b + 1) * rows], capacity) for b in range(blocks)
-        ]
+        hots = [one_hot(slots_ref[b, pl.ds(expert, 1), :], capacity) for b in range(blocks)]
         value = jnp.concatenate(
             [
                 jnp.sum(
@@ -1065,7 +1059,7 @@
         in_specs=[
             whole((total, width)),
             whole((total, width)),
-            whole((ROUTER_ROWS, total)),
+            whole(slots.shape),
             whole((ROUTER_ROWS, width)),
             by_expert((width, units)),
             by_expert((width, units)),
@@ -1124,7 +1118,7 @@
                     span = pl.ds(b * rows, rows)
                     disp = jnp.concatenate(
                         [
-                            one_hot(slots_ref[pl.ds(e, 1), span], capacity).astype(f32)
+                            one_hot(slots_ref[b, pl.ds(e, 1), :], capacity).astype(f32)
                             for e in range(experts)
                         ],
                         axis=0,
@@ -1169,7 +1163,7 @@
         out_shape=[jax.ShapeDtypeStruct((experts, units, cols), bf16)] * (4 * kinds),
         in_specs=[slot_spec] * (2 * kinds)
         + [whole((total, 2 * half)), whole((total, half))]
-        + [whole((ROUTER_ROWS, total))] * 2,
+        + [whole(slots_own.shape)] * 2,
         out_specs=[pl.BlockSpec((1, units, cols), lambda e: (e, 0, 0))] * (4 * kinds),
         scratch_shapes=[pltpu.VMEM((experts, 2 * held, half), bf16)],
         compiler_params=pltpu.CompilerParams(vmem_limit_bytes=60 * 2**20),
@@ -1197,7 +1191,7 @@
                     span = pl.ds(b * rows, rows)
                     disp = jnp.concatenate(
                         [
-                            one_hot(slots_ref[pl.ds(e, 1), span], capacity).astype(f32)
+                            one_hot(slots_ref[b, pl.ds(e, 1), :], capacity).astype(f32)
                             for e in range(experts)
                         ],
                         axis=0,
@@ -1243,12 +1237,21 @@
     return (places >= first_ref[span, :]) & (places <= last_ref[span, :])
 
 
+def stored_runs(total):
+    ctx = lax.axis_size("ctx")
+    rows = total // ctx
+    run = rows // 2
+    starts = [i * rows for i in range(ctx)]
+    return starts + [i * rows + run for i in reversed(range(ctx))], run
+
+
 def attend(projected, scales, gains, cosine, sine_part, first, last, places, cols):
     total = projected.shape[0]
     head_dim = cosine.shape[1]
     heads = cols // head_dim
     size = math.gcd(total, 256)
     score_scale = head_dim ** (-0.5)
+    starts, run = stored_runs(total)
     f32, bf16 = jnp.float32, jnp.bfloat16
 
     def kernel(
@@ -1272,33 +1275,36 @@
                 if kind < 2:
                     values = values * scales_ref[:, kind : kind + 1] * gains_ref[:, span]
                     values = values * cos_ref[...] + roll_half(values) * sin_ref[...]
-                low_ref[:, span] = values.astype(bf16)
+                values = values.astype(bf16)
+                for place, start in enumerate(starts):
+                    low_ref[pl.ds(place * run, run), span] = values[start : start + run]
         for h in range(heads):
             head = pl.ds(h * head_dim, head_dim)
-            keys = low_ref[:, pl.ds(cols + h * head_dim, head_dim)]
-            values = low_ref[:, pl.ds(2 * cols + h * head_dim, head_dim)]
-
-            def step(b, carry):
-                span = pl.ds(pl.multiple_of(b * size, size), size)
+            for b in range(total // size):
+                span, seen = pl.ds(b * size, size), pl.ds(0, (b + 1) * size)
                 scores = lax.dot_general(
                     low_ref[span, head],
-                    keys,
+                    low_ref[seen, pl.ds(cols + h * head_dim, head_dim)],
                     (((1,), (1,)), ((), ())),
                     preferred_element_type=f32,
                 )
-                allowed = allowed_keys(first_ref, last_ref, span, places_ref[...])
+                allowed = allowed_keys(first_ref, last_ref, span, places_ref[:, seen])
                 scores = jnp.where(allowed, scores * score_scale, MASKED)
                 top = jnp.max(scores, axis=1, keepdims=True)
                 weights = jnp.exp(scores - top)
                 sums = jnp.sum(weights, axis=1, keepdims=True)
                 probs = (weights * (1.0 / sums)).astype(bf16)
-                attended = jnp.dot(probs, values, preferred_element_type=f32)
+                attended = jnp.dot(
+                    probs,
+                    low_ref[seen, pl.ds(2 * cols + h * head_dim, head_dim)],
+                    preferred_element_type=f32,
+                )
                 attended_ref[span, head] = attended
-                attended_low_ref[span, head] = attended.astype(bf16)
+                attended_low = attended.astype(bf16)
+                for i in range(size // run):
+                    start = starts[b * (size // run) + i]
+                    attended_low_ref[pl.ds(start, run), head] = attended_low[i * run : (i + 1) * run]
                 top_ref[span, head] = jnp.broadcast_to(top + jnp.log(sums), (size, head_dim))
-                return carry
-
-            lax.fori_loop(0, total // size, step, 0)
 
     return pl.pallas_call(
         kernel,
@@ -1328,6 +1334,7 @@
     score_scale = head_dim ** (-0.5)
     f32, bf16 = jnp.float32, jnp.bfloat16
     contract_rows = (((0,), (0,)), ((), ()))
+    starts, run = stored_runs(total)
 
     def kernel(
         grad_ref,
@@ -1349,26 +1356,35 @@
         query_grad,
         key_grad,
         value_grad,
+        grads_moved,
     ):
+        for place, start in enumerate(starts):
+            grads_moved[pl.ds(place * run, run), :] = grad_ref[pl.ds(start, run), :]
+
+        def stored(values):
+            pieces = sorted((start, place) for place, start in enumerate(starts))
+            return jnp.concatenate([values[p * run : (p + 1) * run] for _, p in pieces], axis=0)
+
         totals = [jnp.zeros((total, 1), f32) for _ in range(2)]
         for h in range(heads):
             head = pl.ds(h * head_dim, head_dim)
-            keys = low_ref[:, pl.ds(cols + h * head_dim, head_dim)]
-            values = low_ref[:, pl.ds(2 * cols + h * head_dim, head_dim)]
             key_grad[...] = jnp.zeros_like(key_grad)
             value_grad[...] = jnp.zeros_like(value_grad)
-
-            def step(b, carry):
-                span = pl.ds(pl.multiple_of(b * size, size), size)
-                queries, grads = low_ref[span, head], grad_ref[span, head]
+            for b in range(total // size):
+                span, seen = pl.ds(b * size, size), pl.ds(0, (b + 1) * size)
+                queries, grads = low_ref[span, head], grads_moved[span, head]
+                keys = low_ref[seen, pl.ds(cols + h * head_dim, head_dim)]
                 scores = lax.dot_general(
                     queries, keys, (((1,), (1,)), ((), ())), preferred_element_type=f32
                 )
-                allowed = allowed_keys(first_ref, last_ref, span, places_ref[...])
+                allowed = allowed_keys(first_ref, last_ref, span, places_ref[:, seen])
                 scores = jnp.where(allowed, scores * score_scale, MASKED)
                 probs = jnp.exp(scores - top_ref[span, head][:, :1])
                 prob_grad = lax.dot_general(
-                    grads, values, (((1,), (1,)), ((), ())), preferred_element_type=f32
+                    grads,
+                    low_ref[seen, pl.ds(2 * cols + h * head_dim, head_dim)],
+                    (((1,), (1,)), ((), ())),
+                    preferred_element_type=f32,
                 )
                 delta = jnp.sum(
                     grads.astype(f32) * attended_ref[span, head], axis=1, keepdims=True
@@ -1377,17 +1393,15 @@
                 query_grad[span, :] = (
                     jnp.dot(score_grad, keys, preferred_element_type=f32) * score_scale
                 )
-                key_grad[...] += lax.dot_general(
+                key_grad[seen, :] += lax.dot_general(
                     score_grad, queries, contract_rows, preferred_element_type=f32
                 )
-                value_grad[...] += lax.dot_general(
+                value_grad[seen, :] += lax.dot_general(
                     probs.astype(bf16), grads, contract_rows, preferred_element_type=f32
                 )
-                return carry
-
-            lax.fori_loop(0, total // size, step, 0)
-            value_ref[:, head] = value_grad[...].astype(bf16)
+            value_ref[:, head] = stored(value_grad[...].astype(bf16))
             for kind, grad in ((0, query_grad[...]), (1, key_grad[...] * score_scale)):
+                grad = stored(grad)
                 span = pl.ds(kind * cols + h * head_dim, head_dim)
                 unit = lin_ref[:, span] * scales_ref[:, kind : kind + 1]
                 grad = grad * cos_ref[...] - roll_half(grad) * sin_ref[...]
@@ -1408,7 +1422,7 @@
         ],
         in_specs=[VMEM] * 12,
         out_specs=[VMEM] * 4,
-        scratch_shapes=[pltpu.VMEM((total, head_dim), f32)] * 3,
+        scratch_shapes=[pltpu.VMEM((total, head_dim), f32)] * 3 + [pltpu.VMEM((total, cols), bf16)],
         compiler_params=pltpu.CompilerParams(vmem_limit_bytes=60 * 2**20),
         cost_estimate=pl.CostEstimate(flops=0, bytes_accessed=2**20, transcendentals=0),
         name="attend_back",
@@ -2188,7 +2202,7 @@
         ],
         in_specs=[
             pl.BlockSpec((2, size, cols), lambda i: (0, jnp.minimum(i, steps - 1), 0)),
-            by_rows(wide),
+            by_rows(2 * cols),
             by_rows(2),
             by_rows(2),
             by_rows(cols),
@@ -2240,8 +2254,14 @@
     router_rows = jnp.pad(w_router.T, ((0, ROUTER_ROWS - experts), (0, 0)))
     pairs = jnp.concatenate([routes[0].T, slot_order[0].T], axis=0)
     pairs = jnp.pad(pairs, ((0, -pairs.shape[0] % 8), (0, 0)))
-    tokens_all, qkv_weight, dy_all, gains, router_rows, *pairs, dy_parts = gather_inputs(
-        tokens[0], w_qkv, cotangent[0], [gains, router_rows], pairs, [1, 2, 4, 6], 9
+    tokens_all, qkv_weight, dy_all, gains, router_rows, *slots, dy_parts = gather_inputs(
+        tokens[0],
+        w_qkv,
+        cotangent[0],
+        [gains, router_rows],
+        slots_of(pairs, experts, top),
+        [1, 2, 4, 6],
+        9,
     )
     row_gain_one, gain_query, gain_key, row_gain_two = (
         gains[i : i + 1].astype(f32) for i in range(4)
@@ -2250,16 +2270,17 @@
     dy_parts = lax.all_gather(dy_parts, "fsdp", axis=0)
 
     stream_pos = dealt_position(jnp.arange(total, dtype=jnp.int32), rows, ctx)
-    stream_doc, stream_inner = document_info(stream_pos, lengths)
+    stream_inner = document_info(stream_pos, lengths)[1]
     cosine, sine_part = rope_tables(stream_inner, head_dim)
     turn_tables = (
         jnp.concatenate([cosine, cosine], axis=1),
         jnp.concatenate([-sine_part, sine_part], axis=1),
     )
+    places = jnp.arange(total, dtype=jnp.int32)
     sight = (
-        (stream_pos - stream_inner).reshape(total, 1),
-        stream_pos.reshape(total, 1),
-        stream_pos.reshape(1, total),
+        (places - document_info(places, lengths)[1]).reshape(total, 1),
+        places.reshape(total, 1),
+        places.reshape(1, total),
     )
     normed_all, projected, squares = project(tokens_all, row_gain_one, qkv_weight)
     squares = squares.T
@@ -2285,10 +2306,11 @@
         6,
         True,
         [],
+        16,
     )
 
     capacity = rows * top // experts
-    slot_by_expert, slots_other, *slots_line = slots_of(pairs, experts, top)
+    slot_by_expert, slots_other, *slots_line = slots
     moved_part, group_grad, g_router, scaled, gate_low, up_low = run_experts(
         group, dy_all, slot_by_expert, router_rows, w_gate, w_up, w_down, fsdp, capacity
     )
@@ -2302,6 +2324,7 @@
         7,
         False,
         [gate_low, up_low],
+        60,
     )
     g_ffn_gain = g_ffn_gain[0]
     crossed = lax.all_gather(crossed, "fsdp", axis=0, tiled=True)

time: 503 us -> 496 us (0.986)
  local copies, waits for them, and re-layouts: 34.3 us -> 28.8 us
    pallas_call x1, Pallas kernels: 9.44 us -> 18.6 us  [down_grads(): pl.pallas_call(kernel, grid=(experts,), out_shape=jax.ShapeDtypeStruct((2...]
    unnamed x79 -> x59, local copies, waits for them, and re-layouts: 21.8 us -> 14.7 us
  transfers between devices with their start and end apart: 9 -> 9, of which waited for: 1 -> 0; matrix products, arithmetic and copies ran while one was open for 2% -> 3% of each run, Pallas kernels for 32% -> 33%
where the time goes in v2:
time: 496 us; the launch traced here: 486 us
  Pallas kernels  421 us (85%)
  local copies, waits for them, and re-layouts  28.8 us (6%)
  between operations  14.4 us (3%)
  matrix products  8.38 us (2%)
  starting transfers between devices  7.51 us (2%)
    pallas_call x1, Pallas kernels, finish_sums(): comm_call(kernel, 'finish_sums', collective_id, [jax.ShapeDtypeStruct(gra...  137 us
    pallas_call x2, Pallas kernels, reduce_then_gather(): comm_call(kernel, name, collective_id, [jax.ShapeDtypeStruct(partial.shap...  69.3 us
    pallas_call x1, Pallas kernels, gather_inputs(): comm_call(kernel, 'gather_inputs', collective_id, [jax.ShapeDtypeStruct((...  55.3 us
    pallas_call x1, Pallas kernels, run_experts(): pl.pallas_call(kernel, grid=(experts,), out_shape=[jax.ShapeDtypeStruct((...  25.2 us
    pallas_call x1, Pallas kernels, rows_to_heads(): comm_call(kernel, 'rows_to_heads', collective_id, jax.ShapeDtypeStruct((c...  24.7 us
    pallas_call x1, Pallas kernels, expert_grads(): pl.pallas_call(kernel, grid=(experts,), out_shape=[jax.ShapeDtypeStruct((...  20.3 us
    pallas_call x1, Pallas kernels, down_grads(): pl.pallas_call(kernel, grid=(experts,), out_shape=jax.ShapeDtypeStruct((2...  18.6 us
    pallas_call x1, Pallas kernels, heads_to_rows(): comm_call(kernel, 'heads_to_rows', collective_id, jax.ShapeDtypeStruct((f...  16 us
  transfers between devices with their start and end apart: 9, of which 0 were waited for; matrix products, arithmetic and copies ran while one was open for 3% of the time, Pallas kernels for 33%

profile of v2, /device:TPU:5, one launch (start us, length us, event | category | flops | bytes accessed | tf_op | source)
XLA Modules:
  0.0 486.1 jit_solution(2284525713886166830)
XLA Ops:
  7.2 0.0 all-gather.4.cloned.1.call-start
  7.3 0.8 copy_bitcast_fusion
  8.1 0.6 pad.13.pairs_ref
  8.7 1.6 slots_of.1.refs_5_
  10.3 0.7 pad_maximum_fusion.2
  11.1 0.6 reshape.93.refs_3_
  11.7 1.3 pad.12.refs_4_
  13.0 55.3 %gather_inputs.1 = (bf16[1024,2048]{1,0:T(8,128)(2,1)}, bf16[2048,768]{1,0:T(8,128)(2,1)}, bf16[512,2048]{1,0:T(8,128)(2,1)}, bf16[4,2048]{1,0:T(4,128)(2,1)}, b...) custom-call(bf16[128,2048]{1,0:T(8,128)(2,1)} %bitcast.36, ...), custom_call_target="tpu_custom_call" | custom-call | bytes 157286400 | tf_op jit(solution)/shard_map/gather_inputs/pallas_call | solution.py:2063
  68.3 1.5 slice_convert_fusion
  69.8 9.3 %project.1 = (bf16[1024,2048]{1,0:T(8,128)(2,1)}, f32[1024,768]{1,0:T(8,128)}, f32[1024,2]{1,0:T(8,128)}) custom-call(bf16[1024,2048]{1,0:T(8,128)(2,1)} %get-tuple-element.110.tokens_ref, f32[1,2048]{1,0:T(1,128)} %get-tuple-element.217.gain_ref, bf16[2048,768]{1,0:T(8,128)(2,1)} %get-tuple-element.112.weight_ref), custom_call_target="tpu_custom_call" | custom-call | flops 3000000000 | bytes 15728640 | tf_op jit(solution)/shard_map/project/pallas_call | solution.py:2116
  79.2 1.2 copy.41
  80.4 5.4 %ctx_sum.2 = f32[16,128]{1,0:T(8,128)S(1)} custom-call(f32[16,128]{1,0:T(8,128)S(1)} %reshape.94.own_ref), custom_call_target="tpu_custom_call" | custom-call | bytes 20971520 | tf_op jit(solution)/shard_map/ctx_sum/pallas_call | solution.py:537
  85.9 0.2 copy.42
  86.1 0.1 select_reduce_fusion.2
  86.3 0.1 select_reduce_fusion
  86.4 1.0 copy.43.first_ref
  87.4 1.9 fusion
  89.3 0.3 pad_maximum_fusion
  89.8 6.5 %attend.1 = (bf16[1024,768]{1,0:T(8,128)(2,1)S(1)}, f32[1024,256]{1,0:T(8,128)S(1)}, bf16[1024,256]{1,0:T(8,128)(2,1)S(1)}, f32[1024,256]{1,0:T(8,128)S(1)}) custom-call(f32[1024,768]{1,0:T(8,128)S(1)} %copy-done.1, f32[1024,2]{1,0:T(8,128)S(1)} %bitcast.39, f32[1,512]{1,0:T(1,128)S(1)} %pad_maximum_fusion.3.gains_ref, ...), custom_call_target="tpu_custom_call" | custom-call | flops 2000000000 | bytes 20971520 | tf_op jit(solution)/shard_map/attend/pallas_call | solution.py:1309
  96.4 16.0 %heads_to_rows.1 = bf16[512,512]{1,0:T(8,128)(2,1)S(1)} custom-call(bf16[1024,256]{1,0:T(8,128)(2,1)S(1)} %get-tuple-element.115.own_ref), custom_call_target="tpu_custom_call" | custom-call | bytes 41943040 | tf_op jit(solution)/shard_map/heads_to_rows/pallas_call | solution.py:626
  112.4 1.3 convolution_convert_fusion.1.refs_0_
  113.7 29.1 %mix_and_norm.1 = (bf16[512,2048]{1,0:T(8,128)(2,1)S(1)}, f32[128,2048]{1,0:T(8,128)S(1)}, bf16[128,1024]{1,0:T(8,128)(2,1)}) custom-call(bf16[512,2048]{1,0:T(8,128)(2,1)S(1)} %convolution_convert_fusion.1.refs_0_, bf16[128,2048]{1,0:T(8,128)(2,1)S(1)} %bitcast.38, f32[1,2048]{1,0:T(1,128)S(1)} %get-tuple-element.214.refs_2_), custom_call_target="tpu_custom_call" | custom-call | bytes 104857600 | tf_op jit(solution)/shard_map/mix_and_norm/pallas_call | solution.py:821
  142.9 1.0 copy-done.4
  143.8 1.4 copy-done.5
  145.2 0.0 all-gather.6.cloned.1.call-start
  145.3 0.7 all-gather.6.cloned.1.call-update
  146.0 0.0 reduce-scatter.2.cloned.1.call-start
  146.0 25.2 %run_experts.1 = (bf16[512,2048]{1,0:T(8,128)(2,1)}, bf16[512,2048]{1,0:T(8,128)(2,1)}, f32[16,2048]{1,0:T(8,128)}, bf16[6,256,256]{2,1,0:T(8,128)(2,1)}, bf16[6...) custom-call(bf16[512,2048]{1,0:T(8,128)(2,1)} %copy-done.5, bf16[512,2048]{1,0:T(8,128)(2,1)} %get-tuple-element.117.dy_ref, ...), custom_call_target="tpu_custom_call" | custom-call | flops 30000001024 | bytes 31457280 | tf_op jit(solution)/shard_map/run_experts/pallas_call | solution.py:1050
  171.2 0.9 collective-permute-start
  172.1 4.5 collective-permute-start.1
  176.6 40.1 %norm_back.1 = (bf16[512,2048]{1,0:T(8,128)(2,1)}, f32[128,2048]{1,0:T(8,128)}, f32[1,2048]{1,0:T(1,128)}, bf16[6,256,256]{2,1,0:T(8,128)(2,1)}, bf16[6,256,256]{2,1,0:T(8,128)(2,1)}) custom-call(bf16[512,2048]{1,0:T(8,128)(2,1)} %get-tuple-element.122.refs_0_, f32[128,2048]{1,0:T(8,128)} %copy-done.4, f32[1,2048]{1,0:T(1,128)} %copy-done.13, ...), custom_call_target="tpu_custom_call" | custom-call | bytes 104857600 | tf_op jit(solution)/shard_map/norm_back/pallas_call | solution.py:821
  216.7 0.0 all-gather.4.cloned.1.call-done.refs_5_
  216.7 20.3 %expert_grads.1 = (bf16[6,256,256]{2,1,0:T(8,128)(2,1)}, bf16[6,256,256]{2,1,0:T(8,128)(2,1)}, bf16[6,256,256]{2,1,0:T(8,128)(2,1)}, bf16[6,256,256]{2,1,0:T(8,1...) custom-call(bf16[6,256,256]{2,1,0:T(8,128)(2,1)} %get-tuple-element., ...), custom_call_target="tpu_custom_call" | custom-call | bytes 1048576 | tf_op jit(solution)/shard_map/expert_grads/pallas_call | solution.py:1160
  237.0 2.9 convolution_convert_fusion.2.own_ref
  239.9 24.7 %rows_to_heads.1.grad_ref = bf16[1024,256]{1,0:T(8,128)(2,1)S(1)} custom-call(bf16[512,512]{1,0:T(8,128)(2,1)S(1)} %convolution_convert_fusion.2.own_ref), custom_call_target="tpu_custom_call" | custom-call | bytes 1048576 | tf_op jit(solution)/shard_map/rows_to_heads/pallas_call | solution.py:713
  264.6 0.8 copy-done.9
  265.4 0.0 reduce-scatter.2.cloned.1.call-update
  265.4 0.4 collective-permute-start.3
  265.8 1.2 collective-permute-start.4
  267.0 4.3 convolution_convert_fusion.g_out_ref
  271.2 18.6 %down_grads.1.downs_ref = bf16[2,6,256,256]{3,2,1,0:T(8,128)(2,1)} custom-call(bf16[6,256,256]{2,1,0:T(8,128)(2,1)} %get-tuple-element.157.refs_0_, bf16[6,256,256]{2,1,0:T(8,128)(2,1)} %copy-done.20, bf16[6,256,256]{2,1,0:T(8,128)(2,1)} %collective-permute-done.1.refs_2_, bf16[6,256,256]{2,1,0:T(8,128)(2,1)} %collective-permute-done.2.refs_3_, ...), custom_call_target="tpu_custom_call" | custom-call | bytes 1048576 | tf_op jit(solution)/shard_map/down_grads/pallas_call | solution.py:1217
  289.8 0.8 iota.41.last_ref
  290.6 0.6 iota.42.places_ref
  291.2 12.2 %attend_back.1 = (f32[2,1024,256]{2,1,0:T(8,128)}, bf16[1024,256]{1,0:T(8,128)(2,1)}, f32[2,1,256]{2,1,0:T(1,128)}, f32[1024,2]{1,0:T(8,128)}) custom-call(bf16[1024,256]{1,0:T(8,128)(2,1)} %copy-done.9, bf16[1024,768]{1,0:T(8,128)(2,1)} %copy-done.10, f32[1024,256]{1,0:T(8,128)} %copy-done.11, f32[1024,256]{1,0:T(8,128)} %copy-done.12, ...), custom_call_target="tpu_custom_call" | custom-call | bytes 1048576 | tf_op jit(solution)/shard_map/attend_back/pallas_call | solution.py:1415
  303.5 1.2 copy.45
  304.7 5.4 %ctx_sum.3 = f32[16,128]{1,0:T(8,128)S(1)} custom-call(f32[16,128]{1,0:T(8,128)S(1)} %reshape.96.own_ref), custom_call_target="tpu_custom_call" | custom-call | bytes 20971520 | tf_op jit(solution)/shard_map/ctx_sum/pallas_call | solution.py:537
  310.1 0.5 collective-permute-start.5
  310.7 1.0 copy.46
  311.7 14.9 %project_back.1 = (bf16[1024,2048]{1,0:T(8,128)(2,1)}, bf16[2048,768]{1,0:T(8,128)(2,1)}, f32[1,2048]{1,0:T(1,128)}) custom-call(f32[2,1024,256]{2,1,0:T(8,128)} %get-tuple-element.187.back_ref, f32[1024,768]{1,0:T(8,128)} %get-tuple-element.113.lin_ref, f32[1024,2]{1,0:T(8,128)} %bitcast.41, f32[1024,2]{1,0:T(8,128)} %bitcast.44, ...), custom_call_target="tpu_custom_call" | custom-call | bytes 1048576 | tf_op jit(solution)/shard_map/project_back/pallas_call | solution.py:2195
  326.7 0.9 concatenate.23
  327.6 0.7 pad.14.small_ref
  328.3 0.9 copy-done.19
  329.2 136.6 %finish_sums.1 = (f32[6,256,256]{2,1,0:T(8,128)}, f32[6,256,256]{2,1,0:T(8,128)}, f32[6,256,256]{2,1,0:T(8,128)}, f32[128,2048]{1,0:T(8,128)}, f32[512,256]{1,0:...) custom-call(bf16[2,6,256,256]{3,2,1,0:T(8,128)(2,1)} %down_grads.1.downs_ref, ...), custom_call_target="tpu_custom_call" | custom-call | bytes 734003200 | tf_op jit(solution)/shard_map/finish_sums/pallas_call | solution.py:1762
  465.8 1.5 slice_bitcast_fusion
  467.3 1.5 fusion.16
  468.7 1.9 copy.61
  470.6 2.3 copy.62
  472.9 1.1 copy.63
  474.1 0.2 copy-done.21
  474.3 0.8 copy.64
  475.1 1.1 copy.65
  476.2 1.1 copy.66
  477.4 0.8 copy-done.15
  478.2 1.1 copy.67
  (76 shorter events, 0.4 us)
Async XLA Ops:
  7.2 105.2 %copy-start = (bf16[512,2048]{1,0:T(8,128)(2,1)S(1)}, bf16[512,2048]{1,0:T(8,128)(2,1)}, u32[]{:S(2)}) copy-start(bf16[512,2048]{1,0:T(8,128)(2,1)} %param.23) | copy-start | bytes 6291460
  7.2 209.5 %all-gather.4.cloned.1.call-start = ((), (), s32[]{:S(2)}) async-start(), calls=%async_computation.1 | async-start | bytes 1310720 | tf_op jit(solution)/shard_map/all_gather | solution.py:2330
  69.8 43.9 %copy-start.13 = (f32[1,2048]{1,0:T(1,128)}, f32[1,2048]{1,0:T(1,128)S(1)}, u32[]{:S(2)}) copy-start(f32[1,2048]{1,0:T(1,128)S(1)} %get-tuple-element.214.refs_2_) | copy-start | bytes 24580
  69.8 16.3 %copy-start.25 = (s32[1,16]{1,0:T(1,128)S(1)}, s32[1,16]{1,0:T(1,128)}, u32[]{:S(2)}) copy-start(s32[1,16]{1,0:T(1,128)} %param.16) | copy-start | bytes 196
  86.1 3.6 copy-start.3
  87.4 2.4 copy-start.14
  87.4 2.4 copy-start.1
  87.4 2.4 copy-start.8
  89.7 6.6 %copy-start.6 = (f32[1024,128]{1,0:T(8,128)}, f32[1024,128]{1,0:T(8,128)S(1)}, u32[]{:S(2)}) copy-start(f32[1024,128]{1,0:T(8,128)S(1)} %get-tuple-element.223.cos_ref) | copy-start | bytes 1572868
  89.7 6.6 %copy-start.7 = (f32[1024,128]{1,0:T(8,128)}, f32[1024,128]{1,0:T(8,128)S(1)}, u32[]{:S(2)}) copy-start(f32[1024,128]{1,0:T(8,128)S(1)} %get-tuple-element.224.sin_ref) | copy-start | bytes 1572868
  96.3 17.3 %copy-start.10 = (bf16[1024,768]{1,0:T(8,128)(2,1)}, bf16[1024,768]{1,0:T(8,128)(2,1)S(1)}, u32[]{:S(2)}) copy-start(bf16[1024,768]{1,0:T(8,128)(2,1)S(1)} %get-tuple-element.168.low_ref) | copy-start | bytes 4718596
  96.3 17.3 %copy-start.11 = (f32[1024,256]{1,0:T(8,128)}, f32[1024,256]{1,0:T(8,128)S(1)}, u32[]{:S(2)}) copy-start(f32[1024,256]{1,0:T(8,128)S(1)} %get-tuple-element.169.attended_ref) | copy-start | bytes 3145732
  96.4 17.3 %copy-start.12 = (f32[1024,256]{1,0:T(8,128)}, f32[1024,256]{1,0:T(8,128)S(1)}, u32[]{:S(2)}) copy-start(f32[1024,256]{1,0:T(8,128)S(1)} %get-tuple-element.170.top_ref) | copy-start | bytes 3145732
  112.4 1.3 copy-start.2
  142.9 1.0 copy-start.4
  143.8 1.4 copy-start.5
  145.2 126.0 %all-gather.6.cloned.1.call-start = ((), (), s32[]{:S(2)}) async-start(), calls=%async_computation.3 | async-start | bytes 2621440 | tf_op jit(solution)/shard_map/all_gather | solution.py:2270
  146.0 182.3 %reduce-scatter.2.cloned.1.call-start = ((), (), s32[]{:S(2)}) async-start(), calls=%async_computation.2 | async-start | bytes 2621440 | tf_op jit(solution)/shard_map/reduce_scatter | solution.py:2340
  171.2 94.2 %collective-permute-start = (bf16[6,256,256]{2,1,0:T(8,128)(2,1)}, bf16[6,256,256]{2,1,0:T(8,128)(2,1)S(1)}, u32[]{:S(2)}, u32[]{:S(2)}) collective-permute-start(bf16[6,256,256]{2,1,0:T(8,128)(2,1)} %get-tuple-element.157.refs_0_), channel_id=1, source_target_pairs={{0,8},{4,12},{8,0},{12,4},{16,24},{20,28},{24,16},{28,20},{1,9},{5... | collective-permute-start | bytes 2359304 | tf_op jit(solution)/shard_map/ppermute | solution.py:733
  172.1 93.3 %collective-permute-start.1 = (bf16[6,256,256]{2,1,0:T(8,128)(2,1)}, bf16[6,256,256]{2,1,0:T(8,128)(2,1)}, u32[]{:S(2)}, u32[]{:S(2)}) collective-permute-start(bf16[6,256,256]{2,1,0:T(8,128)(2,1)} %get-tuple-element.157.refs_0_), channel_id=1, source_target_pairs={{0,16},{4,20},{8,24},{12,28},{16,0},{20,4},{24,8},{28,12},{1,17},{... | collective-permute-start | bytes 2359304 | tf_op jit(solution)/shard_map/ppermute | solution.py:733
  176.6 88.9 %collective-permute-start.2 = (bf16[6,256,256]{2,1,0:T(8,128)(2,1)}, bf16[6,256,256]{2,1,0:T(8,128)(2,1)}, u32[]{:S(2)}, u32[]{:S(2)}) collective-permute-start(bf16[6,256,256]{2,1,0:T(8,128)(2,1)} %get-tuple-element.157.refs_0_), channel_id=1, source_target_pairs={{0,24},{4,28},{8,16},{12,20},{16,8},{20,12},{24,0},{28,4},{1,25},{... | collective-permute-start | bytes 2359304 | tf_op jit(solution)/shard_map/ppermute | solution.py:733
  264.6 0.8 copy-start.9
  265.4 5.8 %copy-start.20 = (bf16[6,256,256]{2,1,0:T(8,128)(2,1)}, bf16[6,256,256]{2,1,0:T(8,128)(2,1)S(1)}, u32[]{:S(2)}) copy-start(bf16[6,256,256]{2,1,0:T(8,128)(2,1)S(1)} %collective-permute-done.refs_1_) | copy-start | bytes 2359300
  265.4 38.0 %collective-permute-start.3 = (bf16[6,256,256]{2,1,0:T(8,128)(2,1)}, bf16[6,256,256]{2,1,0:T(8,128)(2,1)}, u32[]{:S(2)}, u32[]{:S(2)}) collective-permute-start(bf16[6,256,256]{2,1,0:T(8,128)(2,1)} %get-tuple-element.152), channel_id=1, source_target_pairs={{0,8},{4,12},{8,0},{12,4},{16,24},{20,28},{24,16},{28,20},{1,9},{5... | collective-permute-start | bytes 2359304 | tf_op jit(solution)/shard_map/ppermute | solution.py:733
  265.8 37.6 %collective-permute-start.4 = (bf16[6,256,256]{2,1,0:T(8,128)(2,1)}, bf16[6,256,256]{2,1,0:T(8,128)(2,1)}, u32[]{:S(2)}, u32[]{:S(2)}) collective-permute-start(bf16[6,256,256]{2,1,0:T(8,128)(2,1)} %get-tuple-element.151), channel_id=1, source_target_pairs={{0,8},{4,12},{8,0},{12,4},{16,24},{20,28},{24,16},{28,20},{1,9},{5... | collective-permute-start | bytes 2359304 | tf_op jit(solution)/shard_map/ppermute | solution.py:733
  291.2 19.5 %copy-start.22 = (f32[16,2048]{1,0:T(8,128)S(1)}, f32[16,2048]{1,0:T(8,128)}, u32[]{:S(2)}) copy-start(f32[16,2048]{1,0:T(8,128)} %get-tuple-element.197) | copy-start | bytes 393220
  310.1 18.1 %collective-permute-start.5 = (bf16[6,256,256]{2,1,0:T(8,128)(2,1)}, bf16[6,256,256]{2,1,0:T(8,128)(2,1)S(1)}, u32[]{:S(2)}, u32[]{:S(2)}) collective-permute-start(bf16[6,256,256]{2,1,0:T(8,128)(2,1)} %get-tuple-element.186), channel_id=1, source_target_pairs={{0,8},{4,12},{8,0},{12,4},{16,24},{20,28},{24,16},{28,20},{1,9},{5... | collective-permute-start | bytes 2359304 | tf_op jit(solution)/shard_map/ppermute | solution.py:733
  311.7 14.9 %copy-start.24 = (f32[2,1,256]{2,1,0:T(1,128)S(1)}, f32[2,1,256]{2,1,0:T(1,128)}, u32[]{:S(2)}) copy-start(f32[2,1,256]{2,1,0:T(1,128)} %get-tuple-element.195) | copy-start | bytes 6148
  311.7 15.0 %copy-start.23 = (f32[1,2048]{1,0:T(1,128)S(1)}, f32[1,2048]{1,0:T(1,128)}, u32[]{:S(2)}) copy-start(f32[1,2048]{1,0:T(1,128)} %get-tuple-element.196) | copy-start | bytes 24580
  328.3 0.9 copy-start.19
  465.8 7.1 %copy-start.18 = (f32[512,768]{1,0:T(8,128)S(1)}, f32[512,768]{1,0:T(8,128)}, u32[]{:S(2)}) copy-start(f32[512,768]{1,0:T(8,128)} %get-tuple-element.240) | copy-start | bytes 4718596
  472.9 1.4 copy-start.21
  472.9 2.2 copy-start.17
  474.3 1.9 copy-start.16
  476.2 2.0 copy-start.15
Sparse Core Ops, SparseCore 0:
  145.4 18.1 all-gather.3
  165.1 25.6 all-gather.5
  265.6 29.2 reduce-scatter.1

commit v3 on v2

--- a/solution.py
+++ b/solution.py
@@ -2346,9 +2346,9 @@
     back, value_grad, own_g_gains, inner_sums = attend_back(
         output_grad, low, attended, tops, projected, scales, own_gains, *turn_tables, *sight
     )
-    inner_sums, gate_far, gate_own = lax.optimization_barrier((inner_sums, gate_far, gate_own))
+    inner_sums, gate_far = lax.optimization_barrier((inner_sums, gate_far))
     inner_sums = ctx_sum(inner_sums.T.reshape(-1, 128), 1)
-    inner_sums, ups = lax.optimization_barrier((inner_sums, ups))
+    inner_sums, ups, gate_own = lax.optimization_barrier((inner_sums, ups, gate_own))
     up_far = swap(ups[7], 2)
     inner_sums = inner_sums.reshape(2, total).T / width
 

time: 496 us -> 493 us (level)
  no operation moved by 1% of the time
where the time goes in v3:
time: 493 us; the launch traced here: 486 us
  Pallas kernels  421 us (85%)
  local copies, waits for them, and re-layouts  28.8 us (6%)
  between operations  14.4 us (3%)
  matrix products  8.38 us (2%)
  starting transfers between devices  7.51 us (2%)
    pallas_call x1, Pallas kernels, finish_sums(): comm_call(kernel, 'finish_sums', collective_id, [jax.ShapeDtypeStruct(gra...  137 us
    pallas_call x2, Pallas kernels, reduce_then_gather(): comm_call(kernel, name, collective_id, [jax.ShapeDtypeStruct(partial.shap...  69.2 us
    pallas_call x1, Pallas kernels, gather_inputs(): comm_call(kernel, 'gather_inputs', collective_id, [jax.ShapeDtypeStruct((...  55.3 us
    pallas_call x1, Pallas kernels, run_experts(): pl.pallas_call(kernel, grid=(experts,), out_shape=[jax.ShapeDtypeStruct((...  25.2 us
    pallas_call x1, Pallas kernels, rows_to_heads(): comm_call(kernel, 'rows_to_heads', collective_id, jax.ShapeDtypeStruct((c...  24.7 us
    pallas_call x1, Pallas kernels, expert_grads(): pl.pallas_call(kernel, grid=(experts,), out_shape=[jax.ShapeDtypeStruct((...  20.3 us
    pallas_call x1, Pallas kernels, down_grads(): pl.pallas_call(kernel, grid=(experts,), out_shape=jax.ShapeDtypeStruct((2...  18.5 us
    pallas_call x1, Pallas kernels, heads_to_rows(): comm_call(kernel, 'heads_to_rows', collective_id, jax.ShapeDtypeStruct((f...  16 us
  transfers between devices with their start and end apart: 9, of which 0 were waited for; matrix products, arithmetic and copies ran while one was open for 3% of the time, Pallas kernels for 33%

profile of v3, /device:TPU:5, one launch (start us, length us, event | category | flops | bytes accessed | tf_op | source)
XLA Modules:
  0.0 486.1 jit_solution(17246799744617527126)
XLA Ops:
  7.2 0.0 all-gather.4.cloned.1.call-start
  7.3 0.8 copy_bitcast_fusion
  8.1 0.6 pad.13.pairs_ref
  8.7 1.6 slots_of.1.refs_5_
  10.3 0.7 pad_maximum_fusion.2
  11.1 0.6 reshape.93.refs_3_
  11.7 1.3 pad.12.refs_4_
  13.0 55.3 %gather_inputs.1 = (bf16[1024,2048]{1,0:T(8,128)(2,1)}, bf16[2048,768]{1,0:T(8,128)(2,1)}, bf16[512,2048]{1,0:T(8,128)(2,1)}, bf16[4,2048]{1,0:T(4,128)(2,1)}, b...) custom-call(bf16[128,2048]{1,0:T(8,128)(2,1)} %bitcast.36, ...), custom_call_target="tpu_custom_call" | custom-call | bytes 157286400 | tf_op jit(solution)/shard_map/gather_inputs/pallas_call | solution.py:2063
  68.3 1.5 slice_convert_fusion
  69.8 9.3 %project.1 = (bf16[1024,2048]{1,0:T(8,128)(2,1)}, f32[1024,768]{1,0:T(8,128)}, f32[1024,2]{1,0:T(8,128)}) custom-call(bf16[1024,2048]{1,0:T(8,128)(2,1)} %get-tuple-element.110.tokens_ref, f32[1,2048]{1,0:T(1,128)} %get-tuple-element.217.gain_ref, bf16[2048,768]{1,0:T(8,128)(2,1)} %get-tuple-element.112.weight_ref), custom_call_target="tpu_custom_call" | custom-call | flops 3000000000 | bytes 15728640 | tf_op jit(solution)/shard_map/project/pallas_call | solution.py:2116
  79.2 1.2 copy.41
  80.4 5.4 %ctx_sum.2 = f32[16,128]{1,0:T(8,128)S(1)} custom-call(f32[16,128]{1,0:T(8,128)S(1)} %reshape.94.own_ref), custom_call_target="tpu_custom_call" | custom-call | bytes 20971520 | tf_op jit(solution)/shard_map/ctx_sum/pallas_call | solution.py:537
  85.9 0.2 copy.42
  86.1 0.1 select_reduce_fusion.2
  86.3 0.1 select_reduce_fusion
  86.4 1.0 copy.43.first_ref
  87.4 1.9 fusion
  89.3 0.3 pad_maximum_fusion
  89.8 6.5 %attend.1 = (bf16[1024,768]{1,0:T(8,128)(2,1)S(1)}, f32[1024,256]{1,0:T(8,128)S(1)}, bf16[1024,256]{1,0:T(8,128)(2,1)S(1)}, f32[1024,256]{1,0:T(8,128)S(1)}) custom-call(f32[1024,768]{1,0:T(8,128)S(1)} %copy-done.1, f32[1024,2]{1,0:T(8,128)S(1)} %bitcast.39, f32[1,512]{1,0:T(1,128)S(1)} %pad_maximum_fusion.3.gains_ref, ...), custom_call_target="tpu_custom_call" | custom-call | flops 2000000000 | bytes 20971520 | tf_op jit(solution)/shard_map/attend/pallas_call | solution.py:1309
  96.4 16.0 %heads_to_rows.1 = bf16[512,512]{1,0:T(8,128)(2,1)S(1)} custom-call(bf16[1024,256]{1,0:T(8,128)(2,1)S(1)} %get-tuple-element.115.own_ref), custom_call_target="tpu_custom_call" | custom-call | bytes 41943040 | tf_op jit(solution)/shard_map/heads_to_rows/pallas_call | solution.py:626
  112.4 1.3 convolution_convert_fusion.1.refs_0_
  113.7 29.1 %mix_and_norm.1 = (bf16[512,2048]{1,0:T(8,128)(2,1)S(1)}, f32[128,2048]{1,0:T(8,128)S(1)}, bf16[128,1024]{1,0:T(8,128)(2,1)}) custom-call(bf16[512,2048]{1,0:T(8,128)(2,1)S(1)} %convolution_convert_fusion.1.refs_0_, bf16[128,2048]{1,0:T(8,128)(2,1)S(1)} %bitcast.38, f32[1,2048]{1,0:T(1,128)S(1)} %get-tuple-element.214.refs_2_), custom_call_target="tpu_custom_call" | custom-call | bytes 104857600 | tf_op jit(solution)/shard_map/mix_and_norm/pallas_call | solution.py:821
  142.9 1.0 copy-done.4
  143.8 1.4 copy-done.5
  145.2 0.0 all-gather.6.cloned.1.call-start
  145.3 0.7 all-gather.6.cloned.1.call-update
  146.0 0.0 reduce-scatter.2.cloned.1.call-start
  146.0 25.2 %run_experts.1 = (bf16[512,2048]{1,0:T(8,128)(2,1)}, bf16[512,2048]{1,0:T(8,128)(2,1)}, f32[16,2048]{1,0:T(8,128)}, bf16[6,256,256]{2,1,0:T(8,128)(2,1)}, bf16[6...) custom-call(bf16[512,2048]{1,0:T(8,128)(2,1)} %copy-done.5, bf16[512,2048]{1,0:T(8,128)(2,1)} %get-tuple-element.117.dy_ref, ...), custom_call_target="tpu_custom_call" | custom-call | flops 30000001024 | bytes 31457280 | tf_op jit(solution)/shard_map/run_experts/pallas_call | solution.py:1050
  171.2 0.9 collective-permute-start
  172.1 4.5 collective-permute-start.1
  176.6 40.1 %norm_back.1 = (bf16[512,2048]{1,0:T(8,128)(2,1)}, f32[128,2048]{1,0:T(8,128)}, f32[1,2048]{1,0:T(1,128)}, bf16[6,256,256]{2,1,0:T(8,128)(2,1)}, bf16[6,256,256]{2,1,0:T(8,128)(2,1)}) custom-call(bf16[512,2048]{1,0:T(8,128)(2,1)} %get-tuple-element.122.refs_0_, f32[128,2048]{1,0:T(8,128)} %copy-done.4, f32[1,2048]{1,0:T(1,128)} %copy-done.13, ...), custom_call_target="tpu_custom_call" | custom-call | bytes 104857600 | tf_op jit(solution)/shard_map/norm_back/pallas_call | solution.py:821
  216.7 0.0 all-gather.4.cloned.1.call-done.refs_5_
  216.7 20.3 %expert_grads.1 = (bf16[6,256,256]{2,1,0:T(8,128)(2,1)}, bf16[6,256,256]{2,1,0:T(8,128)(2,1)}, bf16[6,256,256]{2,1,0:T(8,128)(2,1)}, bf16[6,256,256]{2,1,0:T(8,1...) custom-call(bf16[6,256,256]{2,1,0:T(8,128)(2,1)} %get-tuple-element., ...), custom_call_target="tpu_custom_call" | custom-call | bytes 1048576 | tf_op jit(solution)/shard_map/expert_grads/pallas_call | solution.py:1160
  237.0 2.9 convolution_convert_fusion.2.own_ref
  239.9 24.7 %rows_to_heads.1.grad_ref = bf16[1024,256]{1,0:T(8,128)(2,1)S(1)} custom-call(bf16[512,512]{1,0:T(8,128)(2,1)S(1)} %convolution_convert_fusion.2.own_ref), custom_call_target="tpu_custom_call" | custom-call | bytes 1048576 | tf_op jit(solution)/shard_map/rows_to_heads/pallas_call | solution.py:713
  264.6 0.8 copy-done.9
  265.4 0.0 reduce-scatter.2.cloned.1.call-update
  265.5 0.4 collective-permute-start.3
  265.8 1.2 collective-permute-start.4
  267.0 4.3 convolution_convert_fusion.g_out_ref
  271.3 18.5 %down_grads.1.downs_ref = bf16[2,6,256,256]{3,2,1,0:T(8,128)(2,1)} custom-call(bf16[6,256,256]{2,1,0:T(8,128)(2,1)} %get-tuple-element.157.refs_0_, bf16[6,256,256]{2,1,0:T(8,128)(2,1)} %copy-done.20, bf16[6,256,256]{2,1,0:T(8,128)(2,1)} %collective-permute-done.1.refs_2_, bf16[6,256,256]{2,1,0:T(8,128)(2,1)} %collective-permute-done.2.refs_3_, ...), custom_call_target="tpu_custom_call" | custom-call | bytes 1048576 | tf_op jit(solution)/shard_map/down_grads/pallas_call | solution.py:1217
  289.8 0.8 iota.41.last_ref
  290.6 0.6 iota.42.places_ref
  291.2 12.2 %attend_back.1 = (f32[2,1024,256]{2,1,0:T(8,128)}, bf16[1024,256]{1,0:T(8,128)(2,1)}, f32[2,1,256]{2,1,0:T(1,128)}, f32[1024,2]{1,0:T(8,128)}) custom-call(bf16[1024,256]{1,0:T(8,128)(2,1)} %copy-done.9, bf16[1024,768]{1,0:T(8,128)(2,1)} %copy-done.10, f32[1024,256]{1,0:T(8,128)} %copy-done.11, f32[1024,256]{1,0:T(8,128)} %copy-done.12, ...), custom_call_target="tpu_custom_call" | custom-call | bytes 1048576 | tf_op jit(solution)/shard_map/attend_back/pallas_call | solution.py:1415
  303.4 1.2 copy.45
  304.7 5.4 %ctx_sum.3 = f32[16,128]{1,0:T(8,128)S(1)} custom-call(f32[16,128]{1,0:T(8,128)S(1)} %reshape.96.own_ref), custom_call_target="tpu_custom_call" | custom-call | bytes 20971520 | tf_op jit(solution)/shard_map/ctx_sum/pallas_call | solution.py:537
  310.1 0.5 collective-permute-start.5
  310.7 1.0 copy.46
  311.7 14.9 %project_back.1 = (bf16[1024,2048]{1,0:T(8,128)(2,1)}, bf16[2048,768]{1,0:T(8,128)(2,1)}, f32[1,2048]{1,0:T(1,128)}) custom-call(f32[2,1024,256]{2,1,0:T(8,128)} %get-tuple-element.187.back_ref, f32[1024,768]{1,0:T(8,128)} %get-tuple-element.113.lin_ref, f32[1024,2]{1,0:T(8,128)} %bitcast.41, f32[1024,2]{1,0:T(8,128)} %bitcast.44, ...), custom_call_target="tpu_custom_call" | custom-call | bytes 1048576 | tf_op jit(solution)/shard_map/project_back/pallas_call | solution.py:2195
  326.7 0.9 concatenate.23
  327.6 0.7 pad.14.small_ref
  328.3 0.9 copy-done.19
  329.2 136.6 %finish_sums.1 = (f32[6,256,256]{2,1,0:T(8,128)}, f32[6,256,256]{2,1,0:T(8,128)}, f32[6,256,256]{2,1,0:T(8,128)}, f32[128,2048]{1,0:T(8,128)}, f32[512,256]{1,0:...) custom-call(bf16[2,6,256,256]{3,2,1,0:T(8,128)(2,1)} %down_grads.1.downs_ref, ...), custom_call_target="tpu_custom_call" | custom-call | bytes 734003200 | tf_op jit(solution)/shard_map/finish_sums/pallas_call | solution.py:1762
  465.8 1.5 slice_bitcast_fusion
  467.3 1.5 fusion.16
  468.8 1.9 copy.61
  470.6 2.3 copy.62
  472.9 1.1 copy.63
  474.1 0.2 copy-done.21
  474.3 0.8 copy.64
  475.1 1.1 copy.65
  476.3 1.1 copy.66
  477.4 0.8 copy-done.15
  478.2 1.1 copy.67
  (76 shorter events, 0.4 us)
Async XLA Ops:
  7.2 105.2 %copy-start = (bf16[512,2048]{1,0:T(8,128)(2,1)S(1)}, bf16[512,2048]{1,0:T(8,128)(2,1)}, u32[]{:S(2)}) copy-start(bf16[512,2048]{1,0:T(8,128)(2,1)} %param.23) | copy-start | bytes 6291460
  7.2 209.5 %all-gather.4.cloned.1.call-start = ((), (), s32[]{:S(2)}) async-start(), calls=%async_computation.1 | async-start | bytes 1310720 | tf_op jit(solution)/shard_map/all_gather | solution.py:2330
  69.8 43.9 %copy-start.13 = (f32[1,2048]{1,0:T(1,128)}, f32[1,2048]{1,0:T(1,128)S(1)}, u32[]{:S(2)}) copy-start(f32[1,2048]{1,0:T(1,128)S(1)} %get-tuple-element.214.refs_2_) | copy-start | bytes 24580
  69.8 16.3 %copy-start.25 = (s32[1,16]{1,0:T(1,128)S(1)}, s32[1,16]{1,0:T(1,128)}, u32[]{:S(2)}) copy-start(s32[1,16]{1,0:T(1,128)} %param.16) | copy-start | bytes 196
  86.1 3.6 copy-start.3
  87.4 2.4 copy-start.14
  87.4 2.4 copy-start.1
  87.4 2.4 copy-start.8
  89.7 6.6 %copy-start.6 = (f32[1024,128]{1,0:T(8,128)}, f32[1024,128]{1,0:T(8,128)S(1)}, u32[]{:S(2)}) copy-start(f32[1024,128]{1,0:T(8,128)S(1)} %get-tuple-element.223.cos_ref) | copy-start | bytes 1572868
  89.7 6.6 %copy-start.7 = (f32[1024,128]{1,0:T(8,128)}, f32[1024,128]{1,0:T(8,128)S(1)}, u32[]{:S(2)}) copy-start(f32[1024,128]{1,0:T(8,128)S(1)} %get-tuple-element.224.sin_ref) | copy-start | bytes 1572868
  96.3 17.3 %copy-start.10 = (bf16[1024,768]{1,0:T(8,128)(2,1)}, bf16[1024,768]{1,0:T(8,128)(2,1)S(1)}, u32[]{:S(2)}) copy-start(bf16[1024,768]{1,0:T(8,128)(2,1)S(1)} %get-tuple-element.168.low_ref) | copy-start | bytes 4718596
  96.3 17.3 %copy-start.11 = (f32[1024,256]{1,0:T(8,128)}, f32[1024,256]{1,0:T(8,128)S(1)}, u32[]{:S(2)}) copy-start(f32[1024,256]{1,0:T(8,128)S(1)} %get-tuple-element.169.attended_ref) | copy-start | bytes 3145732
  96.4 17.3 %copy-start.12 = (f32[1024,256]{1,0:T(8,128)}, f32[1024,256]{1,0:T(8,128)S(1)}, u32[]{:S(2)}) copy-start(f32[1024,256]{1,0:T(8,128)S(1)} %get-tuple-element.170.top_ref) | copy-start | bytes 3145732
  112.4 1.3 copy-start.2
  142.9 1.0 copy-start.4
  143.8 1.4 copy-start.5
  145.2 126.0 %all-gather.6.cloned.1.call-start = ((), (), s32[]{:S(2)}) async-start(), calls=%async_computation.3 | async-start | bytes 2621440 | tf_op jit(solution)/shard_map/all_gather | solution.py:2270
  146.0 182.3 %reduce-scatter.2.cloned.1.call-start = ((), (), s32[]{:S(2)}) async-start(), calls=%async_computation.2 | async-start | bytes 2621440 | tf_op jit(solution)/shard_map/reduce_scatter | solution.py:2340
  171.2 94.2 %collective-permute-start = (bf16[6,256,256]{2,1,0:T(8,128)(2,1)}, bf16[6,256,256]{2,1,0:T(8,128)(2,1)S(1)}, u32[]{:S(2)}, u32[]{:S(2)}) collective-permute-start(bf16[6,256,256]{2,1,0:T(8,128)(2,1)} %get-tuple-element.157.refs_0_), channel_id=1, source_target_pairs={{0,8},{4,12},{8,0},{12,4},{16,24},{20,28},{24,16},{28,20},{1,9},{5... | collective-permute-start | bytes 2359304 | tf_op jit(solution)/shard_map/ppermute | solution.py:733
  172.1 93.3 %collective-permute-start.1 = (bf16[6,256,256]{2,1,0:T(8,128)(2,1)}, bf16[6,256,256]{2,1,0:T(8,128)(2,1)}, u32[]{:S(2)}, u32[]{:S(2)}) collective-permute-start(bf16[6,256,256]{2,1,0:T(8,128)(2,1)} %get-tuple-element.157.refs_0_), channel_id=1, source_target_pairs={{0,16},{4,20},{8,24},{12,28},{16,0},{20,4},{24,8},{28,12},{1,17},{... | collective-permute-start | bytes 2359304 | tf_op jit(solution)/shard_map/ppermute | solution.py:733
  176.6 88.9 %collective-permute-start.2 = (bf16[6,256,256]{2,1,0:T(8,128)(2,1)}, bf16[6,256,256]{2,1,0:T(8,128)(2,1)}, u32[]{:S(2)}, u32[]{:S(2)}) collective-permute-start(bf16[6,256,256]{2,1,0:T(8,128)(2,1)} %get-tuple-element.157.refs_0_), channel_id=1, source_target_pairs={{0,24},{4,28},{8,16},{12,20},{16,8},{20,12},{24,0},{28,4},{1,25},{... | collective-permute-start | bytes 2359304 | tf_op jit(solution)/shard_map/ppermute | solution.py:733
  264.6 0.8 copy-start.9
  265.4 5.8 %copy-start.20 = (bf16[6,256,256]{2,1,0:T(8,128)(2,1)}, bf16[6,256,256]{2,1,0:T(8,128)(2,1)S(1)}, u32[]{:S(2)}) copy-start(bf16[6,256,256]{2,1,0:T(8,128)(2,1)S(1)} %collective-permute-done.refs_1_) | copy-start | bytes 2359300
  265.5 38.0 %collective-permute-start.3 = (bf16[6,256,256]{2,1,0:T(8,128)(2,1)}, bf16[6,256,256]{2,1,0:T(8,128)(2,1)}, u32[]{:S(2)}, u32[]{:S(2)}) collective-permute-start(bf16[6,256,256]{2,1,0:T(8,128)(2,1)} %get-tuple-element.152), channel_id=1, source_target_pairs={{0,8},{4,12},{8,0},{12,4},{16,24},{20,28},{24,16},{28,20},{1,9},{5... | collective-permute-start | bytes 2359304 | tf_op jit(solution)/shard_map/ppermute | solution.py:733
  265.8 44.3 %collective-permute-start.4 = (bf16[6,256,256]{2,1,0:T(8,128)(2,1)}, bf16[6,256,256]{2,1,0:T(8,128)(2,1)}, u32[]{:S(2)}, u32[]{:S(2)}) collective-permute-start(bf16[6,256,256]{2,1,0:T(8,128)(2,1)} %get-tuple-element.151), channel_id=1, source_target_pairs={{0,8},{4,12},{8,0},{12,4},{16,24},{20,28},{24,16},{28,20},{1,9},{5... | collective-permute-start | bytes 2359304 | tf_op jit(solution)/shard_map/ppermute | solution.py:733
  291.2 19.5 %copy-start.22 = (f32[16,2048]{1,0:T(8,128)S(1)}, f32[16,2048]{1,0:T(8,128)}, u32[]{:S(2)}) copy-start(f32[16,2048]{1,0:T(8,128)} %get-tuple-element.197) | copy-start | bytes 393220
  310.1 18.1 %collective-permute-start.5 = (bf16[6,256,256]{2,1,0:T(8,128)(2,1)}, bf16[6,256,256]{2,1,0:T(8,128)(2,1)S(1)}, u32[]{:S(2)}, u32[]{:S(2)}) collective-permute-start(bf16[6,256,256]{2,1,0:T(8,128)(2,1)} %get-tuple-element.186), channel_id=1, source_target_pairs={{0,8},{4,12},{8,0},{12,4},{16,24},{20,28},{24,16},{28,20},{1,9},{5... | collective-permute-start | bytes 2359304 | tf_op jit(solution)/shard_map/ppermute | solution.py:733
  311.7 14.9 %copy-start.24 = (f32[2,1,256]{2,1,0:T(1,128)S(1)}, f32[2,1,256]{2,1,0:T(1,128)}, u32[]{:S(2)}) copy-start(f32[2,1,256]{2,1,0:T(1,128)} %get-tuple-element.195) | copy-start | bytes 6148
  311.7 15.0 %copy-start.23 = (f32[1,2048]{1,0:T(1,128)S(1)}, f32[1,2048]{1,0:T(1,128)}, u32[]{:S(2)}) copy-start(f32[1,2048]{1,0:T(1,128)} %get-tuple-element.196) | copy-start | bytes 24580
  328.3 0.9 copy-start.19
  465.8 7.1 %copy-start.18 = (f32[512,768]{1,0:T(8,128)S(1)}, f32[512,768]{1,0:T(8,128)}, u32[]{:S(2)}) copy-start(f32[512,768]{1,0:T(8,128)} %get-tuple-element.240) | copy-start | bytes 4718596
  472.9 1.4 copy-start.21
  472.9 2.2 copy-start.17
  474.3 1.9 copy-start.16
  476.3 2.0 copy-start.15
Sparse Core Ops, SparseCore 0:
  145.4 18.1 all-gather.3
  165.1 25.6 all-gather.5
  265.6 29.2 reduce-scatter.1

commit v4 on v3

--- a/solution.py
+++ b/solution.py
@@ -640,7 +640,7 @@
     share = ctx // fsdp
     rows, cols = values.shape[0] // fsdp, values.shape[1] // share
 
-    def kernel(own_ref, out_ref, stage, stage_send, stage_recv, send_sems, recv_sems, done_sem):
+    def kernel(own_ref, out_ref, stage, stage_send, stage_recv, send_sems, recv_sems):
         me, mine = lax.axis_index("ctx"), lax.axis_index("fsdp")
         ctx_peers = [(lax.rem(me + step, ctx), mine) for step in range(1, ctx)]
         greet(ctx_peers + [(me, lax.rem(mine + step, fsdp)) for step in range(1, fsdp)])
@@ -706,9 +706,6 @@
                 pl.when(jnp.logical_not(far))(keep(step, place).wait)
         for copy in staged.values():
             copy.wait_send()
-        for peer in ctx_peers:
-            pl.semaphore_signal(done_sem, inc=1, device_id=peer, device_id_type=MESH)
-        pl.semaphore_wait(done_sem, ctx - 1)
 
     return comm_call(
         kernel,
@@ -723,7 +720,6 @@
             DMA((fsdp,)),
             DMA((ctx,)),
             DMA((ctx,)),
-            pltpu.SemaphoreType.REGULAR,
         ],
         2**20,
     )(values)

time: 493 us -> 492 us (level)
  no operation moved by 1% of the time
where the time goes in v4:
time: 492 us; the launch traced here: 484 us
  Pallas kernels  417 us (85%)
  local copies, waits for them, and re-layouts  28.8 us (6%)
  between operations  14.4 us (3%)
  starting transfers between devices  9.22 us (2%)
  matrix products  8.38 us (2%)
    pallas_call x1, Pallas kernels, finish_sums(): comm_call(kernel, 'finish_sums', collective_id, [jax.ShapeDtypeStruct(gra...  137 us
    pallas_call x2, Pallas kernels, reduce_then_gather(): comm_call(kernel, name, collective_id, [jax.ShapeDtypeStruct(partial.shap...  69.2 us
    pallas_call x1, Pallas kernels, gather_inputs(): comm_call(kernel, 'gather_inputs', collective_id, [jax.ShapeDtypeStruct((...  55.3 us
    pallas_call x1, Pallas kernels, run_experts(): pl.pallas_call(kernel, grid=(experts,), out_shape=[jax.ShapeDtypeStruct((...  25.2 us
    pallas_call x1, Pallas kernels, rows_to_heads(): comm_call(kernel, 'rows_to_heads', collective_id, jax.ShapeDtypeStruct((c...  20.6 us
    pallas_call x1, Pallas kernels, expert_grads(): pl.pallas_call(kernel, grid=(experts,), out_shape=[jax.ShapeDtypeStruct((...  20.3 us
    pallas_call x1, Pallas kernels, down_grads(): pl.pallas_call(kernel, grid=(experts,), out_shape=jax.ShapeDtypeStruct((2...  18.3 us
    pallas_call x1, Pallas kernels, heads_to_rows(): comm_call(kernel, 'heads_to_rows', collective_id, jax.ShapeDtypeStruct((f...  16 us
  transfers between devices with their start and end apart: 9, of which 0 were waited for; matrix products, arithmetic and copies ran while one was open for 3% of the time, Pallas kernels for 33%

profile of v4, /device:TPU:5, one launch (start us, length us, event | category | flops | bytes accessed | tf_op | source)
XLA Modules:
  0.0 483.6 jit_solution(14766544368685361297)
XLA Ops:
  7.2 0.0 all-gather.4.cloned.1.call-start
  7.3 0.8 copy_bitcast_fusion
  8.1 0.6 pad.13.pairs_ref
  8.7 1.6 slots_of.1.refs_5_
  10.3 0.7 pad_maximum_fusion.2
  11.1 0.6 reshape.93.refs_3_
  11.7 1.3 pad.12.refs_4_
  13.0 55.3 %gather_inputs.1 = (bf16[1024,2048]{1,0:T(8,128)(2,1)}, bf16[2048,768]{1,0:T(8,128)(2,1)}, bf16[512,2048]{1,0:T(8,128)(2,1)}, bf16[4,2048]{1,0:T(4,128)(2,1)}, b...) custom-call(bf16[128,2048]{1,0:T(8,128)(2,1)} %bitcast.36, ...), custom_call_target="tpu_custom_call" | custom-call | bytes 157286400 | tf_op jit(solution)/shard_map/gather_inputs/pallas_call | solution.py:2059
  68.3 1.5 slice_convert_fusion
  69.8 9.3 %project.1 = (bf16[1024,2048]{1,0:T(8,128)(2,1)}, f32[1024,768]{1,0:T(8,128)}, f32[1024,2]{1,0:T(8,128)}) custom-call(bf16[1024,2048]{1,0:T(8,128)(2,1)} %get-tuple-element.110.tokens_ref, f32[1,2048]{1,0:T(1,128)} %get-tuple-element.217.gain_ref, bf16[2048,768]{1,0:T(8,128)(2,1)} %get-tuple-element.112.weight_ref), custom_call_target="tpu_custom_call" | custom-call | flops 3000000000 | bytes 15728640 | tf_op jit(solution)/shard_map/project/pallas_call | solution.py:2112
  79.2 1.2 copy.41
  80.4 5.4 %ctx_sum.2 = f32[16,128]{1,0:T(8,128)S(1)} custom-call(f32[16,128]{1,0:T(8,128)S(1)} %reshape.94.own_ref), custom_call_target="tpu_custom_call" | custom-call | bytes 20971520 | tf_op jit(solution)/shard_map/ctx_sum/pallas_call | solution.py:537
  85.9 0.2 copy.42
  86.1 0.1 select_reduce_fusion.2
  86.3 0.1 select_reduce_fusion
  86.4 1.0 copy.43.first_ref
  87.4 1.9 fusion
  89.3 0.3 pad_maximum_fusion
  89.8 6.5 %attend.1 = (bf16[1024,768]{1,0:T(8,128)(2,1)S(1)}, f32[1024,256]{1,0:T(8,128)S(1)}, bf16[1024,256]{1,0:T(8,128)(2,1)S(1)}, f32[1024,256]{1,0:T(8,128)S(1)}) custom-call(f32[1024,768]{1,0:T(8,128)S(1)} %copy-done.1, f32[1024,2]{1,0:T(8,128)S(1)} %bitcast.39, f32[1,512]{1,0:T(1,128)S(1)} %pad_maximum_fusion.3.gains_ref, ...), custom_call_target="tpu_custom_call" | custom-call | flops 2000000000 | bytes 20971520 | tf_op jit(solution)/shard_map/attend/pallas_call | solution.py:1305
  96.4 16.0 %heads_to_rows.1 = bf16[512,512]{1,0:T(8,128)(2,1)S(1)} custom-call(bf16[1024,256]{1,0:T(8,128)(2,1)S(1)} %get-tuple-element.115.own_ref), custom_call_target="tpu_custom_call" | custom-call | bytes 41943040 | tf_op jit(solution)/shard_map/heads_to_rows/pallas_call | solution.py:626
  112.4 1.3 convolution_convert_fusion.1.refs_0_
  113.7 29.1 %mix_and_norm.1 = (bf16[512,2048]{1,0:T(8,128)(2,1)S(1)}, f32[128,2048]{1,0:T(8,128)S(1)}, bf16[128,1024]{1,0:T(8,128)(2,1)}) custom-call(bf16[512,2048]{1,0:T(8,128)(2,1)S(1)} %convolution_convert_fusion.1.refs_0_, bf16[128,2048]{1,0:T(8,128)(2,1)S(1)} %bitcast.38, f32[1,2048]{1,0:T(1,128)S(1)} %get-tuple-element.214.refs_2_), custom_call_target="tpu_custom_call" | custom-call | bytes 104857600 | tf_op jit(solution)/shard_map/mix_and_norm/pallas_call | solution.py:817
  142.9 1.0 copy-done.4
  143.8 1.4 copy-done.5
  145.2 0.0 all-gather.6.cloned.1.call-start
  145.3 0.7 all-gather.6.cloned.1.call-update
  146.0 0.0 reduce-scatter.2.cloned.1.call-start
  146.0 25.2 %run_experts.1 = (bf16[512,2048]{1,0:T(8,128)(2,1)}, bf16[512,2048]{1,0:T(8,128)(2,1)}, f32[16,2048]{1,0:T(8,128)}, bf16[6,256,256]{2,1,0:T(8,128)(2,1)}, bf16[6...) custom-call(bf16[512,2048]{1,0:T(8,128)(2,1)} %copy-done.5, bf16[512,2048]{1,0:T(8,128)(2,1)} %get-tuple-element.117.dy_ref, ...), custom_call_target="tpu_custom_call" | custom-call | flops 30000001024 | bytes 31457280 | tf_op jit(solution)/shard_map/run_experts/pallas_call | solution.py:1046
  171.2 0.9 collective-permute-start
  172.1 4.5 collective-permute-start.1
  176.6 40.1 %norm_back.1 = (bf16[512,2048]{1,0:T(8,128)(2,1)}, f32[128,2048]{1,0:T(8,128)}, f32[1,2048]{1,0:T(1,128)}, bf16[6,256,256]{2,1,0:T(8,128)(2,1)}, bf16[6,256,256]{2,1,0:T(8,128)(2,1)}) custom-call(bf16[512,2048]{1,0:T(8,128)(2,1)} %get-tuple-element.122.refs_0_, f32[128,2048]{1,0:T(8,128)} %copy-done.4, f32[1,2048]{1,0:T(1,128)} %copy-done.13, ...), custom_call_target="tpu_custom_call" | custom-call | bytes 104857600 | tf_op jit(solution)/shard_map/norm_back/pallas_call | solution.py:817
  216.7 0.0 all-gather.4.cloned.1.call-done.refs_5_
  216.7 20.3 %expert_grads.1 = (bf16[6,256,256]{2,1,0:T(8,128)(2,1)}, bf16[6,256,256]{2,1,0:T(8,128)(2,1)}, bf16[6,256,256]{2,1,0:T(8,128)(2,1)}, bf16[6,256,256]{2,1,0:T(8,1...) custom-call(bf16[6,256,256]{2,1,0:T(8,128)(2,1)} %get-tuple-element., ...), custom_call_target="tpu_custom_call" | custom-call | bytes 1048576 | tf_op jit(solution)/shard_map/expert_grads/pallas_call | solution.py:1156
  237.0 2.9 convolution_convert_fusion.2.own_ref
  239.9 20.6 %rows_to_heads.1.grad_ref = bf16[1024,256]{1,0:T(8,128)(2,1)S(1)} custom-call(bf16[512,512]{1,0:T(8,128)(2,1)S(1)} %convolution_convert_fusion.2.own_ref), custom_call_target="tpu_custom_call" | custom-call | bytes 1048576 | tf_op jit(solution)/shard_map/rows_to_heads/pallas_call | solution.py:710
  260.5 0.8 copy-done.9
  261.3 0.0 reduce-scatter.2.cloned.1.call-update
  261.4 3.2 collective-permute-start.3
  264.5 0.1 collective-permute-start.4
  264.6 4.3 convolution_convert_fusion.g_out_ref
  268.9 18.3 %down_grads.1.downs_ref = bf16[2,6,256,256]{3,2,1,0:T(8,128)(2,1)} custom-call(bf16[6,256,256]{2,1,0:T(8,128)(2,1)} %get-tuple-element.157.refs_0_, bf16[6,256,256]{2,1,0:T(8,128)(2,1)} %copy-done.20, bf16[6,256,256]{2,1,0:T(8,128)(2,1)} %collective-permute-done.1.refs_2_, bf16[6,256,256]{2,1,0:T(8,128)(2,1)} %collective-permute-done.2.refs_3_, ...), custom_call_target="tpu_custom_call" | custom-call | bytes 1048576 | tf_op jit(solution)/shard_map/down_grads/pallas_call | solution.py:1213
  287.2 0.8 iota.41.last_ref
  288.0 0.6 iota.42.places_ref
  288.6 12.2 %attend_back.1 = (f32[2,1024,256]{2,1,0:T(8,128)}, bf16[1024,256]{1,0:T(8,128)(2,1)}, f32[2,1,256]{2,1,0:T(1,128)}, f32[1024,2]{1,0:T(8,128)}) custom-call(bf16[1024,256]{1,0:T(8,128)(2,1)} %copy-done.9, bf16[1024,768]{1,0:T(8,128)(2,1)} %copy-done.10, f32[1024,256]{1,0:T(8,128)} %copy-done.11, f32[1024,256]{1,0:T(8,128)} %copy-done.12, ...), custom_call_target="tpu_custom_call" | custom-call | bytes 1048576 | tf_op jit(solution)/shard_map/attend_back/pallas_call | solution.py:1411
  300.8 1.2 copy.45
  302.1 5.7 %ctx_sum.3 = f32[16,128]{1,0:T(8,128)S(1)} custom-call(f32[16,128]{1,0:T(8,128)S(1)} %reshape.96.own_ref), custom_call_target="tpu_custom_call" | custom-call | bytes 20971520 | tf_op jit(solution)/shard_map/ctx_sum/pallas_call | solution.py:537
  307.8 0.5 collective-permute-start.5
  308.3 1.0 copy.46
  309.3 14.9 %project_back.1 = (bf16[1024,2048]{1,0:T(8,128)(2,1)}, bf16[2048,768]{1,0:T(8,128)(2,1)}, f32[1,2048]{1,0:T(1,128)}) custom-call(f32[2,1024,256]{2,1,0:T(8,128)} %get-tuple-element.187.back_ref, f32[1024,768]{1,0:T(8,128)} %get-tuple-element.113.lin_ref, f32[1024,2]{1,0:T(8,128)} %bitcast.41, f32[1024,2]{1,0:T(8,128)} %bitcast.44, ...), custom_call_target="tpu_custom_call" | custom-call | bytes 1048576 | tf_op jit(solution)/shard_map/project_back/pallas_call | solution.py:2191
  324.3 0.9 concatenate.23
  325.2 0.7 pad.14.small_ref
  325.9 0.9 copy-done.19
  326.8 136.6 %finish_sums.1 = (f32[6,256,256]{2,1,0:T(8,128)}, f32[6,256,256]{2,1,0:T(8,128)}, f32[6,256,256]{2,1,0:T(8,128)}, f32[128,2048]{1,0:T(8,128)}, f32[512,256]{1,0:...) custom-call(bf16[2,6,256,256]{3,2,1,0:T(8,128)(2,1)} %down_grads.1.downs_ref, ...), custom_call_target="tpu_custom_call" | custom-call | bytes 734003200 | tf_op jit(solution)/shard_map/finish_sums/pallas_call | solution.py:1758
  463.4 1.5 slice_bitcast_fusion
  464.8 1.5 fusion.16
  466.3 1.9 copy.61
  468.2 2.3 copy.62
  470.5 1.1 copy.63
  471.6 0.2 copy-done.21
  471.9 0.8 copy.64
  472.7 1.1 copy.65
  473.8 1.1 copy.66
  474.9 0.8 copy-done.15
  475.8 1.1 copy.67
  (76 shorter events, 0.4 us)
Async XLA Ops:
  7.2 105.2 %copy-start = (bf16[512,2048]{1,0:T(8,128)(2,1)S(1)}, bf16[512,2048]{1,0:T(8,128)(2,1)}, u32[]{:S(2)}) copy-start(bf16[512,2048]{1,0:T(8,128)(2,1)} %param.23) | copy-start | bytes 6291460
  7.2 209.5 %all-gather.4.cloned.1.call-start = ((), (), s32[]{:S(2)}) async-start(), calls=%async_computation.1 | async-start | bytes 1310720 | tf_op jit(solution)/shard_map/all_gather | solution.py:2326
  69.8 43.9 %copy-start.13 = (f32[1,2048]{1,0:T(1,128)}, f32[1,2048]{1,0:T(1,128)S(1)}, u32[]{:S(2)}) copy-start(f32[1,2048]{1,0:T(1,128)S(1)} %get-tuple-element.214.refs_2_) | copy-start | bytes 24580
  69.8 16.3 %copy-start.25 = (s32[1,16]{1,0:T(1,128)S(1)}, s32[1,16]{1,0:T(1,128)}, u32[]{:S(2)}) copy-start(s32[1,16]{1,0:T(1,128)} %param.16) | copy-start | bytes 196
  86.1 3.6 copy-start.3
  87.4 2.4 copy-start.14
  87.4 2.4 copy-start.1
  87.4 2.4 copy-start.8
  89.7 6.6 %copy-start.6 = (f32[1024,128]{1,0:T(8,128)}, f32[1024,128]{1,0:T(8,128)S(1)}, u32[]{:S(2)}) copy-start(f32[1024,128]{1,0:T(8,128)S(1)} %get-tuple-element.223.cos_ref) | copy-start | bytes 1572868
  89.7 6.6 %copy-start.7 = (f32[1024,128]{1,0:T(8,128)}, f32[1024,128]{1,0:T(8,128)S(1)}, u32[]{:S(2)}) copy-start(f32[1024,128]{1,0:T(8,128)S(1)} %get-tuple-element.224.sin_ref) | copy-start | bytes 1572868
  96.3 17.3 %copy-start.10 = (bf16[1024,768]{1,0:T(8,128)(2,1)}, bf16[1024,768]{1,0:T(8,128)(2,1)S(1)}, u32[]{:S(2)}) copy-start(bf16[1024,768]{1,0:T(8,128)(2,1)S(1)} %get-tuple-element.168.low_ref) | copy-start | bytes 4718596
  96.3 17.3 %copy-start.11 = (f32[1024,256]{1,0:T(8,128)}, f32[1024,256]{1,0:T(8,128)S(1)}, u32[]{:S(2)}) copy-start(f32[1024,256]{1,0:T(8,128)S(1)} %get-tuple-element.169.attended_ref) | copy-start | bytes 3145732
  96.4 17.3 %copy-start.12 = (f32[1024,256]{1,0:T(8,128)}, f32[1024,256]{1,0:T(8,128)S(1)}, u32[]{:S(2)}) copy-start(f32[1024,256]{1,0:T(8,128)S(1)} %get-tuple-element.170.top_ref) | copy-start | bytes 3145732
  112.4 1.3 copy-start.2
  142.9 1.0 copy-start.4
  143.8 1.4 copy-start.5
  145.2 123.6 %all-gather.6.cloned.1.call-start = ((), (), s32[]{:S(2)}) async-start(), calls=%async_computation.3 | async-start | bytes 2621440 | tf_op jit(solution)/shard_map/all_gather | solution.py:2266
  146.0 179.9 %reduce-scatter.2.cloned.1.call-start = ((), (), s32[]{:S(2)}) async-start(), calls=%async_computation.2 | async-start | bytes 2621440 | tf_op jit(solution)/shard_map/reduce_scatter | solution.py:2336
  171.2 90.1 %collective-permute-start = (bf16[6,256,256]{2,1,0:T(8,128)(2,1)}, bf16[6,256,256]{2,1,0:T(8,128)(2,1)S(1)}, u32[]{:S(2)}, u32[]{:S(2)}) collective-permute-start(bf16[6,256,256]{2,1,0:T(8,128)(2,1)} %get-tuple-element.157.refs_0_), channel_id=1, source_target_pairs={{0,8},{4,12},{8,0},{12,4},{16,24},{20,28},{24,16},{28,20},{1,9},{5... | collective-permute-start | bytes 2359304 | tf_op jit(solution)/shard_map/ppermute | solution.py:729
  172.1 89.2 %collective-permute-start.1 = (bf16[6,256,256]{2,1,0:T(8,128)(2,1)}, bf16[6,256,256]{2,1,0:T(8,128)(2,1)}, u32[]{:S(2)}, u32[]{:S(2)}) collective-permute-start(bf16[6,256,256]{2,1,0:T(8,128)(2,1)} %get-tuple-element.157.refs_0_), channel_id=1, source_target_pairs={{0,16},{4,20},{8,24},{12,28},{16,0},{20,4},{24,8},{28,12},{1,17},{... | collective-permute-start | bytes 2359304 | tf_op jit(solution)/shard_map/ppermute | solution.py:729
  176.6 84.8 %collective-permute-start.2 = (bf16[6,256,256]{2,1,0:T(8,128)(2,1)}, bf16[6,256,256]{2,1,0:T(8,128)(2,1)}, u32[]{:S(2)}, u32[]{:S(2)}) collective-permute-start(bf16[6,256,256]{2,1,0:T(8,128)(2,1)} %get-tuple-element.157.refs_0_), channel_id=1, source_target_pairs={{0,24},{4,28},{8,16},{12,20},{16,8},{20,12},{24,0},{28,4},{1,25},{... | collective-permute-start | bytes 2359304 | tf_op jit(solution)/shard_map/ppermute | solution.py:729
  260.5 0.8 copy-start.9
  261.3 7.5 %copy-start.20 = (bf16[6,256,256]{2,1,0:T(8,128)(2,1)}, bf16[6,256,256]{2,1,0:T(8,128)(2,1)S(1)}, u32[]{:S(2)}) copy-start(bf16[6,256,256]{2,1,0:T(8,128)(2,1)S(1)} %collective-permute-done.refs_1_) | copy-start | bytes 2359300
  261.4 39.5 %collective-permute-start.3 = (bf16[6,256,256]{2,1,0:T(8,128)(2,1)}, bf16[6,256,256]{2,1,0:T(8,128)(2,1)}, u32[]{:S(2)}, u32[]{:S(2)}) collective-permute-start(bf16[6,256,256]{2,1,0:T(8,128)(2,1)} %get-tuple-element.152), channel_id=1, source_target_pairs={{0,8},{4,12},{8,0},{12,4},{16,24},{20,28},{24,16},{28,20},{1,9},{5... | collective-permute-start | bytes 2359304 | tf_op jit(solution)/shard_map/ppermute | solution.py:729
  264.5 43.2 %collective-permute-start.4 = (bf16[6,256,256]{2,1,0:T(8,128)(2,1)}, bf16[6,256,256]{2,1,0:T(8,128)(2,1)}, u32[]{:S(2)}, u32[]{:S(2)}) collective-permute-start(bf16[6,256,256]{2,1,0:T(8,128)(2,1)} %get-tuple-element.151), channel_id=1, source_target_pairs={{0,8},{4,12},{8,0},{12,4},{16,24},{20,28},{24,16},{28,20},{1,9},{5... | collective-permute-start | bytes 2359304 | tf_op jit(solution)/shard_map/ppermute | solution.py:729
  288.6 19.7 %copy-start.22 = (f32[16,2048]{1,0:T(8,128)S(1)}, f32[16,2048]{1,0:T(8,128)}, u32[]{:S(2)}) copy-start(f32[16,2048]{1,0:T(8,128)} %get-tuple-element.197) | copy-start | bytes 393220
  307.8 18.1 %collective-permute-start.5 = (bf16[6,256,256]{2,1,0:T(8,128)(2,1)}, bf16[6,256,256]{2,1,0:T(8,128)(2,1)S(1)}, u32[]{:S(2)}, u32[]{:S(2)}) collective-permute-start(bf16[6,256,256]{2,1,0:T(8,128)(2,1)} %get-tuple-element.186), channel_id=1, source_target_pairs={{0,8},{4,12},{8,0},{12,4},{16,24},{20,28},{24,16},{28,20},{1,9},{5... | collective-permute-start | bytes 2359304 | tf_op jit(solution)/shard_map/ppermute | solution.py:729
  309.3 14.9 %copy-start.24 = (f32[2,1,256]{2,1,0:T(1,128)S(1)}, f32[2,1,256]{2,1,0:T(1,128)}, u32[]{:S(2)}) copy-start(f32[2,1,256]{2,1,0:T(1,128)} %get-tuple-element.195) | copy-start | bytes 6148
  309.3 15.0 %copy-start.23 = (f32[1,2048]{1,0:T(1,128)S(1)}, f32[1,2048]{1,0:T(1,128)}, u32[]{:S(2)}) copy-start(f32[1,2048]{1,0:T(1,128)} %get-tuple-element.196) | copy-start | bytes 24580
  325.9 0.9 copy-start.19
  463.3 7.1 %copy-start.18 = (f32[512,768]{1,0:T(8,128)S(1)}, f32[512,768]{1,0:T(8,128)}, u32[]{:S(2)}) copy-start(f32[512,768]{1,0:T(8,128)} %get-tuple-element.240) | copy-start | bytes 4718596
  470.5 1.4 copy-start.21
  470.5 2.2 copy-start.17
  471.9 1.9 copy-start.16
  473.8 2.0 copy-start.15
Sparse Core Ops, SparseCore 0:
  145.4 18.1 all-gather.3
  165.1 25.6 all-gather.5
  261.5 32.6 reduce-scatter.1
